TPU v7x, 128 devices: a whole 4x4x4 slice. The times are simulated.
128 devices in a mesh: lat: 8 (over z, core), lon: 16 (over x, y).
Axes of the slice: x: 4, y: 4, z: 4, core: 2. Of those that a mesh axis runs over, the one named last changes fastest.
Arguments:
- state: bfloat16 [1, 6, 24, 524288], P(None, None, None, ('lat', 'lon')), may hold values from -6 to 6
- conv_in: bfloat16 [64, 3, 6], replicated, may hold values from -1.5 to 1.5
- bias_in: float32 [64], replicated, may hold values from -3 to 3
- conv_out: bfloat16 [2, 3, 64], replicated, may hold values from -0.4375 to 0.4375
- bias_out: float32 [2], replicated, may hold values from -3 to 3
- spectral_gain: float32 [344], replicated, may hold values from 0.3 to 3
- mix_in: bfloat16 [64, 3, 8], replicated, may hold values from -1.25 to 1.25
- blend_bias: float32 [64], replicated, may hold values from -3 to 3
- mix_out: bfloat16 [6, 3, 64], replicated, may hold values from -0.4375 to 0.4375
- mix_out_bias: float32 [6], replicated, may hold values from -3 to 3
- level_order: int32 [48], replicated, may hold values from 0 to 47, each once
- wave_order: int32 [344], replicated, may hold values from 0 to 343, each once
Outputs:
- spectrum: float32 [48, 344, 688], P('lon', 'lat')
- increment: float32 [1, 6, 24, 524288], P(None, None, None, ('lat', 'lon'))
Inputs may be any that keep to these rules, and one draw needn't show every extreme that they name: `level_order`: a permutation: each item slot holds a different field level. `wave_order`: a permutation: each wavenumber slot holds a different wavenumber.
All inputs are finite; a program needn't handle non-finite values.
Results may differ from a plain program's by a relative error of at most 0.0057.
Values may be sent and summed in bfloat16 or wider, within the bound.
No kernel may reach another device: no remote copies, remote signals or barrier semaphores. Data moves between devices by JAX's collectives and lax.ppermute only.
A program may use at most 128 MiB of HBM per device.

v0:
```python
import math

import jax
import jax.numpy as jnp
from jax import lax
from jax.sharding import PartitionSpec as P

NLAT = 512
NLON = 1024
LEVEL_SPACING = 2


def vertical_conv(value_entries, weight, offset):
    level_stack = value_entries.shape[2]
    padded_levels = jnp.pad(value_entries, ((0, 0), (0, 0), (LEVEL_SPACING, LEVEL_SPACING), (0, 0)))
    summed = offset[None, :, None, None]
    for kernel_tap_index in range(3):
        sliding_frame = padded_levels[
            :, :, kernel_tap_index * LEVEL_SPACING : kernel_tap_index * LEVEL_SPACING + level_stack
        ]
        summed = summed + jnp.einsum(
            "oc,sclx->solx",
            weight[:, kernel_tap_index],
            sliding_frame,
            preferred_element_type=jnp.float32,
        )
    return summed


def legendre_tables(waves, lat_total, wave_total):
    lat_index = jnp.arange(lat_total, dtype=jnp.float32)
    latitude = jnp.pi * (lat_index + 0.5) / lat_total - jnp.pi / 2
    sine_lat = jnp.sin(latitude)[None, :]
    cosine = jnp.cos(latitude)[None, :]
    quadrature = jnp.pi * cosine / math.sqrt(lat_total)
    wave_float = waves.astype(jnp.float32)[:, None]
    log_start = (
        0.5 * jnp.log(jnp.float32(0.5))
        + 0.5
        * (
            lax.lgamma(wave_float + 1.5)
            - lax.lgamma(wave_float + 1.0)
            - lax.lgamma(jnp.float32(1.5))
        )
        + wave_float * jnp.log(cosine)
    )

    def advance(carry, degree_up):
        previous, earlier, log_scale = carry
        degree = wave_float + degree_up
        below = degree - 1.0
        factor_up = jnp.sqrt(
            (4.0 * degree * degree - 1.0)
            / jnp.maximum(degree * degree - wave_float * wave_float, 1.0)
        )
        factor_down = jnp.sqrt(
            jnp.maximum(below * below - wave_float * wave_float, 0.0)
            / jnp.maximum(4.0 * below * below - 1.0, 1.0)
        )
        stepped = factor_up * (sine_lat * previous - factor_down * earlier)
        current = jnp.where(degree_up == 0.0, jnp.ones_like(stepped), stepped)
        too_large = jnp.abs(current) > 1e16
        shrink = jnp.where(too_large, 1e-16, 1.0)
        current = current * shrink
        previous = previous * shrink
        log_scale = log_scale + jnp.where(too_large, jnp.log(jnp.float32(1e16)), 0.0)
        legendre = jnp.where(degree <= wave_total - 1, current * jnp.exp(log_scale), 0.0)
        return (
            (current, previous, log_scale),
            ((legendre * quadrature).astype(jnp.bfloat16), legendre.astype(jnp.bfloat16)),
        )

    zeros = jnp.zeros_like(log_start)
    initial = (zeros, zeros, log_start)
    degrees_up = jnp.arange(0, wave_total, dtype=jnp.float32)
    _, tables = lax.scan(advance, initial, degrees_up, unroll=8)
    return (tables[0], tables[1])


def transform_tables(waves, lon_total, lat_total):
    lon_index = jnp.arange(lon_total, dtype=jnp.int32)
    phase_index = waves[None, :] * lon_index[:, None] % lon_total
    angles = 2.0 * jnp.pi * phase_index.astype(jnp.float32) / lon_total
    forward_table = (
        jnp.stack([jnp.cos(angles), jnp.sin(angles)], axis=2) / math.sqrt(lon_total)
    ).reshape(lon_total, 2 * waves.shape[0])
    factor = jnp.where(waves == 0, 1.0, 2.0).astype(jnp.float32) / math.sqrt(lat_total * lon_total)
    inverse_table = (
        jnp.stack([jnp.cos(angles).T, jnp.sin(angles).T], axis=1) * factor[:, None, None]
    )
    inverse_table = inverse_table.reshape(2 * waves.shape[0], lon_total)
    return (forward_table.astype(jnp.bfloat16), inverse_table.astype(jnp.bfloat16))


def per_device(
    state,
    conv_in,
    bias_in,
    conv_out,
    bias_out,
    spectral_gain,
    mix_in,
    blend_bias,
    mix_out,
    mix_out_bias,
    level_order,
    wave_order,
):
    samples, var_count, level_stack, columns = state.shape
    fields = conv_out.shape[0]
    lat_count = lax.axis_size("lat")
    lon_count = lax.axis_size("lon")
    lat_rows = NLAT // lat_count
    lon_cols = NLON // lon_count
    block_width = math.gcd(columns, 256)

    def first_block(block_index, tendency):
        column_piece = lax.dynamic_slice_in_dim(state, block_index * block_width, block_width, 3)
        hidden = jax.nn.gelu(vertical_conv(column_piece, conv_in, bias_in)).astype(jnp.bfloat16)
        result = vertical_conv(hidden, conv_out, bias_out).astype(jnp.bfloat16)
        return lax.dynamic_update_slice_in_dim(tendency, result, block_index * block_width, 3)

    tendency = lax.fori_loop(
        0,
        columns // block_width,
        first_block,
        jnp.zeros((samples, fields, level_stack, columns), jnp.bfloat16),
    )
    item_total = samples * fields * level_stack
    tendency = tendency.reshape(item_total, lat_rows, lon_cols)
    lat_total = lat_rows * lat_count
    lon_total = lon_cols * lon_count
    wave_total = wave_order.shape[0]
    owned = wave_total // lat_count
    owned_waves = lax.dynamic_slice_in_dim(wave_order, lax.axis_index("lat") * owned, owned)
    forward_basis, inverse_basis = legendre_tables(owned_waves, lat_total, wave_total)
    forward_table, inverse_table = transform_tables(wave_order, lon_total, lat_total)
    padded_gain = jnp.concatenate([spectral_gain, jnp.zeros_like(spectral_gain)])
    degree_gain = padded_gain[
        owned_waves[:, None] + jnp.arange(wave_total, dtype=jnp.int32)[None, :]
    ]
    positions = (
        jnp.zeros((item_total,), jnp.int32)
        .at[level_order]
        .set(jnp.arange(item_total, dtype=jnp.int32))
    )
    group_items = item_total // lon_count
    slab_rows = lat_rows // lon_count
    row_slabs = tendency.reshape(item_total, lon_count, slab_rows, lon_cols)
    coeffs = jnp.dot(
        lax.all_to_all(row_slabs, "lon", split_axis=1, concat_axis=3, tiled=True),
        forward_table,
        preferred_element_type=jnp.float32,
    ).astype(jnp.bfloat16)
    coeffs = jnp.take(coeffs, level_order, axis=0).reshape(
        lon_count, group_items, slab_rows, lat_count, 2 * owned
    )
    coeffs = coeffs.transpose(3, 0, 1, 2, 4).reshape(
        lat_count * lon_count, group_items, slab_rows, 2 * owned
    )
    coeffs = lax.all_to_all(coeffs, ("lat", "lon"), split_axis=0, concat_axis=2, tiled=True)
    spectral_coeffs = coeffs[0]
    item_count = spectral_coeffs.shape[0]
    by_part = spectral_coeffs.reshape(item_count, lat_total, owned, 2)
    spectral = jnp.einsum(
        "kml,nlmp->nmpk", forward_basis, by_part, preferred_element_type=jnp.float32
    )
    scaled = (spectral * degree_gain[None, :, None, :]).astype(jnp.bfloat16)
    returned = jnp.einsum(
        "kml,nmpk->nlmp", inverse_basis, scaled, preferred_element_type=jnp.float32
    ).astype(jnp.bfloat16)
    spectrum, returned = (
        spectral.reshape(item_count, owned, 2 * wave_total),
        returned.reshape(item_count, lat_total, 2 * owned),
    )
    returned = lax.all_to_all(
        returned[None], ("lat", "lon"), split_axis=2, concat_axis=0, tiled=True
    )
    returned = returned.reshape(lat_count, lon_count, group_items, slab_rows, 2 * owned).transpose(
        1, 2, 3, 0, 4
    )
    returned = jnp.take(returned.reshape(item_total, slab_rows, 2 * wave_total), positions, axis=0)
    grid_values = jnp.dot(returned, inverse_table, preferred_element_type=jnp.float32).astype(
        jnp.bfloat16
    )
    natural = lax.all_to_all(grid_values, "lon", split_axis=2, concat_axis=1, tiled=True)
    filtered = natural.reshape(samples, fields, level_stack, columns)
    joined = jnp.concatenate([filtered, state], axis=1)

    def latter_block(block_index, increment):
        column_piece = lax.dynamic_slice_in_dim(joined, block_index * block_width, block_width, 3)
        mixed_hidden = jax.nn.gelu(vertical_conv(column_piece, mix_in, blend_bias)).astype(
            jnp.bfloat16
        )
        result = vertical_conv(mixed_hidden, mix_out, mix_out_bias)
        return lax.dynamic_update_slice_in_dim(increment, result, block_index * block_width, 3)

    increment = lax.fori_loop(
        0,
        columns // block_width,
        latter_block,
        jnp.zeros((samples, var_count, level_stack, columns), jnp.float32),
    )
    return (spectrum, increment)


def solution(mesh):
    return jax.shard_map(
        per_device,
        mesh=mesh,
        in_specs=(
            P(None, None, None, ("lat", "lon")),
            P(),
            P(),
            P(),
            P(),
            P(),
            P(),
            P(),
            P(),
            P(),
            P(),
            P(),
        ),
        out_specs=(P("lon", "lat", None), P(None, None, None, ("lat", "lon"))),
        check_vma=False,
    )
```

profile of v0, /device:TPU:0, one launch (start us, length us, event | category | flops | bytes accessed | tf_op | source)
XLA Modules:
  0.0 1256.3 jit_solution(3501997547262635160)
XLA Ops:
  2.7 37.7 %while.53 = (s32[]{:T(128)}, bf16[1,2,24,4096]{3,2,1,0:T(8,128)(2,1)S(1)}, f32[2]{0:T(128)S(1)}, f32[64]{0:T(128)S(1)}, bf16[1,6,24,4096]{3,1,2,0:T(8,128)(2,1)S...) while((s32[]{:T(128)}, ...), condition=%wide.region_1.2_spmd, body=%wide.region_0.1_spmd.sunk | while | flops 23642116 | bytes 10158755 | solution.py:123
  42.9 7.6 all-to-all-start
  50.9 6.7 fusion.245
  57.8 929.2 %while.55 = (s32[]{:T(128)}, f32[43,512]{1,0:T(8,128)S(1)}, f32[43,512]{1,0:T(8,128)S(1)}, f32[43,512]{1,0:T(8,128)S(1)}, bf16[43,8,43,512]{3,2,1,0:T(8,128)(2,1...) while((s32[]{:T(128)}, f32[43,512]{1,0:T(8,128)S(1)}, ...), condition=%wide.region_3.4_spmd.clone.clone, body=%wide.region_2.3_spmd.clone.clone.sunk | while | flops 18481552 | bytes 6738488 | solution.py:76
  101.7 5.2 fusion.336
  123.3 5.2 fusion.336
  209.7 5.2 fusion.336
  274.4 5.2 fusion.336
  382.4 5.2 fusion.336
  425.7 5.2 fusion.336
  447.3 5.2 fusion.336
  468.9 5.2 fusion.336
  512.3 5.2 fusion.336
  991.9 7.9 fusion.243
  1004.9 11.3 all-to-all-start.1
  1018.3 51.9 %gather_fusion.1 = f32[14792]{0:T(1024)S(1)} fusion(f32[688]{0:T(1024)S(1)} %concatenate.20, s32[15360]{0:T(1024)S(1)} %pad_clamp_fusion), kind=kCustom, calls=%fused_computation.1 | custom fusion | bytes 177504 | tf_op jit(solution)/shard_map/gather | solution.py:139
  1070.3 14.7 %copy.116 = bf16[1,3,128,4,86]{3,2,1,4,0:T(8,128)(2,1)} copy(bf16[1,3,128,4,86]{4,3,1,2,0:T(4,128)(2,1)S(1)} %bitcast.655) | data formatting | bytes 528384 | tf_op jit(solution)/shard_map/reshape;squeeze | solution.py:164
  1084.9 17.0 %reshape.1199 = bf16[3,512,43,2]{1,0,3,2:T(4,128)(2,1)} reshape(bf16[1,3,128,4,86]{3,2,1,4,0:T(8,128)(2,1)} %copy.116) | data formatting | bytes 528384 | tf_op jit(solution)/shard_map/reshape;squeeze | solution.py:164
  1102.0 22.2 %fusion.239 = f32[3,43,2,344]{3,0,2,1:T(4,128)S(1)} fusion(bf16[3,512,43,2]{1,0,3,2:T(4,128)(2,1)} %reshape.1199, bf16[344,43,512,1]{2,1,0,3:T(8,128)(2,1)} %bitcast.628), kind=kOutput, calls=%fused_computation.383 | convolution fusion | flops 90882048 | bytes 15766208 | tf_op jit(solution)/shard_map/kml,nlmp->nmpk/dot_general | solution.py:165
  1124.1 23.3 %fusion.236 = bf16[43,3,2,512]{3,1,2,0:T(4,128)(2,1)} fusion(bf16[344,43,512,1]{2,1,0,3:T(8,128)(2,1)} %bitcast.627, f32[3,43,2,344]{3,0,2,1:T(4,128)S(1)} %fusion.239, f32[43,344]{1,0:T(8,128)S(1)} %reshape.1153), kind=kOutput, calls=%fused_computation.382 | convolution fusion | flops 91191648 | bytes 15825376 | tf_op jit(solution)/shard_map/kml,nmpk->nlmp/dot_general | solution.py:169
  1149.5 10.5 all-to-all-start.2
  1167.6 5.6 all-to-all-done.2
  1193.3 8.1 all-to-all-done.3
  1207.6 48.2 %while.54 = (s32[]{:T(128)}, f32[1,6,24,4096]{3,2,1,0:T(8,128)}, f32[6]{0:T(128)S(1)}, f32[64]{0:T(128)S(1)}, bf16[1,8,24,4096]{3,1,2,0:T(8,128)(2,1)S(1)}, /*in...) while((s32[]{:T(128)}, f32[1,6,24,4096]{3,2,1,0:T(8,128)}, ...), condition=%wide.region_6.7_spmd, body=%wide.region_5.6_spmd.sunk | while | flops 37859332 | bytes 11072675 | solution.py:198
  (1290 shorter events, 788.1 us)
Async XLA Ops:
  0.6 2.0 copy-start.2
  0.6 2.0 copy-start.10
  0.7 2.0 copy-start.7
  0.7 2.0 copy-start.9
  40.4 2.5 copy-start
  41.2 9.4 copy-start.4
  42.9 956.9 %all-to-all-start = ((bf16[16,2,6144]{2,1,0:T(2,128)(2,1)}), bf16[16,2,6144]{2,1,0:T(2,128)(2,1)S(1)}, u32[]{:S(2)}, u32[]{:S(2)}) async-start(bf16[16,2,6144]{2,1,0:T(2,128)(2,1)} %reshape.1205), calls=%async_computation | async-start | bytes 786432 | tf_op jit(solution)/shard_map/all_to_all | solution.py:151
  50.6 7.0 copy-start.11
  1004.9 65.4 %all-to-all-start.1 = ((bf16[128,3,4,86]{3,2,1,0:T(4,128)(2,1)}), bf16[128,3,4,86]{3,2,1,0:T(4,128)(2,1)S(1)}, u32[]{:S(2)}, u32[]{:S(2)}) async-start(bf16[128,3,4,86]{3,2,1,0:T(4,128)(2,1)} %copy.96), calls=%async_computation.1 | async-start | bytes 786432 | tf_op jit(solution)/shard_map/all_to_all | solution.py:161
  1016.3 2.0 copy-start.8
  1149.5 23.7 %all-to-all-start.2 = ((bf16[1,3,512,86]{3,1,0,2:T(4,128)(2,1)}), bf16[1,3,512,86]{3,1,0,2:T(4,128)(2,1)}, u32[]{:S(2)}, u32[]{:S(2)}) async-start(bf16[1,3,512,86]{3,1,0,2:T(4,128)(2,1)} %copy.102), calls=%async_computation.2 | async-start | bytes 1048576 | tf_op jit(solution)/shard_map/all_to_all | solution.py:176
  1184.2 7.8 copy-start.6
  1188.2 13.3 %all-to-all-start.3 = ((bf16[16,2,6144]{2,1,0:T(2,128)(2,1)}), bf16[16,2,6144]{2,1,0:T(2,128)(2,1)S(1)}, u32[]{:S(2)}, u32[]{:S(2)}) async-start(bf16[16,2,6144]{2,1,0:T(2,128)(2,1)} %reshape.1207), calls=%async_computation.3 | async-start | bytes 786432 | tf_op jit(solution)/shard_map/all_to_all | solution.py:186
  1202.5 2.6 copy-start.1
  1205.9 1.7 copy-start.3
  1205.9 1.7 copy-start.5
  1205.9 1.7 copy-start.12
where the time goes:
time: 1270 us; the launch traced here: 1260 us
  other arithmetic  647 us (51%)
  loops' own time  233 us (18%)
  local copies, waits for them, and re-layouts  209 us (16%)
  matrix products  120 us (9%)
  starting transfers between devices  33.4 us (3%)
  waiting for transfers between devices  13.7 us (1%)
    another operation x1, loops' own time, legendre_tables(): _, tables = lax.scan(advance, initial, degrees_up, unroll=8)  231 us
    sqrt x43, other arithmetic, advance(): jnp.sqrt((4.0 * degree * degree - 1.0) / jnp.maximum(degree * degree - wa...  225 us
    le x43, other arithmetic, advance(): degree <= wave_total - 1  223 us
    while x473, other arithmetic  134 us
    dot_general x192, matrix products, vertical_conv(): jnp.einsum('oc,sclx->solx', weight[:, kernel_tap_index], sliding_frame, p...  72.3 us
    gather x2, local copies, waits for them, and re-layouts, per_device(): padded_gain[owned_waves[:, None] + jnp.arange(wave_total, dtype=jnp.int32...  52 us
    dynamic_update_slice x43, local copies, waits for them, and re-layouts, legendre_tables(): _, tables = lax.scan(advance, initial, degrees_up, unroll=8)  42.5 us
    another operation x2, local copies, waits for them, and re-layouts, per_device(): by_part = spectral_coeffs.reshape(item_count, lat_total, owned, 2)  31.7 us
  transfers between devices with their start and end apart: 4, of which 2 were waited for; matrix products, arithmetic and copies ran while one was open for 62% of the time, Pallas kernels for 0%

commit v1 on v0

v1 whole, which is shorter than its diff:
```python
import functools
import math

import jax
import jax.numpy as jnp
import ml_dtypes
import numpy as np
from jax import lax
from jax.experimental import pallas as pl
from jax.experimental.pallas import tpu as pltpu
from jax.sharding import PartitionSpec as P

NLAT, NLON, M = 512, 1024, 344
LV, VARS, CH, FIELDS = 24, 6, 64, 2
N_LAT, N_LON = 8, 16
ROWS, COLS = NLAT // N_LAT, NLON // N_LON
COLUMNS = ROWS * COLS
TILES = COLUMNS // 128
ITEMS = FIELDS * LV
GROUP = ITEMS // N_LON
OWNED = M // N_LAT
MP = 48
KP = 352
HALF = NLAT // 2
HID = CH * LV
SLAB = 49
BF, F32 = jnp.bfloat16, jnp.float32
NT = (((1,), (1,)), ((), ()))

BLOCKS = {(0, 0): (0, 0), (0, 1): (0, 1), (1, 0): (0, 2), (1, 1): (1, 2), (2, 0): (1, 0), (2, 1): (1, 1)}


def slab_of(tile, half):
    part, item = BLOCKS[(tile, half)]
    return part * GROUP + item


def iota(shape, dim):
    return lax.broadcasted_iota(jnp.int32, shape, dim)


def over_levels(index):
    return jnp.floor((index.astype(F32) + 0.5) * (1.0 / LV)).astype(jnp.int32)


def dot(a, b):
    return jnp.dot(a, b, preferred_element_type=F32)


def row_order():
    slots = np.arange(ROWS)
    return 2 * (slots % (ROWS // 2)) + slots // (ROWS // 2)


@functools.lru_cache(None)
def constants():
    n = np.arange(M)[:, None]
    angle = 2 * np.pi * ((n * np.arange(NLON)[None, :]) % NLON) / NLON
    factor = np.where(n == 0, 1.0, 2.0) / math.sqrt(NLAT * NLON)
    trig = np.concatenate(
        [np.cos(angle) / math.sqrt(NLON), np.sin(angle) / math.sqrt(NLON), np.cos(angle) * factor, np.sin(angle) * factor],
        axis=1,
    ).astype(ml_dtypes.bfloat16)
    slots = np.arange(NLAT)
    lat = (slots // ROWS) * ROWS + row_order()[slots % ROWS]
    phi = np.pi * (lat + 0.5) / NLAT - np.pi / 2
    sine, cosine = np.sin(phi), np.cos(phi)
    quad = (np.pi * cosine / math.sqrt(NLAT)).reshape(N_LAT, 1, ROWS)
    quad = np.tile(quad, (1, 1, 2 * GROUP)).astype(np.float32)
    lat_rows = np.zeros((8, HALF), np.float32)
    lat_rows[0], lat_rows[1] = sine[:HALF], np.log(cosine[:HALF])
    start = np.zeros((1, 384), np.float32)
    start[0, :M] = [
        0.5 * math.log(0.5) + 0.5 * (math.lgamma(m + 1.5) - math.lgamma(m + 1.0) - math.lgamma(1.5)) for m in range(M)
    ]
    return trig, quad, lat_rows, start


def weights_kernel(taps, w1_ref, vcol_ref, lcol_ref, w2_ref, frow_ref, lrow_ref, b2_ref, o1_ref, o2_ref, ob_ref):
    width = vcol_ref.shape[1]
    rows = frow_ref.shape[0]
    variables = taps // 3
    weights = w1_ref[...]
    r = iota((HID, CH), 0)
    spread = (over_levels(r) == iota((HID, CH), 1)).astype(F32).astype(BF)
    level_row = iota((HID, width), 0)
    level_row = level_row - LV * over_levels(level_row)
    level_col = lcol_ref[...]
    var_col = vcol_ref[...]
    pick = iota((weights.shape[1], width), 0)
    total = jnp.zeros((HID, width), F32)
    for tap in range(3):
        chosen = (pick == tap * variables + var_col).astype(F32).astype(BF)
        block = (0.5 * dot(weights.astype(BF), chosen)).astype(BF)
        wide = dot(spread, block)
        total = jnp.where(level_col == level_row + 2 * (tap - 1), wide, total)
    bias = 0.5 * weights[:, taps : taps + 1]
    high = bias.astype(BF).astype(F32)
    low = bias - high
    lane = iota((CH, width), 1)
    block = jnp.where(lane == width - 16, high, jnp.where(lane == width - 15, low, 0.0)).astype(BF)
    o1_ref[...] = (total + dot(spread, block)).astype(BF)
    second = w2_ref[...]
    c = iota((CH, HID), 1)
    spread2 = (over_levels(c) == iota((CH, HID), 0)).astype(F32).astype(BF)
    level_hid = iota((rows, HID), 1)
    level_hid = level_hid - LV * over_levels(level_hid)
    frow, lrow = frow_ref[...], lrow_ref[...]
    lane2 = iota((rows, second.shape[0]), 1)
    total2 = jnp.zeros((rows, HID), F32)
    for tap in range(3):
        chosen = (lane2 == 3 * frow + tap).astype(F32).astype(BF)
        block = dot(chosen, second.astype(BF)).astype(BF)
        wide = dot(block, spread2)
        total2 = jnp.where(level_hid == lrow + 2 * (tap - 1), wide, total2)
    o2_ref[...] = total2.astype(BF)
    bias2 = jnp.zeros((rows, 128), F32)
    for field in range(b2_ref.shape[0]):
        bias2 = jnp.where(frow == field, b2_ref[field], bias2)
    ob_ref[...] = bias2


def build_weights(w1, bias1, w2, bias2, vcol, lcol, frow, lrow):
    taps = 3 * w1.shape[2]
    w1p = jnp.concatenate([w1.reshape(CH, taps).astype(F32), bias1[:, None], jnp.zeros((CH, 31 - taps), F32)], axis=1)
    fields = w2.shape[0]
    w2p = jnp.pad(w2.reshape(3 * fields, CH).astype(F32), ((0, 32 - 3 * fields), (0, 0)))
    width, rows = vcol.shape[1], frow.shape[0]
    vmem = pl.BlockSpec(memory_space=pltpu.VMEM)
    return pl.pallas_call(
        functools.partial(weights_kernel, taps),
        out_shape=(
            jax.ShapeDtypeStruct((HID, width), BF),
            jax.ShapeDtypeStruct((rows, HID), BF),
            jax.ShapeDtypeStruct((rows, 128), F32),
        ),
        in_specs=[vmem] * 6 + [pl.BlockSpec(memory_space=pltpu.SMEM)],
        out_specs=(vmem, vmem, vmem),
        compiler_params=pltpu.CompilerParams(vmem_limit_bytes=40 * 2**20),
        cost_estimate=pl.CostEstimate(flops=2 * 10**8, bytes_accessed=2 * 10**6, transcendentals=0),
        name="build_weights",
    )(w1p, vcol, lcol, w2p, frow, lrow, bias2)


def hidden_layer(w1_ref, w2_ref, v_ref, h_ref):
    block = v_ref.shape[1]
    step = 256
    for col in range(0, block, step):
        for row in range(0, HID, 256):
            y = dot(w1_ref[row : row + 256, :], v_ref[:, col : col + step])
            u = y * (2 * math.sqrt(2 / math.pi) + (8 * 0.044715 * math.sqrt(2 / math.pi)) * (y * y))
            h_ref[row : row + 256, col : col + step] = (y + y * jnp.tanh(u)).astype(BF)
    return dot(w2_ref[...], h_ref[...])


def first_kernel(block, state_ref, w1_ref, w2_ref, b2_ref, out_ref, v_ref, h_ref, o_ref):
    step = pl.program_id(0)

    @pl.when(step == 0)
    def _():
        v_ref[VARS * LV :, :] = jnp.ones((16, block), BF)

    v_ref[: VARS * LV, :] = state_ref[...]
    result = hidden_layer(w1_ref, w2_ref, v_ref, h_ref)
    bias = b2_ref[...]
    for tile in range(block // 128):
        o_ref[pl.ds(step * (block // 128) + tile, ITEMS, stride=TILES + 1), :] = result[:, tile * 128 : (tile + 1) * 128] + bias

    @pl.when(step == pl.num_programs(0) - 1)
    def _():
        for item in range(ITEMS):
            out_ref[item] = o_ref[item * (TILES + 1) : item * (TILES + 1) + TILES, :].astype(BF)


def first_conv(state, w1, w2, b2, block=512):
    full = lambda *shape: pl.BlockSpec(shape, lambda i: (0,) * len(shape))
    return pl.pallas_call(
        functools.partial(first_kernel, block),
        grid=(COLUMNS // block,),
        out_shape=jax.ShapeDtypeStruct((ITEMS, TILES, 128), BF),
        in_specs=[
            pl.BlockSpec((VARS * LV, block), lambda i: (0, i)),
            full(HID, VARS * LV + 16),
            full(ITEMS, HID),
            full(ITEMS, 128),
        ],
        out_specs=full(ITEMS, TILES, 128),
        scratch_shapes=[
            pltpu.VMEM((VARS * LV + 16, block), BF),
            pltpu.VMEM((HID, block), BF),
            pltpu.VMEM((ITEMS * (TILES + 1), 128), F32),
        ],
        compiler_params=pltpu.CompilerParams(vmem_limit_bytes=40 * 2**20),
        cost_estimate=pl.CostEstimate(flops=3 * 10**9, bytes_accessed=2 * 10**6, transcendentals=HID * COLUMNS),
        name="first_conv",
    )(state, w1, w2, b2)


def second_kernel(block, state_ref, filt_ref, w1_ref, w2_ref, b2_ref, out_ref, v_ref, h_ref, f_ref):
    step = pl.program_id(0)
    base = VARS * LV

    @pl.when(step == 0)
    def _():
        v_ref[base + ITEMS :, :] = jnp.ones((16, block), BF)
        for item in range(ITEMS):
            f_ref[item * (TILES + 1) : item * (TILES + 1) + TILES, :] = filt_ref[item].astype(F32)

    v_ref[:base, :] = state_ref[...]
    for tile in range(block // 128):
        piece = f_ref[pl.ds(step * (block // 128) + tile, ITEMS, stride=TILES + 1), :]
        v_ref[base : base + ITEMS, tile * 128 : (tile + 1) * 128] = piece.astype(BF)
    result = hidden_layer(w1_ref, w2_ref, v_ref, h_ref)
    bias = b2_ref[...]
    for tile in range(block // 128):
        out_ref[:, tile * 128 : (tile + 1) * 128] = result[:, tile * 128 : (tile + 1) * 128] + bias


def second_conv(state, filtered, w1, w2, b2, block=512):
    full = lambda *shape: pl.BlockSpec(shape, lambda i: (0,) * len(shape))
    width = VARS * LV + ITEMS + 16
    return pl.pallas_call(
        functools.partial(second_kernel, block),
        grid=(COLUMNS // block,),
        out_shape=jax.ShapeDtypeStruct((VARS * LV, COLUMNS), F32),
        in_specs=[
            pl.BlockSpec((VARS * LV, block), lambda i: (0, i)),
            full(ITEMS, TILES, 128),
            full(HID, width),
            full(VARS * LV, HID),
            full(VARS * LV, 128),
        ],
        out_specs=pl.BlockSpec((VARS * LV, block), lambda i: (0, i)),
        scratch_shapes=[
            pltpu.VMEM((width, block), BF),
            pltpu.VMEM((HID, block), BF),
            pltpu.VMEM((ITEMS * (TILES + 1), 128), F32),
        ],
        compiler_params=pltpu.CompilerParams(vmem_limit_bytes=40 * 2**20),
        cost_estimate=pl.CostEstimate(flops=4 * 10**9, bytes_accessed=4 * 10**6, transcendentals=HID * COLUMNS),
        name="second_conv",
    )(state, filtered, w1, w2, b2)


CHUNK = 16
STRIDE = CHUNK + 1


def table_kernel(wave_ref, lat_ref, start_ref, out_ref, now_ref, old_ref, log_ref, ratio_ref, s_ref):
    step = pl.program_id(0)
    wave = jnp.broadcast_to(wave_ref[...], (MP, 128))
    sine = [lat_ref[0:1, 128 * h : 128 * h + 128] for h in range(2)]

    @pl.when(step == 0)
    def _():
        match = iota((MP, 384), 1).astype(F32) == wave_ref[...]
        start = jnp.sum(jnp.where(match, start_ref[...], 0.0), axis=1, keepdims=True)
        for h in range(2):
            log_cos = lat_ref[1:2, 128 * h : 128 * h + 128]
            log_ref[h] = jnp.where(wave > 500.0, -1e4, start + wave * log_cos)
            now_ref[h] = jnp.zeros((MP, 128), F32)
            old_ref[h] = jnp.zeros((MP, 128), F32)
        ratio_ref[...] = jnp.zeros((MP, 128), F32)

    now = [now_ref[h] for h in range(2)]
    old = [old_ref[h] for h in range(2)]
    log_scale = [log_ref[h] for h in range(2)]
    ratio = ratio_ref[...]
    scale = [None, None]
    first = (step * CHUNK).astype(F32)
    for kk in range(CHUNK):
        if kk % 8 == 0:
            for h in range(2):
                big = jnp.abs(now[h]) > 1e8
                shrink = jnp.where(big, 1e-12, 1.0)
                now[h] = now[h] * shrink
                old[h] = old[h] * shrink
                log_scale[h] = log_scale[h] + jnp.where(big, math.log(1e12), 0.0)
                scale[h] = jnp.exp(log_scale[h])
        k = first + kk
        n = wave + k
        top = 4.0 * (n * n) - 1.0
        bottom = k * (wave + n)
        root = lax.rsqrt(jnp.maximum(top * bottom, 1e-30))
        up = jnp.where(n <= M - 1.0, top * root, 0.0)
        for h in range(2):
            stepped = up * (sine[h] * now[h] - ratio * old[h])
            if kk == 0:
                stepped = jnp.where(step == 0, 1.0, stepped)
            old[h], now[h] = now[h], stepped
            s_ref[h, pl.ds(kk, MP, stride=STRIDE), :] = stepped * scale[h]
        ratio = bottom * root
    for h in range(2):
        now_ref[h], old_ref[h], log_ref[h] = now[h], old[h], log_scale[h]
    ratio_ref[...] = ratio
    for m in range(MP):
        for h in range(2):
            out_ref[m, :, 128 * h : 128 * h + 128] = s_ref[h, m * STRIDE : m * STRIDE + CHUNK, :].astype(BF)


def legendre_table(waves_f, lat_rows, start):
    full = lambda *shape: pl.BlockSpec(shape, lambda i: (0,) * len(shape))
    return pl.pallas_call(
        table_kernel,
        grid=(KP // CHUNK,),
        out_shape=jax.ShapeDtypeStruct((MP, KP, HALF), BF),
        in_specs=[full(MP, 1), full(8, HALF), full(1, 384)],
        out_specs=pl.BlockSpec((MP, CHUNK, HALF), lambda i: (0, i, 0)),
        scratch_shapes=[pltpu.VMEM((2, MP, 128), F32)] * 3
        + [pltpu.VMEM((MP, 128), F32), pltpu.VMEM((2, MP * STRIDE, 128), F32)],
        compiler_params=pltpu.CompilerParams(vmem_limit_bytes=32 * 2**20),
        cost_estimate=pl.CostEstimate(flops=2 * 10**8, bytes_accessed=9 * 10**6, transcendentals=0),
        name="legendre_table",
    )(waves_f, lat_rows, start)


def swap_halves(x):
    return pltpu.roll(x, 64, 1)


def forward_kernel(y_ref, f_ref, g_ref, q_ref, out_ref, x0_ref, x1_ref):
    low = iota((TILES, 128), 1) < 64
    x0_ref[192:256, :] = jnp.zeros((64, NLON), BF)
    x1_ref[0:64, :] = jnp.zeros((64, NLON), BF)
    place0, place1 = (0, 64, 128), (128, 192, 64)
    for pair in range(N_LON // 2):
        for item in range(GROUP):
            a = y_ref[2 * pair, item].astype(F32)
            b = y_ref[2 * pair + 1, item].astype(F32)
            even = jnp.where(low, a, swap_halves(b)).astype(BF)
            odd = jnp.where(low, swap_halves(a), b).astype(BF)
            lanes = slice(128 * pair, 128 * pair + 128)
            for ref, place in ((x0_ref, place0), (x1_ref, place1)):
                ref[place[item] : place[item] + 32, lanes] = even
                ref[place[item] + 32 : place[item] + 64, lanes] = odd
    quad = q_ref[...]
    cosines = lax.dot_general(f_ref[...], x0_ref[...], NT, preferred_element_type=F32)
    sines = lax.dot_general(g_ref[...], x1_ref[...], NT, preferred_element_type=F32)
    tiles = (cosines[:, :128], cosines[:, 128:] + sines[:, :128], sines[:, 128:])
    for t, value in enumerate(tiles):
        value = (value * quad[:, 128 * t : 128 * t + 128]).astype(BF)
        for group in range(N_LAT):
            out_ref[group, :, 128 * t : 128 * t + 128] = value[group * MP : (group + 1) * MP]


def forward_fourier(pieces, tables, quad):
    full = lambda *shape: pl.BlockSpec(shape, lambda i: (0,) * len(shape))
    return pl.pallas_call(
        forward_kernel,
        grid=(1,),
        out_shape=jax.ShapeDtypeStruct((N_LAT, MP, 384), BF),
        in_specs=[
            full(N_LON, GROUP, TILES, 128),
            pl.BlockSpec((N_LAT * MP, NLON), lambda i: (0, 0)),
            pl.BlockSpec((N_LAT * MP, NLON), lambda i: (0, 1)),
            full(1, 384),
        ],
        out_specs=full(N_LAT, MP, 384),
        scratch_shapes=[pltpu.VMEM((256, NLON), BF)] * 2,
        compiler_params=pltpu.CompilerParams(vmem_limit_bytes=32 * 2**20),
        cost_estimate=pl.CostEstimate(flops=4 * 10**8, bytes_accessed=3 * 10**6, transcendentals=0),
        name="forward_fourier",
    )(pieces, tables, tables, quad)


def inverse_kernel(r_ref, f_ref, g_ref, out_ref):
    turned = [r_ref[:, 128 * t : 128 * t + 128].astype(F32).T.astype(BF) for t in range(3)]
    cosines = jnp.concatenate([turned[0], turned[1][:64]], axis=0)
    sines = jnp.concatenate([turned[2], turned[1][64:]], axis=0)
    grid = dot(cosines, f_ref[...]) + dot(sines, g_ref[...])
    low = iota((TILES, 128), 1) < 64
    for pair in range(N_LON // 2):
        for item in range(GROUP):
            lanes = slice(128 * pair, 128 * pair + 128)
            even = grid[64 * item : 64 * item + 32, lanes]
            odd = grid[64 * item + 32 : 64 * item + 64, lanes]
            out_ref[2 * pair, item] = jnp.where(low, even, swap_halves(odd)).astype(BF)
            out_ref[2 * pair + 1, item] = jnp.where(low, swap_halves(even), odd).astype(BF)


def inverse_fourier(returned, tables):
    full = lambda *shape: pl.BlockSpec(shape, lambda i: (0,) * len(shape))
    return pl.pallas_call(
        inverse_kernel,
        grid=(1,),
        out_shape=jax.ShapeDtypeStruct((N_LON, GROUP, TILES, 128), BF),
        in_specs=[
            full(N_LAT * MP, 384),
            pl.BlockSpec((N_LAT * MP, NLON), lambda i: (0, 2)),
            pl.BlockSpec((N_LAT * MP, NLON), lambda i: (0, 3)),
        ],
        out_specs=full(N_LON, GROUP, TILES, 128),
        compiler_params=pltpu.CompilerParams(vmem_limit_bytes=32 * 2**20),
        cost_estimate=pl.CostEstimate(flops=4 * 10**8, bytes_accessed=3 * 10**6, transcendentals=0),
        name="inverse_fourier",
    )(returned, tables, tables)


WAVES = 8


def spectral_kernel(wave_ref, x_ref, t_ref, gain_ref, spec_ref, out_ref, c_ref, n_ref, r_ref, m_ref):
    step = pl.program_id(0)
    low = iota((MP, 128), 1) < 64
    mirror = (iota((HALF, HALF), 0) + iota((HALF, HALF), 1) == HALF - 1).astype(F32).astype(BF)

    @pl.when(step == 0)
    def _():
        for slab in (6, 7, 14, 15):
            for h in range(2):
                c_ref[h, slab * SLAB : slab * SLAB + MP, :] = jnp.zeros((MP, 128), F32)
        north = {}
        for pair in range(N_LAT // 2):
            for tile in range(3):
                a = x_ref[2 * pair, :, 128 * tile : 128 * tile + 128].astype(F32)
                b = x_ref[2 * pair + 1, :, 128 * tile : 128 * tile + 128].astype(F32)
                both = jnp.where(low, a, swap_halves(b)), jnp.where(low, swap_halves(a), b)
                for half in range(2):
                    slab = slab_of(tile, half)
                    if pair < 2:
                        c_ref[pair, slab * SLAB : slab * SLAB + MP, :] = both[half]
                    else:
                        m_ref[slab * MP : slab * MP + MP, 128 * (pair - 2) : 128 * (pair - 2) + 128] = both[half].astype(BF)
        turned = dot(m_ref[...], mirror)
        for slab in range(6):
            for h in range(2):
                a = c_ref[h, slab * SLAB : slab * SLAB + MP, :]
                b = turned[slab * MP : slab * MP + MP, 128 * h : 128 * h + 128]
                c_ref[h, slab * SLAB : slab * SLAB + MP, :] = a + b
                c_ref[h, (8 + slab) * SLAB : (8 + slab) * SLAB + MP, :] = a - b

    even = iota((8, KP), 1) % 2 == 0
    gain = gain_ref[...]
    for mm in range(WAVES):
        m = step * WAVES + mm
        left = jnp.concatenate([c_ref[h, pl.ds(m, 16, stride=SLAB), :] for h in range(2)], axis=1).astype(BF)
        table = t_ref[mm]
        both = lax.dot_general(left, table, NT, preferred_element_type=F32)
        natural = jnp.where(even, both[:8], both[8:])
        n_ref[0, pl.ds(m, 8, stride=SLAB), :] = natural[:, :128]
        n_ref[1, pl.ds(m, 8, stride=SLAB), :] = natural[:, 128:256]
        n_ref[2, pl.ds(m, 8, stride=SLAB), :] = jnp.concatenate([natural[:, 256:], jnp.zeros((8, 384 - KP), F32)], axis=1)
        scaled = natural * pltpu.roll(gain, 768 - wave_ref[m], 1)[:, :KP]
        right = jnp.concatenate([jnp.where(even, scaled, 0.0), jnp.where(even, 0.0, scaled)], axis=0).astype(BF)
        back = dot(right, table)
        north, south = back[:8] + back[8:], back[:8] - back[8:]
        for h in range(2):
            r_ref[h, pl.ds(m, 8, stride=SLAB), :] = north[:, 128 * h : 128 * h + 128]
            r_ref[2 + h, pl.ds(m, 8, stride=SLAB), :] = south[:, 128 * h : 128 * h + 128]

    @pl.when(step == pl.num_programs(0) - 1)
    def _():
        for slab in range(6):
            for h in range(2):
                m_ref[slab * MP : slab * MP + MP, 128 * h : 128 * h + 128] = r_ref[2 + h, slab * SLAB : slab * SLAB + MP, :].astype(BF)
        turned = dot(m_ref[...], mirror)

        def tile_of(slab, j):
            if j < 2:
                return r_ref[j, slab * SLAB : slab * SLAB + MP, :]
            return turned[slab * MP : slab * MP + MP, 128 * (j - 2) : 128 * (j - 2) + 128]

        for pair in range(N_LAT // 2):
            for tile in range(3):
                a = tile_of(slab_of(tile, 0), pair)
                b = tile_of(slab_of(tile, 1), pair)
                lanes = slice(128 * tile, 128 * tile + 128)
                out_ref[2 * pair, :, lanes] = jnp.where(low, a, swap_halves(b)).astype(BF)
                out_ref[2 * pair + 1, :, lanes] = jnp.where(low, swap_halves(a), b).astype(BF)
        wide = iota((MP, 768), 1) < M
        zeros = jnp.zeros((MP, 384), F32)
        for item in range(GROUP):
            parts = []
            for part in range(2):
                at = (part * GROUP + item) * SLAB
                parts.append(jnp.concatenate([n_ref[h, at : at + MP, :] for h in range(3)] + [zeros], axis=1))
            value = jnp.where(wide, parts[0], pltpu.roll(parts[1], M, 1))
            spec_ref[item] = value[:OWNED, : 2 * M]


def spectral_step(waves, coeffs, table, gain):
    full = lambda *shape: pl.BlockSpec(shape, lambda i, w: (0,) * len(shape))
    return pl.pallas_call(
        spectral_kernel,
        grid_spec=pltpu.PrefetchScalarGridSpec(
            num_scalar_prefetch=1,
            grid=(MP // WAVES,),
            in_specs=[
                full(N_LAT, MP, 384),
                pl.BlockSpec((WAVES, KP, HALF), lambda i, w: (i, 0, 0)),
                full(8, 768),
            ],
            out_specs=(full(GROUP, OWNED, 2 * M), full(N_LAT, MP, 384)),
            scratch_shapes=[
                pltpu.VMEM((2, 16 * SLAB, 128), F32),
                pltpu.VMEM((3, 8 * SLAB, 128), F32),
                pltpu.VMEM((4, 8 * SLAB, 128), F32),
                pltpu.VMEM((6 * MP, HALF), BF),
            ],
        ),
        out_shape=(
            jax.ShapeDtypeStruct((GROUP, OWNED, 2 * M), F32),
            jax.ShapeDtypeStruct((N_LAT, MP, 384), BF),
        ),
        compiler_params=pltpu.CompilerParams(vmem_limit_bytes=40 * 2**20),
        cost_estimate=pl.CostEstimate(flops=4 * 10**9, bytes_accessed=10**7, transcendentals=0),
        name="spectral_step",
    )(waves, coeffs, table, gain)


def per_device(
    state, conv_in, bias_in, conv_out, bias_out, spectral_gain, mix_in, blend_bias, mix_out, mix_out_bias, level_order, wave_order
):
    trig, quad, lat_rows, start = constants()
    band = lax.axis_index("lat")
    columns = state.reshape(VARS * LV, COLUMNS)

    slot_field = (level_order >= LV).astype(jnp.int32)
    slot_level = level_order - LV * slot_field
    state_rows = np.arange(VARS * LV, dtype=np.int32)
    none = np.full((16,), -100, np.int32)
    w1, w2, b2 = build_weights(
        conv_in,
        bias_in,
        conv_out,
        bias_out,
        jnp.asarray(np.concatenate([state_rows // LV, none])[None]),
        jnp.asarray(np.concatenate([state_rows % LV, none])[None]),
        slot_field[:, None],
        slot_level[:, None],
    )
    tendency = first_conv(columns, w1, w2, b2)
    pieces = lax.all_to_all(tendency.reshape(N_LON, GROUP, TILES, 128), "lon", 0, 0, tiled=True)

    grouped = jnp.pad(wave_order.reshape(N_LAT, OWNED), ((0, 0), (0, MP - OWNED)), constant_values=-1)
    chosen = (grouped.reshape(N_LAT * MP)[:, None] == jnp.arange(M, dtype=jnp.int32)[None, :]).astype(BF)
    tables = dot(chosen, jnp.asarray(trig)).astype(BF)
    owned = lax.dynamic_slice_in_dim(grouped, band, 1, 0)[0]
    waves_f = jnp.where(owned < 0, 1000, owned).astype(F32)[:, None]
    table = legendre_table(waves_f, jnp.asarray(lat_rows), jnp.asarray(start))
    band_quad = lax.dynamic_slice_in_dim(jnp.asarray(quad), band, 1, 0)[0]
    gain = jnp.broadcast_to(jnp.pad(spectral_gain, (0, 768 - M))[None], (8, 768))

    coeffs = forward_fourier(pieces, tables, band_quad)
    coeffs = lax.all_to_all(coeffs, "lat", 0, 0, tiled=True)
    spectrum, returned = spectral_step(jnp.maximum(owned, 0), coeffs, table, gain)
    returned = lax.all_to_all(returned, "lat", 0, 0, tiled=True)
    grid_values = inverse_fourier(returned.reshape(N_LAT * MP, 384), tables)
    filtered = lax.all_to_all(grid_values, "lon", 0, 0, tiled=True)

    m1, m2, mb = build_weights(
        mix_in,
        blend_bias,
        mix_out,
        mix_out_bias,
        jnp.concatenate([jnp.asarray(FIELDS + state_rows // LV), slot_field, jnp.asarray(none)])[None],
        jnp.concatenate([jnp.asarray(state_rows % LV), slot_level, jnp.asarray(none)])[None],
        jnp.asarray(state_rows // LV)[:, None],
        jnp.asarray(state_rows % LV)[:, None],
    )
    increment = second_conv(columns, filtered.reshape(ITEMS, TILES, 128), m1, m2, mb)
    return spectrum, increment.reshape(1, VARS, LV, COLUMNS)


def solution(mesh):
    return jax.shard_map(
        per_device,
        mesh=mesh,
        in_specs=(P(None, None, None, ("lat", "lon")),) + (P(),) * 11,
        out_specs=(P("lon", "lat", None), P(None, None, None, ("lat", "lon"))),
        check_vma=False,
    )
```

time: 1270 us -> 116 us (0.09); the launches traced: 1260 us -> 115 us
  other arithmetic: 647 us -> 4.13 us
  loops' own time: 233 us -> 0 us
  local copies, waits for them, and re-layouts: 209 us -> 18.6 us
  matrix products: 120 us -> 3.64 us
  Pallas kernels: 0 us -> 49.8 us
    another operation x3 -> x0, loops' own time: 233 us -> none  [the longest x1 231 us: legendre_tables(): _, tables = lax.scan(advance, initial, degrees_up, unroll=8)]
    sqrt x43 -> x0, other arithmetic: 225 us -> none  [advance(): jnp.sqrt((4.0 * degree * degree - 1.0) / jnp.maximum(degree * degree - wa...]
    le x43 -> x0, other arithmetic: 223 us -> none  [advance(): degree <= wave_total - 1]
    while x473 -> x0, other arithmetic: 134 us -> none
    dot_general x196 -> x1, matrix products: 120 us -> 3.64 us  [dot(): return jnp.dot(a, b, preferred_element_type=F32)]
    gather x5 -> x0, local copies, waits for them, and re-layouts: 55.8 us -> none  [the longest x2 52 us: per_device(): padded_gain[owned_waves[:, None] + jnp.arange(wave_total, dtype=jnp.int32...]
    dynamic_update_slice x75 -> x0, local copies, waits for them, and re-layouts: 54.1 us -> none  [the longest x43 42.5 us: legendre_tables(): _, tables = lax.scan(advance, initial, degrees_up, unroll=8)]
    pallas_call x0 -> x8, Pallas kernels: none -> 49.8 us  [the longest x1 11.1 us: second_conv(): pl.pallas_call(functools.partial(second_kernel, block), grid=(COLUMNS //...]
  transfers between devices with their start and end apart: 4 -> 4, of which waited for: 2 -> 3; matrix products, arithmetic and copies ran while one was open for 62% -> 6% of each run, Pallas kernels for 0% -> 12%
where the time goes in v1:
time: 116 us; the launch traced here: 115 us
  Pallas kernels  49.8 us (43%)
  starting transfers between devices  20.9 us (18%)
  local copies, waits for them, and re-layouts  18.6 us (16%)
  waiting for transfers between devices  17.4 us (15%)
  other arithmetic  4.13 us (4%)
  matrix products  3.64 us (3%)
    unnamed x45, local copies, waits for them, and re-layouts  14.9 us
    pallas_call x1, Pallas kernels, second_conv(): pl.pallas_call(functools.partial(second_kernel, block), grid=(COLUMNS //...  11.1 us
    pallas_call x1, Pallas kernels, legendre_table(): pl.pallas_call(table_kernel, grid=(KP // CHUNK,), out_shape=jax.ShapeDtyp...  11 us
    pallas_call x1, Pallas kernels, first_conv(): pl.pallas_call(functools.partial(first_kernel, block), grid=(COLUMNS // b...  10.5 us
    pallas_call x1, Pallas kernels, spectral_step(): pl.pallas_call(spectral_kernel, grid_spec=pltpu.PrefetchScalarGridSpec(nu...  9.87 us
    all_to_all x1, waiting for transfers between devices, per_device(): returned = lax.all_to_all(returned, 'lat', 0, 0, tiled=True)  7.87 us
    all_to_all x1, starting transfers between devices, per_device(): lax.all_to_all(tendency.reshape(N_LON, GROUP, TILES, 128), 'lon', 0, 0, t...  7.12 us
    all_to_all x1, starting transfers between devices, per_device(): coeffs = lax.all_to_all(coeffs, 'lat', 0, 0, tiled=True)  5.31 us
  transfers between devices with their start and end apart: 4, of which 3 were waited for; matrix products, arithmetic and copies ran while one was open for 6% of the time, Pallas kernels for 12%

profile of v1, /device:TPU:0, one launch (start us, length us, event | category | flops | bytes accessed | tf_op | source)
XLA Modules:
  0.0 115.4 jit_solution(17225606702503240445)
XLA Ops:
  0.6 1.2 %compare_convert_fusion = (s32[48]{0:T(128)}, s32[48,1]{0,1:T(1,128)S(1)}) fusion(s32[48]{0:T(128)} %param.33), kind=kLoop, calls=%fused_computation.14 | loop fusion | flops 96 | bytes 576 | tf_op jit(solution)/shard_map/convert_element_type | solution.py:518
  1.8 1.2 %fusion.2 = (s32[48]{0:T(128)}, s32[48,1]{0,1:T(1,128)S(1)}) fusion(s32[48]{0:T(128)} %param.33), kind=kLoop, calls=%fused_computation.15 | loop fusion | flops 144 | bytes 576 | tf_op jit(solution)/shard_map/sub | solution.py:519
  7.7 2.5 %build_weights.2 = (bf16[1536,160]{1,0:T(8,128)(2,1)S(1)}, bf16[48,1536]{1,0:T(8,128)(2,1)S(1)}, f32[48,128]{1,0:T(8,128)S(1)}) custom-call(f32[64,32]{1,0:T(8,128)S(1)} %maximum_maximum_fusion.w1_ref, s32[1,160]{1,0:T(1,128)S(1)} %copy-done.12, s32[1,160]{1,0:T(1,128)S(1)} %copy-done.13, f32[32,64]{1,0:T(8,128)S(1)} %pad_convert_fusion.1.w2_ref, ...), custom_call_target="tpu_custom_call" | custom-call | flops 200000000 | bytes 2000000 | tf_op jit(solution)/shard_map/build_weights/pallas_call | solution.py:130
  10.1 1.3 %copy-done.6 = bf16[1,6,24,4096]{3,2,1,0:T(8,128)(2,1)S(1)} copy-done((bf16[1,6,24,4096]{3,2,1,0:T(8,128)(2,1)S(1)}, bf16[1,6,24,4096]{3,2,1,0:T(8,128)(2,1)}, u32[]{:S(2)}) %copy-start.6) | copy-done | bytes 1179672
  11.4 10.5 %first_conv.1 = bf16[48,32,128]{2,1,0:T(8,128)(2,1)} custom-call(bf16[144,4096]{1,0:T(8,128)(2,1)S(1)} %bitcast.29, bf16[1536,160]{1,0:T(8,128)(2,1)S(1)} %get-tuple-element.10.w1_ref, bf16[48,1536]{1,0:T(8,128)(2,1)S(1)} %get-tuple-element.11.w2_ref, f32[48,128]{1,0:T(8,128)S(1)} %get-tuple-element.12.b2_ref), custom_call_target="tpu_custom_call" | custom-call | flops 3000000000 | bytes 2000000 | tf_op jit(solution)/shard_map/first_conv/pallas_call | solution.py:177
  21.9 7.1 %all-to-all-start = ((bf16[16,3,32,128]{3,2,1,0:T(8,128)(2,1)}), bf16[16,3,32,128]{3,2,1,0:T(8,128)(2,1)S(1)}, u32[]{:S(2)}, u32[]{:S(2)}) async-start(bf16[16,3,32,128]{3,2,1,0:T(8,128)(2,1)} %bitcast.5), calls=%async_computation | async-start | bytes 786432 | tf_op jit(solution)/shard_map/all_to_all | solution.py:533
  30.4 3.6 %convolution_convert_fusion.f_ref.g_ref = bf16[384,4096]{1,0:T(8,128)(2,1)S(1)} fusion(bf16[344,4096]{1,0:T(8,128)(2,1)} %constant.46.clone, s32[384]{0:T(512)S(1)} %eq.15), kind=kOutput, calls=%fused_computation | convolution fusion | flops 1083835392 | bytes 5965312 | tf_op jit(solution)/shard_map/dot_general | solution.py:47
  34.1 4.8 %all-to-all-done.y_ref = bf16[16,3,32,128]{3,2,1,0:T(8,128)(2,1)S(1)} async-done(((bf16[16,3,32,128]{3,2,1,0:T(8,128)(2,1)}), bf16[16,3,32,128]{3,2,1,0:T(8,128)(2,1)S(1)}, u32[]{:S(2)}, u32[]{:S(2)}) %all-to-all-start) | async-done | bytes 393248 | tf_op jit(solution)/shard_map/all_to_all | solution.py:533
  40.3 5.3 %all-to-all-start.1 = ((bf16[8,48,384]{2,1,0:T(8,128)(2,1)}), bf16[8,48,384]{2,1,0:T(8,128)(2,1)S(1)}, u32[]{:S(2)}, u32[]{:S(2)}) async-start(bf16[8,48,384]{2,1,0:T(8,128)(2,1)} %copy-done.2), calls=%async_computation.1 | async-start | bytes 589824 | tf_op jit(solution)/shard_map/all_to_all | solution.py:545
  45.6 0.8 fusion.3
  47.2 11.0 %legendre_table.1.t_ref = bf16[48,352,256]{2,1,0:T(8,128)(2,1)S(1)} custom-call(f32[48,1]{1,0:T(8,128)S(1)} %fusion.1.wave_ref, f32[8,256]{1,0:T(8,128)S(1)} %copy-done.4, f32[1,384]{1,0:T(1,128)S(1)} %copy-done.5), custom_call_target="tpu_custom_call" | custom-call | flops 200000000 | bytes 9000000 | tf_op jit(solution)/shard_map/legendre_table/pallas_call | solution.py:303
  58.2 3.4 %copy-done = bf16[48,352,256]{2,1,0:T(8,128)(2,1)} copy-done((bf16[48,352,256]{2,1,0:T(8,128)(2,1)}, bf16[48,352,256]{2,1,0:T(8,128)(2,1)S(1)}, u32[]{:S(2)}) %copy-start) | copy-done | bytes 8650776
  61.6 3.5 %copy-done.1 = bf16[48,352,256]{2,1,0:T(8,128)(2,1)S(1)} copy-done((bf16[48,352,256]{2,1,0:T(8,128)(2,1)S(1)}, bf16[48,352,256]{2,1,0:T(8,128)(2,1)}, u32[]{:S(2)}) %copy-start.1) | copy-done | bytes 8650776
  65.1 9.9 %spectral_step.1 = (f32[3,43,688]{2,1,0:T(8,128)}, bf16[8,48,384]{2,1,0:T(8,128)(2,1)S(1)}) custom-call(s32[48]{0:T(128)S(1)} %get-tuple-element.19.wave_ref, bf16[8,48,384]{2,1,0:T(8,128)(2,1)S(1)} %all-to-all-done.1.x_ref, bf16[48,352,256]{2,1,0:T(8,128)(2,1)S(1)} %copy-done.1, f32[8,768]{1,0:T(8,128)S(1)} %broadcast_in_dim.47.gain_ref), custom_call_target="tpu_custom_call" | custom-call | flops 4000000000 | bytes 10000000 | tf_op jit(solution)/shard_map/spectral_step/pallas_call | solution.py:483
  75.6 4.8 %all-to-all-start.2 = ((bf16[8,48,384]{2,1,0:T(8,128)(2,1)}), bf16[8,48,384]{2,1,0:T(8,128)(2,1)S(1)}, u32[]{:S(2)}, u32[]{:S(2)}) async-start(bf16[8,48,384]{2,1,0:T(8,128)(2,1)} %copy-done.3), calls=%async_computation.2 | async-start | bytes 589824 | tf_op jit(solution)/shard_map/all_to_all | solution.py:547
  80.5 7.9 %all-to-all-done.2 = bf16[8,48,384]{2,1,0:T(8,128)(2,1)S(1)} async-done(((bf16[8,48,384]{2,1,0:T(8,128)(2,1)}), bf16[8,48,384]{2,1,0:T(8,128)(2,1)S(1)}, u32[]{:S(2)}, u32[]{:S(2)}) %all-to-all-start.2) | async-done | bytes 294944 | tf_op jit(solution)/shard_map/all_to_all | solution.py:547
  88.4 1.5 %inverse_fourier.1 = bf16[16,3,32,128]{3,2,1,0:T(8,128)(2,1)} custom-call(bf16[384,384]{1,0:T(8,128)(2,1)S(1)} %bitcast.25, bf16[384,4096]{1,0:T(8,128)(2,1)S(1)} %convolution_convert_fusion.f_ref.g_ref, bf16[384,4096]{1,0:T(8,128)(2,1)S(1)} %convolution_convert_fusion.f_ref.g_ref), custom_call_target="tpu_custom_call" | custom-call | flops 400000000 | bytes 3000000 | tf_op jit(solution)/shard_map/inverse_fourier/pallas_call | solution.py:383
  89.8 3.7 %all-to-all-start.3 = ((bf16[16,3,32,128]{3,2,1,0:T(8,128)(2,1)}), bf16[16,3,32,128]{3,2,1,0:T(8,128)(2,1)S(1)}, u32[]{:S(2)}, u32[]{:S(2)}) async-start(bf16[16,3,32,128]{3,2,1,0:T(8,128)(2,1)} %inverse_fourier.1), calls=%async_computation.3 | async-start | bytes 786432 | tf_op jit(solution)/shard_map/all_to_all | solution.py:549
  93.6 0.8 pad_add_fusion
  94.8 0.9 copy-done.11
  95.6 2.7 %build_weights.3 = (bf16[1536,208]{1,0:T(8,128)(2,1)S(1)}, bf16[144,1536]{1,0:T(8,128)(2,1)S(1)}, f32[144,128]{1,0:T(8,128)S(1)}) custom-call(f32[64,32]{1,0:T(8,128)S(1)} %maximum_maximum_fusion.1.w1_ref, s32[1,208]{1,0:T(1,128)S(1)} %bitcast.28, s32[1,208]{1,0:T(1,128)S(1)} %bitcast.27, f32[32,64]{1,0:T(8,128)S(1)} %pad_convert_fusion.w2_ref, ...), custom_call_target="tpu_custom_call" | custom-call | flops 200000000 | bytes 2000000 | tf_op jit(solution)/shard_map/build_weights/pallas_call | solution.py:130
  98.3 4.7 %all-to-all-done.3 = bf16[16,3,32,128]{3,2,1,0:T(8,128)(2,1)S(1)} async-done(((bf16[16,3,32,128]{3,2,1,0:T(8,128)(2,1)}), bf16[16,3,32,128]{3,2,1,0:T(8,128)(2,1)S(1)}, u32[]{:S(2)}, u32[]{:S(2)}) %all-to-all-start.3) | async-done | bytes 393248 | tf_op jit(solution)/shard_map/all_to_all | solution.py:549
  103.0 1.3 %copy-done.7 = bf16[1,6,24,4096]{3,2,1,0:T(8,128)(2,1)S(1)} copy-done((bf16[1,6,24,4096]{3,2,1,0:T(8,128)(2,1)S(1)}, bf16[1,6,24,4096]{3,2,1,0:T(8,128)(2,1)}, u32[]{:S(2)}) %copy-start.7) | copy-done | bytes 1179672
  104.3 11.1 %second_conv.1 = f32[144,4096]{1,0:T(8,128)} custom-call(bf16[144,4096]{1,0:T(8,128)(2,1)S(1)} %bitcast.30, bf16[48,32,128]{2,1,0:T(8,128)(2,1)S(1)} %bitcast.26, bf16[1536,208]{1,0:T(8,128)(2,1)S(1)} %get-tuple-element.15.w1_ref, bf16[144,1536]{1,0:T(8,128)(2,1)S(1)} %get-tuple-element.16.w2_ref, f32[144,128]{1,0:T(8,128)S(1)} %get-tuple-element.17.b2_ref), custom_call_target="tpu_custom_call" | custom-call | flops 4000000000 | bytes 4000000 | tf_op jit(solution)/shard_map/second_conv/pallas_call | solution.py:222
  (69 shorter events, 9.3 us)
Async XLA Ops:
  6.3 0.7 copy-start.12
  7.0 0.7 copy-start.13
  10.1 1.3 %copy-start.6 = (bf16[1,6,24,4096]{3,2,1,0:T(8,128)(2,1)S(1)}, bf16[1,6,24,4096]{3,2,1,0:T(8,128)(2,1)}, u32[]{:S(2)}) copy-start(bf16[1,6,24,4096]{3,2,1,0:T(8,128)(2,1)} %param.23) | copy-start | bytes 3538948
  11.4 17.7 %copy-start.17 = (s32[344]{0:T(512)S(1)}, s32[344]{0:T(512)}, u32[]{:S(2)}) copy-start(s32[344]{0:T(512)} %param.34) | copy-start | bytes 4132
  21.9 16.9 %all-to-all-start = ((bf16[16,3,32,128]{3,2,1,0:T(8,128)(2,1)}), bf16[16,3,32,128]{3,2,1,0:T(8,128)(2,1)S(1)}, u32[]{:S(2)}, u32[]{:S(2)}) async-start(bf16[16,3,32,128]{3,2,1,0:T(8,128)(2,1)} %bitcast.5), calls=%async_computation | async-start | bytes 786432 | tf_op jit(solution)/shard_map/all_to_all | solution.py:533
  34.1 13.1 %copy-start.4 = (f32[8,256]{1,0:T(8,128)S(1)}, f32[8,256]{1,0:T(8,128)}, u32[]{:S(2)}) copy-start(f32[8,256]{1,0:T(8,128)} %constant.47.clone.lat_ref) | copy-start | bytes 24580
  34.1 13.1 %copy-start.5 = (f32[1,384]{1,0:T(1,128)S(1)}, f32[1,384]{1,0:T(1,128)}, u32[]{:S(2)}) copy-start(f32[1,384]{1,0:T(1,128)} %constant.48.clone.start_ref) | copy-start | bytes 4612
  39.6 0.7 copy-start.2
  40.3 21.3 %all-to-all-start.1 = ((bf16[8,48,384]{2,1,0:T(8,128)(2,1)}), bf16[8,48,384]{2,1,0:T(8,128)(2,1)S(1)}, u32[]{:S(2)}, u32[]{:S(2)}) async-start(bf16[8,48,384]{2,1,0:T(8,128)(2,1)} %copy-done.2), calls=%async_computation.1 | async-start | bytes 589824 | tf_op jit(solution)/shard_map/all_to_all | solution.py:545
  58.2 3.4 %copy-start = (bf16[48,352,256]{2,1,0:T(8,128)(2,1)}, bf16[48,352,256]{2,1,0:T(8,128)(2,1)S(1)}, u32[]{:S(2)}) copy-start(bf16[48,352,256]{2,1,0:T(8,128)(2,1)S(1)} %legendre_table.1.t_ref) | copy-start | bytes 25952260
  61.6 3.5 %copy-start.1 = (bf16[48,352,256]{2,1,0:T(8,128)(2,1)S(1)}, bf16[48,352,256]{2,1,0:T(8,128)(2,1)}, u32[]{:S(2)}) copy-start(bf16[48,352,256]{2,1,0:T(8,128)(2,1)} %copy-done) | copy-start | bytes 25952260
  65.1 15.4 %copy-start.16 = (bf16[64,3,8]{0,2,1:T(8,128)(2,1)S(1)}, bf16[64,3,8]{0,2,1:T(8,128)(2,1)}, u32[]{:S(2)}) copy-start(bf16[64,3,8]{0,2,1:T(8,128)(2,1)} %param.29) | copy-start | bytes 9220
  74.9 0.7 copy-start.3
  75.6 12.7 %all-to-all-start.2 = ((bf16[8,48,384]{2,1,0:T(8,128)(2,1)}), bf16[8,48,384]{2,1,0:T(8,128)(2,1)S(1)}, u32[]{:S(2)}, u32[]{:S(2)}) async-start(bf16[8,48,384]{2,1,0:T(8,128)(2,1)} %copy-done.3), calls=%async_computation.2 | async-start | bytes 589824 | tf_op jit(solution)/shard_map/all_to_all | solution.py:547
  88.3 5.2 %copy-start.18 = (s32[144]{0:T(256)S(1)}, s32[144]{0:T(256)}, u32[]{:S(2)}) copy-start(s32[144]{0:T(256)} %constant.50.clone) | copy-start | bytes 1732
  88.3 5.2 %copy-start.19 = (s32[144]{0:T(256)S(1)}, s32[144]{0:T(256)}, u32[]{:S(2)}) copy-start(s32[144]{0:T(256)} %constant.52.clone) | copy-start | bytes 1732
  88.3 5.3 %copy-start.21 = (s32[48]{0:T(128)S(1)}, s32[48]{0:T(128)}, u32[]{:S(2)}) copy-start(s32[48]{0:T(128)} %get-tuple-element.24) | copy-start | bytes 580
  88.3 6.1 %copy-start.20 = (f32[64]{0:T(128)S(1)}, f32[64]{0:T(128)}, u32[]{:S(2)}) copy-start(f32[64]{0:T(128)} %param.30) | copy-start | bytes 772
  88.3 6.3 %copy-start.15 = (bf16[6,3,64]{2,1,0:T(4,128)(2,1)S(1)}, bf16[6,3,64]{2,1,0:T(4,128)(2,1)}, u32[]{:S(2)}) copy-start(bf16[6,3,64]{2,1,0:T(4,128)(2,1)} %param.31) | copy-start | bytes 6916
  88.4 6.4 %copy-start.9 = (f32[6]{0:T(128)S(1)}, f32[6]{0:T(128)}, u32[]{:S(2)}) copy-start(f32[6]{0:T(128)} %b2_ref.3) | copy-start | bytes 76
  88.4 6.4 %copy-start.10 = (s32[144,1]{1,0:T(8,128)S(1)}, s32[144,1]{1,0:T(8,128)}, u32[]{:S(2)}) copy-start(s32[144,1]{1,0:T(8,128)} %constant.62.frow_ref) | copy-start | bytes 1732
  89.8 13.2 %all-to-all-start.3 = ((bf16[16,3,32,128]{3,2,1,0:T(8,128)(2,1)}), bf16[16,3,32,128]{3,2,1,0:T(8,128)(2,1)S(1)}, u32[]{:S(2)}, u32[]{:S(2)}) async-start(bf16[16,3,32,128]{3,2,1,0:T(8,128)(2,1)} %inverse_fourier.1), calls=%async_computation.3 | async-start | bytes 786432 | tf_op jit(solution)/shard_map/all_to_all | solution.py:549
  94.7 0.9 copy-start.11
  103.0 1.3 %copy-start.7 = (bf16[1,6,24,4096]{3,2,1,0:T(8,128)(2,1)S(1)}, bf16[1,6,24,4096]{3,2,1,0:T(8,128)(2,1)}, u32[]{:S(2)}) copy-start(bf16[1,6,24,4096]{3,2,1,0:T(8,128)(2,1)} %param.23) | copy-start | bytes 3538948
  (2 other events, 1.3 us)

commit v2 on v1

--- a/solution.py
+++ b/solution.py
@@ -20,6 +20,7 @@
 GROUP = ITEMS // N_LON
 OWNED = M // N_LAT
 MP = 48
+MH = MP // 2
 KP = 352
 HALF = NLAT // 2
 HID = CH * LV
@@ -41,6 +42,10 @@
 
 def over_levels(index):
     return jnp.floor((index.astype(F32) + 0.5) * (1.0 / LV)).astype(jnp.int32)
+
+
+def hbm(x):
+    return pltpu.with_memory_space_constraint(x, pltpu.HBM)
 
 
 def dot(a, b):
@@ -76,70 +81,86 @@
     return trig, quad, lat_rows, start
 
 
-def weights_kernel(taps, w1_ref, vcol_ref, lcol_ref, w2_ref, frow_ref, lrow_ref, b2_ref, o1_ref, o2_ref, ob_ref):
-    width = vcol_ref.shape[1]
-    rows = frow_ref.shape[0]
-    variables = taps // 3
-    weights = w1_ref[...]
+def to_column(row):
+    n = row.shape[1]
+    return jnp.sum(jnp.where(iota((n, n), 0) == iota((n, n), 1), row, jnp.zeros_like(row)), axis=1, keepdims=True)
+
+
+def make_weights(w1_ref, bias1_ref, w2_ref, order_ref, bias2_ref, slots_in, o1_ref, o2_ref, ob_ref):
+    width, rows = o1_ref.shape[1], o2_ref.shape[0]
+    variables, fields = w1_ref.shape[1], w2_ref.shape[1]
+    order = order_ref[...]
+    base = VARS * LV
+    column = iota((1, width), 1)
+    var_col = over_levels(column)
+    level_col = column - LV * var_col
+    if slots_in:
+        wide_order = jnp.concatenate([jnp.zeros((1, base), jnp.int32), order, jnp.zeros((1, width - base - ITEMS), jnp.int32)], axis=1)
+        slot_field = (wide_order >= LV).astype(jnp.int32)
+        var_col = jnp.where(column < base, var_col + FIELDS, slot_field)
+        level_col = jnp.where(column < base, level_col, wide_order - LV * slot_field)
+    level_col = jnp.where(column < width - 16, level_col, -100)
     r = iota((HID, CH), 0)
     spread = (over_levels(r) == iota((HID, CH), 1)).astype(F32).astype(BF)
     level_row = iota((HID, width), 0)
     level_row = level_row - LV * over_levels(level_row)
-    level_col = lcol_ref[...]
-    var_col = vcol_ref[...]
-    pick = iota((weights.shape[1], width), 0)
     total = jnp.zeros((HID, width), F32)
+    pick = (iota((variables, width), 0) == var_col).astype(F32).astype(BF)
     for tap in range(3):
-        chosen = (pick == tap * variables + var_col).astype(F32).astype(BF)
-        block = (0.5 * dot(weights.astype(BF), chosen)).astype(BF)
-        wide = dot(spread, block)
+        tall = lax.dot_general(spread, w1_ref[tap], NT, preferred_element_type=F32)
+        wide = dot((0.5 * tall).astype(BF), pick)
         total = jnp.where(level_col == level_row + 2 * (tap - 1), wide, total)
-    bias = 0.5 * weights[:, taps : taps + 1]
+    bias = 0.5 * to_column(bias1_ref[...])
     high = bias.astype(BF).astype(F32)
     low = bias - high
-    lane = iota((CH, width), 1)
-    block = jnp.where(lane == width - 16, high, jnp.where(lane == width - 15, low, 0.0)).astype(BF)
+    block = jnp.where(column == width - 16, high, jnp.where(column == width - 15, low, 0.0)).astype(BF)
     o1_ref[...] = (total + dot(spread, block)).astype(BF)
-    second = w2_ref[...]
+    if slots_in:
+        row = iota((rows, 1), 0)
+        field_row = over_levels(row)
+    else:
+        row = to_column(order.astype(F32)).astype(jnp.int32)
+        field_row = (row >= LV).astype(jnp.int32)
+    level_out = row - LV * field_row
     c = iota((CH, HID), 1)
     spread2 = (over_levels(c) == iota((CH, HID), 0)).astype(F32).astype(BF)
     level_hid = iota((rows, HID), 1)
     level_hid = level_hid - LV * over_levels(level_hid)
-    frow, lrow = frow_ref[...], lrow_ref[...]
-    lane2 = iota((rows, second.shape[0]), 1)
     total2 = jnp.zeros((rows, HID), F32)
+    bias2 = jnp.zeros((rows, 128), F32)
     for tap in range(3):
-        chosen = (lane2 == 3 * frow + tap).astype(F32).astype(BF)
-        block = dot(chosen, second.astype(BF)).astype(BF)
-        wide = dot(block, spread2)
-        total2 = jnp.where(level_hid == lrow + 2 * (tap - 1), wide, total2)
+        block = jnp.zeros((rows, CH), F32)
+        for field in range(fields):
+            block = jnp.where(field_row == field, w2_ref[tap].astype(F32)[field : field + 1, :], block)
+        wide = dot(block.astype(BF), spread2)
+        total2 = jnp.where(level_hid == level_out + 2 * (tap - 1), wide, total2)
     o2_ref[...] = total2.astype(BF)
-    bias2 = jnp.zeros((rows, 128), F32)
-    for field in range(b2_ref.shape[0]):
-        bias2 = jnp.where(frow == field, b2_ref[field], bias2)
+    for field in range(fields):
+        bias2 = jnp.where(field_row == field, bias2_ref[0:1, field : field + 1], bias2)
     ob_ref[...] = bias2
 
 
-def build_weights(w1, bias1, w2, bias2, vcol, lcol, frow, lrow):
-    taps = 3 * w1.shape[2]
-    w1p = jnp.concatenate([w1.reshape(CH, taps).astype(F32), bias1[:, None], jnp.zeros((CH, 31 - taps), F32)], axis=1)
-    fields = w2.shape[0]
-    w2p = jnp.pad(w2.reshape(3 * fields, CH).astype(F32), ((0, 32 - 3 * fields), (0, 0)))
-    width, rows = vcol.shape[1], frow.shape[0]
-    vmem = pl.BlockSpec(memory_space=pltpu.VMEM)
-    return pl.pallas_call(
-        functools.partial(weights_kernel, taps),
+def weights_kernel(w1_ref, bias1_ref, w2_ref, order_ref, bias2_ref, o1_ref, o2_ref, ob_ref):
+    make_weights(w1_ref, bias1_ref, w2_ref, order_ref, bias2_ref, True, o1_ref, o2_ref, ob_ref)
+
+
+def second_weights(w1, bias1, w2, bias2, order):
+    full = lambda *shape: pl.BlockSpec(shape, lambda i: (0,) * len(shape))
+    width, rows = VARS * LV + ITEMS + 16, VARS * LV
+    return pl.pallas_call(
+        weights_kernel,
         out_shape=(
-            jax.ShapeDtypeStruct((HID, width), BF),
-            jax.ShapeDtypeStruct((rows, HID), BF),
-            jax.ShapeDtypeStruct((rows, 128), F32),
+            pltpu.HBM((HID, width), BF),
+            pltpu.HBM((rows, HID), BF),
+            pltpu.HBM((rows, 128), F32),
         ),
-        in_specs=[vmem] * 6 + [pl.BlockSpec(memory_space=pltpu.SMEM)],
-        out_specs=(vmem, vmem, vmem),
-        compiler_params=pltpu.CompilerParams(vmem_limit_bytes=40 * 2**20),
+        grid=(1,),
+        in_specs=[full(*w1.shape), full(1, CH), full(*w2.shape), full(1, ITEMS), full(1, bias2.shape[0])],
+        out_specs=(full(HID, width), full(rows, HID), full(rows, 128)),
+        compiler_params=pltpu.CompilerParams(vmem_limit_bytes=20 * 2**20),
         cost_estimate=pl.CostEstimate(flops=2 * 10**8, bytes_accessed=2 * 10**6, transcendentals=0),
-        name="build_weights",
-    )(w1p, vcol, lcol, w2p, frow, lrow, bias2)
+        name="second_weights",
+    )(hbm(w1), hbm(bias1.reshape(1, CH)), hbm(w2), hbm(order.reshape(1, ITEMS)), hbm(bias2.reshape(1, -1)))
 
 
 def hidden_layer(w1_ref, w2_ref, v_ref, h_ref):
@@ -153,11 +174,14 @@
     return dot(w2_ref[...], h_ref[...])
 
 
-def first_kernel(block, state_ref, w1_ref, w2_ref, b2_ref, out_ref, v_ref, h_ref, o_ref):
+def first_kernel(
+    block, state_ref, c1_ref, bias1_ref, c2_ref, order_ref, bias2_ref, out_ref, w1_ref, w2_ref, b2_ref, v_ref, h_ref, o_ref
+):
     step = pl.program_id(0)
 
     @pl.when(step == 0)
     def _():
+        make_weights(c1_ref, bias1_ref, c2_ref, order_ref, bias2_ref, False, w1_ref, w2_ref, b2_ref)
         v_ref[VARS * LV :, :] = jnp.ones((16, block), BF)
 
     v_ref[: VARS * LV, :] = state_ref[...]
@@ -172,28 +196,33 @@
             out_ref[item] = o_ref[item * (TILES + 1) : item * (TILES + 1) + TILES, :].astype(BF)
 
 
-def first_conv(state, w1, w2, b2, block=512):
+def first_conv(state, w1, bias1, w2, bias2, order, block=512):
     full = lambda *shape: pl.BlockSpec(shape, lambda i: (0,) * len(shape))
     return pl.pallas_call(
         functools.partial(first_kernel, block),
         grid=(COLUMNS // block,),
-        out_shape=jax.ShapeDtypeStruct((ITEMS, TILES, 128), BF),
+        out_shape=pltpu.HBM((ITEMS, TILES, 128), BF),
         in_specs=[
             pl.BlockSpec((VARS * LV, block), lambda i: (0, i)),
-            full(HID, VARS * LV + 16),
-            full(ITEMS, HID),
-            full(ITEMS, 128),
+            full(*w1.shape),
+            full(1, CH),
+            full(*w2.shape),
+            full(1, ITEMS),
+            full(1, bias2.shape[0]),
         ],
         out_specs=full(ITEMS, TILES, 128),
         scratch_shapes=[
+            pltpu.VMEM((HID, VARS * LV + 16), BF),
+            pltpu.VMEM((ITEMS, HID), BF),
+            pltpu.VMEM((ITEMS, 128), F32),
             pltpu.VMEM((VARS * LV + 16, block), BF),
             pltpu.VMEM((HID, block), BF),
             pltpu.VMEM((ITEMS * (TILES + 1), 128), F32),
         ],
-        compiler_params=pltpu.CompilerParams(vmem_limit_bytes=40 * 2**20),
+        compiler_params=pltpu.CompilerParams(vmem_limit_bytes=24 * 2**20),
         cost_estimate=pl.CostEstimate(flops=3 * 10**9, bytes_accessed=2 * 10**6, transcendentals=HID * COLUMNS),
         name="first_conv",
-    )(state, w1, w2, b2)
+    )(hbm(state), hbm(w1), hbm(bias1.reshape(1, CH)), hbm(w2), hbm(order.reshape(1, ITEMS)), hbm(bias2.reshape(1, -1)))
 
 
 def second_kernel(block, state_ref, filt_ref, w1_ref, w2_ref, b2_ref, out_ref, v_ref, h_ref, f_ref):
@@ -222,7 +251,7 @@
     return pl.pallas_call(
         functools.partial(second_kernel, block),
         grid=(COLUMNS // block,),
-        out_shape=jax.ShapeDtypeStruct((VARS * LV, COLUMNS), F32),
+        out_shape=pltpu.HBM((VARS * LV, COLUMNS), F32),
         in_specs=[
             pl.BlockSpec((VARS * LV, block), lambda i: (0, i)),
             full(ITEMS, TILES, 128),
@@ -236,10 +265,10 @@
             pltpu.VMEM((HID, block), BF),
             pltpu.VMEM((ITEMS * (TILES + 1), 128), F32),
         ],
-        compiler_params=pltpu.CompilerParams(vmem_limit_bytes=40 * 2**20),
+        compiler_params=pltpu.CompilerParams(vmem_limit_bytes=24 * 2**20),
         cost_estimate=pl.CostEstimate(flops=4 * 10**9, bytes_accessed=4 * 10**6, transcendentals=HID * COLUMNS),
         name="second_conv",
-    )(state, filtered, w1, w2, b2)
+    )(hbm(state), filtered, w1, w2, b2)
 
 
 CHUNK = 16
@@ -248,19 +277,19 @@
 
 def table_kernel(wave_ref, lat_ref, start_ref, out_ref, now_ref, old_ref, log_ref, ratio_ref, s_ref):
     step = pl.program_id(0)
-    wave = jnp.broadcast_to(wave_ref[...], (MP, 128))
+    wave = jnp.broadcast_to(wave_ref[...], (MH, 128))
     sine = [lat_ref[0:1, 128 * h : 128 * h + 128] for h in range(2)]
 
     @pl.when(step == 0)
     def _():
-        match = iota((MP, 384), 1).astype(F32) == wave_ref[...]
+        match = iota((MH, 384), 1).astype(F32) == wave_ref[...]
         start = jnp.sum(jnp.where(match, start_ref[...], 0.0), axis=1, keepdims=True)
         for h in range(2):
             log_cos = lat_ref[1:2, 128 * h : 128 * h + 128]
             log_ref[h] = jnp.where(wave > 500.0, -1e4, start + wave * log_cos)
-            now_ref[h] = jnp.zeros((MP, 128), F32)
-            old_ref[h] = jnp.zeros((MP, 128), F32)
-        ratio_ref[...] = jnp.zeros((MP, 128), F32)
+            now_ref[h] = jnp.zeros((MH, 128), F32)
+            old_ref[h] = jnp.zeros((MH, 128), F32)
+        ratio_ref[...] = jnp.zeros((MH, 128), F32)
 
     now = [now_ref[h] for h in range(2)]
     old = [old_ref[h] for h in range(2)]
@@ -288,12 +317,12 @@
             if kk == 0:
                 stepped = jnp.where(step == 0, 1.0, stepped)
             old[h], now[h] = now[h], stepped
-            s_ref[h, pl.ds(kk, MP, stride=STRIDE), :] = stepped * scale[h]
+            s_ref[h, pl.ds(kk, MH, stride=STRIDE), :] = stepped * scale[h]
         ratio = bottom * root
     for h in range(2):
         now_ref[h], old_ref[h], log_ref[h] = now[h], old[h], log_scale[h]
     ratio_ref[...] = ratio
-    for m in range(MP):
+    for m in range(MH):
         for h in range(2):
             out_ref[m, :, 128 * h : 128 * h + 128] = s_ref[h, m * STRIDE : m * STRIDE + CHUNK, :].astype(BF)
 
@@ -303,12 +332,12 @@
     return pl.pallas_call(
         table_kernel,
         grid=(KP // CHUNK,),
-        out_shape=jax.ShapeDtypeStruct((MP, KP, HALF), BF),
-        in_specs=[full(MP, 1), full(8, HALF), full(1, 384)],
-        out_specs=pl.BlockSpec((MP, CHUNK, HALF), lambda i: (0, i, 0)),
-        scratch_shapes=[pltpu.VMEM((2, MP, 128), F32)] * 3
-        + [pltpu.VMEM((MP, 128), F32), pltpu.VMEM((2, MP * STRIDE, 128), F32)],
-        compiler_params=pltpu.CompilerParams(vmem_limit_bytes=32 * 2**20),
+        out_shape=pltpu.HBM((MH, KP, HALF), BF),
+        in_specs=[full(MH, 1), full(8, HALF), full(1, 384)],
+        out_specs=pl.BlockSpec((MH, CHUNK, HALF), lambda i: (0, i, 0)),
+        scratch_shapes=[pltpu.VMEM((2, MH, 128), F32)] * 3
+        + [pltpu.VMEM((MH, 128), F32), pltpu.VMEM((2, MH * STRIDE, 128), F32)],
+        compiler_params=pltpu.CompilerParams(vmem_limit_bytes=20 * 2**20),
         cost_estimate=pl.CostEstimate(flops=2 * 10**8, bytes_accessed=9 * 10**6, transcendentals=0),
         name="legendre_table",
     )(waves_f, lat_rows, start)
@@ -348,7 +377,7 @@
     return pl.pallas_call(
         forward_kernel,
         grid=(1,),
-        out_shape=jax.ShapeDtypeStruct((N_LAT, MP, 384), BF),
+        out_shape=pltpu.HBM((N_LAT, MP, 384), BF),
         in_specs=[
             full(N_LON, GROUP, TILES, 128),
             pl.BlockSpec((N_LAT * MP, NLON), lambda i: (0, 0)),
@@ -357,7 +386,7 @@
         ],
         out_specs=full(N_LAT, MP, 384),
         scratch_shapes=[pltpu.VMEM((256, NLON), BF)] * 2,
-        compiler_params=pltpu.CompilerParams(vmem_limit_bytes=32 * 2**20),
+        compiler_params=pltpu.CompilerParams(vmem_limit_bytes=20 * 2**20),
         cost_estimate=pl.CostEstimate(flops=4 * 10**8, bytes_accessed=3 * 10**6, transcendentals=0),
         name="forward_fourier",
     )(pieces, tables, tables, quad)
@@ -383,14 +412,14 @@
     return pl.pallas_call(
         inverse_kernel,
         grid=(1,),
-        out_shape=jax.ShapeDtypeStruct((N_LON, GROUP, TILES, 128), BF),
+        out_shape=pltpu.HBM((N_LON, GROUP, TILES, 128), BF),
         in_specs=[
             full(N_LAT * MP, 384),
-            pl.BlockSpec((N_LAT * MP, NLON), lambda i: (0, 2)),
-            pl.BlockSpec((N_LAT * MP, NLON), lambda i: (0, 3)),
+            pl.BlockSpec((N_LAT * MP, NLON), lambda i: (0, 0)),
+            pl.BlockSpec((N_LAT * MP, NLON), lambda i: (0, 1)),
         ],
         out_specs=full(N_LON, GROUP, TILES, 128),
-        compiler_params=pltpu.CompilerParams(vmem_limit_bytes=32 * 2**20),
+        compiler_params=pltpu.CompilerParams(vmem_limit_bytes=20 * 2**20),
         cost_estimate=pl.CostEstimate(flops=4 * 10**8, bytes_accessed=3 * 10**6, transcendentals=0),
         name="inverse_fourier",
     )(returned, tables, tables)
@@ -399,7 +428,7 @@
 WAVES = 8
 
 
-def spectral_kernel(wave_ref, x_ref, t_ref, gain_ref, spec_ref, out_ref, c_ref, n_ref, r_ref, m_ref):
+def spectral_kernel(wave_ref, x_ref, t0_ref, t1_ref, gain_ref, spec_ref, out_ref, c_ref, n_ref, r_ref, m_ref):
     step = pl.program_id(0)
     low = iota((MP, 128), 1) < 64
     mirror = (iota((HALF, HALF), 0) + iota((HALF, HALF), 1) == HALF - 1).astype(F32).astype(BF)
@@ -431,22 +460,27 @@
 
     even = iota((8, KP), 1) % 2 == 0
     gain = gain_ref[...]
-    for mm in range(WAVES):
-        m = step * WAVES + mm
-        left = jnp.concatenate([c_ref[h, pl.ds(m, 16, stride=SLAB), :] for h in range(2)], axis=1).astype(BF)
-        table = t_ref[mm]
-        both = lax.dot_general(left, table, NT, preferred_element_type=F32)
-        natural = jnp.where(even, both[:8], both[8:])
-        n_ref[0, pl.ds(m, 8, stride=SLAB), :] = natural[:, :128]
-        n_ref[1, pl.ds(m, 8, stride=SLAB), :] = natural[:, 128:256]
-        n_ref[2, pl.ds(m, 8, stride=SLAB), :] = jnp.concatenate([natural[:, 256:], jnp.zeros((8, 384 - KP), F32)], axis=1)
-        scaled = natural * pltpu.roll(gain, 768 - wave_ref[m], 1)[:, :KP]
-        right = jnp.concatenate([jnp.where(even, scaled, 0.0), jnp.where(even, 0.0, scaled)], axis=0).astype(BF)
-        back = dot(right, table)
-        north, south = back[:8] + back[8:], back[:8] - back[8:]
-        for h in range(2):
-            r_ref[h, pl.ds(m, 8, stride=SLAB), :] = north[:, 128 * h : 128 * h + 128]
-            r_ref[2 + h, pl.ds(m, 8, stride=SLAB), :] = south[:, 128 * h : 128 * h + 128]
+
+    def waves(t_ref):
+        for mm in range(WAVES):
+            m = step * WAVES + mm
+            left = jnp.concatenate([c_ref[h, pl.ds(m, 16, stride=SLAB), :] for h in range(2)], axis=1).astype(BF)
+            table = t_ref[mm]
+            both = lax.dot_general(left, table, NT, preferred_element_type=F32)
+            natural = jnp.where(even, both[:8], both[8:])
+            n_ref[0, pl.ds(m, 8, stride=SLAB), :] = natural[:, :128]
+            n_ref[1, pl.ds(m, 8, stride=SLAB), :] = natural[:, 128:256]
+            n_ref[2, pl.ds(m, 8, stride=SLAB), :] = jnp.concatenate([natural[:, 256:], jnp.zeros((8, 384 - KP), F32)], axis=1)
+            scaled = natural * pltpu.roll(gain, 768 - wave_ref[m], 1)[:, :KP]
+            right = jnp.concatenate([jnp.where(even, scaled, 0.0), jnp.where(even, 0.0, scaled)], axis=0).astype(BF)
+            back = dot(right, table)
+            north, south = back[:8] + back[8:], back[:8] - back[8:]
+            for h in range(2):
+                r_ref[h, pl.ds(m, 8, stride=SLAB), :] = north[:, 128 * h : 128 * h + 128]
+                r_ref[2 + h, pl.ds(m, 8, stride=SLAB), :] = south[:, 128 * h : 128 * h + 128]
+
+    pl.when(step < MH // WAVES)(lambda: waves(t0_ref))
+    pl.when(step >= MH // WAVES)(lambda: waves(t1_ref))
 
     @pl.when(step == pl.num_programs(0) - 1)
     def _():
@@ -478,7 +512,7 @@
             spec_ref[item] = value[:OWNED, : 2 * M]
 
 
-def spectral_step(waves, coeffs, table, gain):
+def spectral_step(waves, coeffs, table0, table1, gain):
     full = lambda *shape: pl.BlockSpec(shape, lambda i, w: (0,) * len(shape))
     return pl.pallas_call(
         spectral_kernel,
@@ -487,7 +521,8 @@
             grid=(MP // WAVES,),
             in_specs=[
                 full(N_LAT, MP, 384),
-                pl.BlockSpec((WAVES, KP, HALF), lambda i, w: (i, 0, 0)),
+                pl.BlockSpec((WAVES, KP, HALF), lambda i, w: (jnp.minimum(i, MH // WAVES - 1), 0, 0)),
+                pl.BlockSpec((WAVES, KP, HALF), lambda i, w: (jnp.maximum(i - MH // WAVES, 0), 0, 0)),
                 full(8, 768),
             ],
             out_specs=(full(GROUP, OWNED, 2 * M), full(N_LAT, MP, 384)),
@@ -499,13 +534,13 @@
             ],
         ),
         out_shape=(
-            jax.ShapeDtypeStruct((GROUP, OWNED, 2 * M), F32),
-            jax.ShapeDtypeStruct((N_LAT, MP, 384), BF),
+            pltpu.HBM((GROUP, OWNED, 2 * M), F32),
+            pltpu.HBM((N_LAT, MP, 384), BF),
         ),
-        compiler_params=pltpu.CompilerParams(vmem_limit_bytes=40 * 2**20),
+        compiler_params=pltpu.CompilerParams(vmem_limit_bytes=24 * 2**20),
         cost_estimate=pl.CostEstimate(flops=4 * 10**9, bytes_accessed=10**7, transcendentals=0),
         name="spectral_step",
-    )(waves, coeffs, table, gain)
+    )(waves, coeffs, hbm(table0), hbm(table1), gain)
 
 
 def per_device(
@@ -515,49 +550,38 @@
     band = lax.axis_index("lat")
     columns = state.reshape(VARS * LV, COLUMNS)
 
-    slot_field = (level_order >= LV).astype(jnp.int32)
-    slot_level = level_order - LV * slot_field
-    state_rows = np.arange(VARS * LV, dtype=np.int32)
-    none = np.full((16,), -100, np.int32)
-    w1, w2, b2 = build_weights(
-        conv_in,
-        bias_in,
-        conv_out,
-        bias_out,
-        jnp.asarray(np.concatenate([state_rows // LV, none])[None]),
-        jnp.asarray(np.concatenate([state_rows % LV, none])[None]),
-        slot_field[:, None],
-        slot_level[:, None],
-    )
-    tendency = first_conv(columns, w1, w2, b2)
+    tendency = first_conv(columns, conv_in.transpose(1, 2, 0), bias_in, conv_out.transpose(1, 0, 2), bias_out, level_order)
+    tendency, wave_order, spectral_gain = lax.optimization_barrier((tendency, wave_order, spectral_gain))
     pieces = lax.all_to_all(tendency.reshape(N_LON, GROUP, TILES, 128), "lon", 0, 0, tiled=True)
 
     grouped = jnp.pad(wave_order.reshape(N_LAT, OWNED), ((0, 0), (0, MP - OWNED)), constant_values=-1)
     chosen = (grouped.reshape(N_LAT * MP)[:, None] == jnp.arange(M, dtype=jnp.int32)[None, :]).astype(BF)
-    tables = dot(chosen, jnp.asarray(trig)).astype(BF)
+    tables = dot(chosen, jnp.asarray(trig[:, : 2 * NLON])).astype(BF)
     owned = lax.dynamic_slice_in_dim(grouped, band, 1, 0)[0]
     waves_f = jnp.where(owned < 0, 1000, owned).astype(F32)[:, None]
-    table = legendre_table(waves_f, jnp.asarray(lat_rows), jnp.asarray(start))
+    lat_rows, start = jnp.asarray(lat_rows), jnp.asarray(start)
     band_quad = lax.dynamic_slice_in_dim(jnp.asarray(quad), band, 1, 0)[0]
     gain = jnp.broadcast_to(jnp.pad(spectral_gain, (0, 768 - M))[None], (8, 768))
+    owned = jnp.maximum(owned, 0)
+    table0 = legendre_table(waves_f[:MH], lat_rows, start)
+    pieces, table0, tables, gain, owned = lax.optimization_barrier((pieces, table0, tables, gain, owned))
 
     coeffs = forward_fourier(pieces, tables, band_quad)
+    coeffs, waves_late, chosen = lax.optimization_barrier((coeffs, waves_f[MH:], chosen))
     coeffs = lax.all_to_all(coeffs, "lat", 0, 0, tiled=True)
-    spectrum, returned = spectral_step(jnp.maximum(owned, 0), coeffs, table, gain)
+    table1 = legendre_table(waves_late, lat_rows, start)
+    inverse_tables = dot(chosen, jnp.asarray(trig[:, 2 * NLON :])).astype(BF)
+    coeffs, table1, inverse_tables = lax.optimization_barrier((coeffs, table1, inverse_tables))
+
+    spectrum, returned = spectral_step(owned, coeffs, table0, table1, gain)
+    returned, mix_in, blend_bias, mix_out, mix_out_bias, level_order = lax.optimization_barrier(
+        (returned, mix_in, blend_bias, mix_out, mix_out_bias, level_order)
+    )
     returned = lax.all_to_all(returned, "lat", 0, 0, tiled=True)
-    grid_values = inverse_fourier(returned.reshape(N_LAT * MP, 384), tables)
+    m1, m2, mb = second_weights(mix_in.transpose(1, 2, 0), blend_bias, mix_out.transpose(1, 0, 2), mix_out_bias, level_order)
+    returned, m1, m2, mb = lax.optimization_barrier((returned, m1, m2, mb))
+    grid_values = inverse_fourier(returned.reshape(N_LAT * MP, 384), inverse_tables)
     filtered = lax.all_to_all(grid_values, "lon", 0, 0, tiled=True)
-
-    m1, m2, mb = build_weights(
-        mix_in,
-        blend_bias,
-        mix_out,
-        mix_out_bias,
-        jnp.concatenate([jnp.asarray(FIELDS + state_rows // LV), slot_field, jnp.asarray(none)])[None],
-        jnp.concatenate([jnp.asarray(state_rows % LV), slot_level, jnp.asarray(none)])[None],
-        jnp.asarray(state_rows // LV)[:, None],
-        jnp.asarray(state_rows % LV)[:, None],
-    )
     increment = second_conv(columns, filtered.reshape(ITEMS, TILES, 128), m1, m2, mb)
     return spectrum, increment.reshape(1, VARS, LV, COLUMNS)
 

time: 116 us -> 108 us (0.931)
  local copies, waits for them, and re-layouts: 18.6 us -> 1.74 us
  blocking collectives: 0 us -> 16.6 us
  Pallas kernels: 49.8 us -> 65.3 us
  waiting for transfers between devices: 17.4 us -> 3.79 us
  other arithmetic: 4.13 us -> 0.13 us
  starting transfers between devices: 20.9 us -> 17.2 us
  matrix products: 3.64 us -> 2.03 us
    all_to_all x0 -> x1, blocking collectives: none -> 16.6 us  [per_device(): filtered = lax.all_to_all(grid_values, 'lon', 0, 0, tiled=True)]
    unnamed x45 -> x20, local copies, waits for them, and re-layouts: 14.9 us -> 0.05 us
    pallas_call x5, Pallas kernels: 18.3 us -> 28.4 us  [the longest x2 22.1 us: legendre_table(): pl.pallas_call(table_kernel, grid=(KP // CHUNK,), out_shape=pltpu.HBM((MH...]
    all_to_all x1, waiting for transfers between devices: 4.78 us -> 0.01 us  [per_device(): lax.all_to_all(tendency.reshape(N_LON, GROUP, TILES, 128), 'lon', 0, 0, t...]
    all_to_all x1 -> x0, waiting for transfers between devices: 4.72 us -> none  [per_device(): filtered = lax.all_to_all(grid_values, 'lon', 0, 0, tiled=True)]
    all_to_all x1, waiting for transfers between devices: 7.87 us -> 3.79 us  [per_device(): returned = lax.all_to_all(returned, 'lat', 0, 0, tiled=True)]
    all_to_all x1 -> x0, starting transfers between devices: 3.71 us -> none  [per_device(): filtered = lax.all_to_all(grid_values, 'lon', 0, 0, tiled=True)]
    pallas_call x1, Pallas kernels: 10.5 us -> 13.2 us  [first_conv(): pl.pallas_call(functools.partial(first_kernel, block), grid=(COLUMNS // b...]
  transfers between devices with their start and end apart: 4 -> 3, of which waited for: 3 -> 1; matrix products, arithmetic and copies ran while one was open for 6% -> 4% of each run, Pallas kernels for 12% -> 24%
where the time goes in v2:
time: 108 us
  Pallas kernels  65.3 us (60%)
  starting transfers between devices  17.2 us (16%)
  blocking collectives  16.6 us (15%)
  waiting for transfers between devices  3.79 us (4%)
  matrix products  2.03 us (2%)
  local copies, waits for them, and re-layouts  1.74 us (2%)
    pallas_call x2, Pallas kernels, legendre_table(): pl.pallas_call(table_kernel, grid=(KP // CHUNK,), out_shape=pltpu.HBM((MH...  22.1 us
    all_to_all x1, blocking collectives, per_device(): filtered = lax.all_to_all(grid_values, 'lon', 0, 0, tiled=True)  16.6 us
    pallas_call x1, Pallas kernels, first_conv(): pl.pallas_call(functools.partial(first_kernel, block), grid=(COLUMNS // b...  13.2 us
    pallas_call x1, Pallas kernels, second_conv(): pl.pallas_call(functools.partial(second_kernel, block), grid=(COLUMNS //...  11.9 us
    pallas_call x1, Pallas kernels, spectral_step(): pl.pallas_call(spectral_kernel, grid_spec=pltpu.PrefetchScalarGridSpec(nu...  11.9 us
    all_to_all x1, starting transfers between devices, per_device(): lax.all_to_all(tendency.reshape(N_LON, GROUP, TILES, 128), 'lon', 0, 0, t...  7.12 us
    all_to_all x1, starting transfers between devices, per_device(): coeffs = lax.all_to_all(coeffs, 'lat', 0, 0, tiled=True)  5.32 us
    all_to_all x1, starting transfers between devices, per_device(): returned = lax.all_to_all(returned, 'lat', 0, 0, tiled=True)  4.81 us
  transfers between devices with their start and end apart: 3, of which 1 were waited for; matrix products, arithmetic and copies ran while one was open for 4% of the time, Pallas kernels for 24%

profile of v2, /device:TPU:0, one launch (start us, length us, event | category | flops | bytes accessed | tf_op | source)
XLA Modules:
  0.0 107.7 jit_solution(11540449317734511933)
XLA Ops:
  0.7 0.0 copy-start
  0.7 13.2 %first_conv.1 = bf16[48,32,128]{2,1,0:T(8,128)(2,1)} custom-call(bf16[144,4096]{1,0:T(8,128)(2,1)} %bitcast.33, bf16[3,6,64]{2,1,0:T(8,128)(2,1)} %bitcast.35, f32[1,64]{1,0:T(1,128)} %bitcast.38, bf16[3,2,64]{2,1,0:T(2,128)(2,1)} %bitcast.37, s32[1,48]{1,0:T(1,128)} %bitcast.40, f32[1,2]{1,0:T(1,128)} %bitcast.39), custom_call_target="tpu_custom_call" | custom-call | flops 3000000000 | bytes 2000000 | tf_op jit(solution)/shard_map/first_conv/pallas_call | solution.py:201
  13.9 7.1 %all-to-all-start = ((bf16[16,3,32,128]{3,2,1,0:T(8,128)(2,1)}), bf16[16,3,32,128]{3,2,1,0:T(8,128)(2,1)S(1)}, u32[]{:S(2)}, u32[]{:S(2)}) async-start(bf16[16,3,32,128]{3,2,1,0:T(8,128)(2,1)} %bitcast.31), calls=%async_computation | async-start | bytes 786432 | tf_op jit(solution)/shard_map/all_to_all | solution.py:555
  21.0 0.1 reshape.49
  21.1 0.1 eq.15
  21.2 0.1 slice_bitcast_fusion
  21.2 0.1 copy.19.wave_ref
  21.3 0.1 fusion
  21.5 11.0 %legendre_table.2.t0_ref = bf16[24,352,256]{2,1,0:T(8,128)(2,1)} custom-call(f32[24,1]{1,0:T(8,128)S(1)} %copy.19.wave_ref, f32[8,256]{1,0:T(8,128)S(1)} %copy-done, f32[1,384]{1,0:T(1,128)S(1)} %copy-done.1), custom_call_target="tpu_custom_call" | custom-call | flops 200000000 | bytes 9000000 | tf_op jit(solution)/shard_map/legendre_table/pallas_call | solution.py:332
  32.6 0.7 dynamic-slice_bitcast_fusion.q_ref
  33.2 1.0 convolution_convert_fusion.f_ref.g_ref
  34.3 1.4 %forward_fourier.1 = bf16[8,48,384]{2,1,0:T(8,128)(2,1)} custom-call(bf16[16,3,32,128]{3,2,1,0:T(8,128)(2,1)S(1)} %all-to-all-done.y_ref, bf16[384,2048]{1,0:T(8,128)(2,1)S(1)} %convolution_convert_fusion.f_ref.g_ref, bf16[384,2048]{1,0:T(8,128)(2,1)S(1)} %convolution_convert_fusion.f_ref.g_ref, f32[1,384]{1,0:T(1,128)S(1)} %dynamic-slice_bitcast_fusion.q_ref), custom_call_target="tpu_custom_call" | custom-call | flops 400000000 | bytes 3000000 | tf_op jit(solution)/shard_map/forward_fourier/pallas_call | solution.py:377
  35.7 5.3 %all-to-all-start.1 = ((bf16[8,48,384]{2,1,0:T(8,128)(2,1)}), bf16[8,48,384]{2,1,0:T(8,128)(2,1)S(1)}, u32[]{:S(2)}, u32[]{:S(2)}) async-start(bf16[8,48,384]{2,1,0:T(8,128)(2,1)} %forward_fourier.1), calls=%async_computation.1 | async-start | bytes 589824 | tf_op jit(solution)/shard_map/all_to_all | solution.py:571
  41.0 0.1 copy.20.wave_ref
  41.1 11.0 %legendre_table.3.t1_ref = bf16[24,352,256]{2,1,0:T(8,128)(2,1)} custom-call(f32[24,1]{1,0:T(8,128)S(1)} %copy.20.wave_ref, f32[8,256]{1,0:T(8,128)S(1)} %copy-done, f32[1,384]{1,0:T(1,128)S(1)} %copy-done.1), custom_call_target="tpu_custom_call" | custom-call | flops 200000000 | bytes 9000000 | tf_op jit(solution)/shard_map/legendre_table/pallas_call | solution.py:332
  52.2 1.0 convolution_convert_fusion.1.f_ref.g_ref
  53.2 11.9 %spectral_step.1 = (f32[3,43,688]{2,1,0:T(8,128)}, bf16[8,48,384]{2,1,0:T(8,128)(2,1)}) custom-call(s32[48]{0:T(128)S(1)} %get-tuple-element.34.wave_ref, bf16[8,48,384]{2,1,0:T(8,128)(2,1)S(1)} %all-to-all-done.1.x_ref, bf16[24,352,256]{2,1,0:T(8,128)(2,1)} %legendre_table.2.t0_ref, bf16[24,352,256]{2,1,0:T(8,128)(2,1)} %legendre_table.3.t1_ref, ...), custom_call_target="tpu_custom_call" | custom-call | flops 4000000000 | bytes 10000000 | tf_op jit(solution)/shard_map/spectral_step/pallas_call | solution.py:517
  65.0 4.8 %all-to-all-start.2 = ((bf16[8,48,384]{2,1,0:T(8,128)(2,1)}), bf16[8,48,384]{2,1,0:T(8,128)(2,1)S(1)}, u32[]{:S(2)}, u32[]{:S(2)}) async-start(bf16[8,48,384]{2,1,0:T(8,128)(2,1)} %get-tuple-element.46), calls=%async_computation.2 | async-start | bytes 589824 | tf_op jit(solution)/shard_map/all_to_all | solution.py:580
  69.8 0.6 copy.23
  70.5 3.5 %second_weights.1 = (bf16[1536,208]{1,0:T(8,128)(2,1)}, bf16[144,1536]{1,0:T(8,128)(2,1)}, f32[144,128]{1,0:T(8,128)}) custom-call(bf16[3,8,64]{2,1,0:T(8,128)(2,1)} %bitcast.36, f32[1,64]{1,0:T(1,128)} %bitcast.42, bf16[3,6,64]{2,1,0:T(8,128)(2,1)} %bitcast.32, s32[1,48]{1,0:T(1,128)} %bitcast.41, f32[1,6]{1,0:T(1,128)} %bitcast.43), custom_call_target="tpu_custom_call" | custom-call | flops 200000000 | bytes 2000000 | tf_op jit(solution)/shard_map/second_weights/pallas_call | solution.py:150
  73.9 3.8 %all-to-all-done.2 = bf16[8,48,384]{2,1,0:T(8,128)(2,1)S(1)} async-done(((bf16[8,48,384]{2,1,0:T(8,128)(2,1)}), bf16[8,48,384]{2,1,0:T(8,128)(2,1)S(1)}, u32[]{:S(2)}, u32[]{:S(2)}) %all-to-all-start.2) | async-done | bytes 294944 | tf_op jit(solution)/shard_map/all_to_all | solution.py:580
  77.7 1.4 %inverse_fourier.1 = bf16[16,3,32,128]{3,2,1,0:T(8,128)(2,1)} custom-call(bf16[384,384]{1,0:T(8,128)(2,1)S(1)} %bitcast.29, bf16[384,2048]{1,0:T(8,128)(2,1)S(1)} %convolution_convert_fusion.1.f_ref.g_ref, bf16[384,2048]{1,0:T(8,128)(2,1)S(1)} %convolution_convert_fusion.1.f_ref.g_ref), custom_call_target="tpu_custom_call" | custom-call | flops 400000000 | bytes 3000000 | tf_op jit(solution)/shard_map/inverse_fourier/pallas_call | solution.py:412
  79.2 16.6 %all_to_all.20 = bf16[16,3,32,128]{3,2,1,0:T(8,128)(2,1)S(1)} all-to-all(bf16[16,3,32,128]{3,2,1,0:T(8,128)(2,1)} %inverse_fourier.1), channel_id=1, replica_groups=mesh['lat'=8,'lon'=16] {'lon'}, dimensions={0} | all-to-all | bytes 786432 | tf_op jit(solution)/shard_map/all_to_all | solution.py:584
  95.8 11.9 %second_conv.1 = f32[144,4096]{1,0:T(8,128)} custom-call(bf16[144,4096]{1,0:T(8,128)(2,1)} %bitcast.34, bf16[48,32,128]{2,1,0:T(8,128)(2,1)S(1)} %bitcast.30, bf16[1536,208]{1,0:T(8,128)(2,1)S(1)} %copy-done.2, bf16[144,1536]{1,0:T(8,128)(2,1)S(1)} %copy-done.3, f32[144,128]{1,0:T(8,128)S(1)} %copy-done.4), custom_call_target="tpu_custom_call" | custom-call | flops 4000000000 | bytes 4000000 | tf_op jit(solution)/shard_map/second_conv/pallas_call | solution.py:251
  (25 shorter events, 0.1 us)
Async XLA Ops:
  0.6 20.4 %copy-start.8 = (s32[344]{0:T(512)S(1)}, s32[344]{0:T(512)}, u32[]{:S(2)}) copy-start(s32[344]{0:T(512)} %param.28) | copy-start | bytes 4132
  0.6 20.8 %copy-start.9 = (f32[344]{0:T(512)S(1)}, f32[344]{0:T(512)}, u32[]{:S(2)}) copy-start(f32[344]{0:T(512)} %param.22) | copy-start | bytes 4132
  0.7 20.8 %copy-start = (f32[8,256]{1,0:T(8,128)S(1)}, f32[8,256]{1,0:T(8,128)}, u32[]{:S(2)}) copy-start(f32[8,256]{1,0:T(8,128)} %constant.28.clone.lat_ref) | copy-start | bytes 24580
  0.7 20.8 %copy-start.1 = (f32[1,384]{1,0:T(1,128)S(1)}, f32[1,384]{1,0:T(1,128)}, u32[]{:S(2)}) copy-start(f32[1,384]{1,0:T(1,128)} %constant.29.clone.start_ref) | copy-start | bytes 4612
  13.9 20.4 %all-to-all-start = ((bf16[16,3,32,128]{3,2,1,0:T(8,128)(2,1)}), bf16[16,3,32,128]{3,2,1,0:T(8,128)(2,1)S(1)}, u32[]{:S(2)}, u32[]{:S(2)}) async-start(bf16[16,3,32,128]{3,2,1,0:T(8,128)(2,1)} %bitcast.31), calls=%async_computation | async-start | bytes 786432 | tf_op jit(solution)/shard_map/all_to_all | solution.py:555
  21.5 11.7 %copy-start.6 = (bf16[344,2048]{1,0:T(8,128)(2,1)S(1)}, bf16[344,2048]{1,0:T(8,128)(2,1)}, u32[]{:S(2)}) copy-start(bf16[344,2048]{1,0:T(8,128)(2,1)} %constant.27.clone) | copy-start | bytes 4227076
  35.7 17.5 %all-to-all-start.1 = ((bf16[8,48,384]{2,1,0:T(8,128)(2,1)}), bf16[8,48,384]{2,1,0:T(8,128)(2,1)S(1)}, u32[]{:S(2)}, u32[]{:S(2)}) async-start(bf16[8,48,384]{2,1,0:T(8,128)(2,1)} %forward_fourier.1), calls=%async_computation.1 | async-start | bytes 589824 | tf_op jit(solution)/shard_map/all_to_all | solution.py:571
  41.1 11.0 %copy-start.5 = (bf16[344,2048]{1,0:T(8,128)(2,1)S(1)}, bf16[344,2048]{1,0:T(8,128)(2,1)}, u32[]{:S(2)}) copy-start(bf16[344,2048]{1,0:T(8,128)(2,1)} %constant.31.clone) | copy-start | bytes 4227076
  53.2 16.7 %copy-start.7 = (bf16[6,3,64]{2,1,0:T(4,128)(2,1)S(1)}, bf16[6,3,64]{2,1,0:T(4,128)(2,1)}, u32[]{:S(2)}) copy-start(bf16[6,3,64]{2,1,0:T(4,128)(2,1)} %param.25) | copy-start | bytes 6916
  65.0 12.7 %all-to-all-start.2 = ((bf16[8,48,384]{2,1,0:T(8,128)(2,1)}), bf16[8,48,384]{2,1,0:T(8,128)(2,1)S(1)}, u32[]{:S(2)}, u32[]{:S(2)}) async-start(bf16[8,48,384]{2,1,0:T(8,128)(2,1)} %get-tuple-element.46), calls=%async_computation.2 | async-start | bytes 589824 | tf_op jit(solution)/shard_map/all_to_all | solution.py:580
  77.7 18.1 %copy-start.2 = (bf16[1536,208]{1,0:T(8,128)(2,1)S(1)}, bf16[1536,208]{1,0:T(8,128)(2,1)}, u32[]{:S(2)}) copy-start(bf16[1536,208]{1,0:T(8,128)(2,1)} %get-tuple-element.57.w1_ref) | copy-start | bytes 1916932
  77.7 18.1 %copy-start.3 = (bf16[144,1536]{1,0:T(8,128)(2,1)S(1)}, bf16[144,1536]{1,0:T(8,128)(2,1)}, u32[]{:S(2)}) copy-start(bf16[144,1536]{1,0:T(8,128)(2,1)} %get-tuple-element.58.w2_ref) | copy-start | bytes 1327108
  77.7 18.1 %copy-start.4 = (f32[144,128]{1,0:T(8,128)S(1)}, f32[144,128]{1,0:T(8,128)}, u32[]{:S(2)}) copy-start(f32[144,128]{1,0:T(8,128)} %get-tuple-element.59.b2_ref) | copy-start | bytes 221188

commit v3 on v2

--- a/solution.py
+++ b/solution.py
@@ -165,13 +165,17 @@
 
 def hidden_layer(w1_ref, w2_ref, v_ref, h_ref):
     block = v_ref.shape[1]
-    step = 256
+    step, tall = 256, HID // 2
+    c1, c2 = 2 * math.sqrt(2 / math.pi), 8 * 0.044715 * math.sqrt(2 / math.pi)
+    results = []
     for col in range(0, block, step):
-        for row in range(0, HID, 256):
-            y = dot(w1_ref[row : row + 256, :], v_ref[:, col : col + step])
-            u = y * (2 * math.sqrt(2 / math.pi) + (8 * 0.044715 * math.sqrt(2 / math.pi)) * (y * y))
-            h_ref[row : row + 256, col : col + step] = (y + y * jnp.tanh(u)).astype(BF)
-    return dot(w2_ref[...], h_ref[...])
+        cols = slice(col, col + step)
+        for row in range(0, HID, tall):
+            y = dot(w1_ref[row : row + tall, :], v_ref[:, cols])
+            u = y * (c1 + c2 * (y * y))
+            h_ref[row : row + tall, cols] = (y + y * jnp.tanh(u)).astype(BF)
+        results.append(dot(w2_ref[...], h_ref[:, cols]))
+    return jnp.concatenate(results, axis=1)
 
 
 def first_kernel(
@@ -196,7 +200,7 @@
             out_ref[item] = o_ref[item * (TILES + 1) : item * (TILES + 1) + TILES, :].astype(BF)
 
 
-def first_conv(state, w1, bias1, w2, bias2, order, block=512):
+def first_conv(state, w1, bias1, w2, bias2, order, block=1024):
     full = lambda *shape: pl.BlockSpec(shape, lambda i: (0,) * len(shape))
     return pl.pallas_call(
         functools.partial(first_kernel, block),
@@ -245,7 +249,7 @@
         out_ref[:, tile * 128 : (tile + 1) * 128] = result[:, tile * 128 : (tile + 1) * 128] + bias
 
 
-def second_conv(state, filtered, w1, w2, b2, block=512):
+def second_conv(state, filtered, w1, w2, b2, block=1024):
     full = lambda *shape: pl.BlockSpec(shape, lambda i: (0,) * len(shape))
     width = VARS * LV + ITEMS + 16
     return pl.pallas_call(
@@ -271,7 +275,7 @@
     )(hbm(state), filtered, w1, w2, b2)
 
 
-CHUNK = 16
+CHUNK = 176
 STRIDE = CHUNK + 1
 
 

time: 108 us -> 94.2 us (0.87)
  Pallas kernels: 65.3 us -> 51.2 us
  waiting for transfers between devices: 3.79 us -> 6.5 us
  blocking collectives: 16.6 us -> 14.9 us
    pallas_call x2, Pallas kernels: 22.1 us -> 11.6 us  [legendre_table(): pl.pallas_call(table_kernel, grid=(KP // CHUNK,), out_shape=pltpu.HBM((MH...]
    pallas_call x1, Pallas kernels: 13.2 us -> 11.2 us  [first_conv(): pl.pallas_call(functools.partial(first_kernel, block), grid=(COLUMNS // b...]
    all_to_all x1, blocking collectives: 16.6 us -> 14.9 us  [per_device(): filtered = lax.all_to_all(grid_values, 'lon', 0, 0, tiled=True)]
    all_to_all x1, waiting for transfers between devices: 0.01 us -> 1.75 us  [per_device(): lax.all_to_all(tendency.reshape(N_LON, GROUP, TILES, 128), 'lon', 0, 0, t...]
    pallas_call x1, Pallas kernels: 11.9 us -> 10.1 us  [second_conv(): pl.pallas_call(functools.partial(second_kernel, block), grid=(COLUMNS //...]
  transfers between devices with their start and end apart: 3 -> 3, of which waited for: 1 -> 3; matrix products, arithmetic and copies ran while one was open for 4% -> 4% of each run, Pallas kernels for 24% -> 16%
where the time goes in v3:
time: 94.2 us; the launch traced here: 93.5 us
  Pallas kernels  51.2 us (54%)
  starting transfers between devices  16.3 us (17%)
  blocking collectives  14.9 us (16%)
  waiting for transfers between devices  6.5 us (7%)
  matrix products  2.03 us (2%)
  local copies, waits for them, and re-layouts  1.74 us (2%)
    all_to_all x1, blocking collectives, per_device(): filtered = lax.all_to_all(grid_values, 'lon', 0, 0, tiled=True)  14.9 us
    pallas_call x1, Pallas kernels, spectral_step(): pl.pallas_call(spectral_kernel, grid_spec=pltpu.PrefetchScalarGridSpec(nu...  11.9 us
    pallas_call x2, Pallas kernels, legendre_table(): pl.pallas_call(table_kernel, grid=(KP // CHUNK,), out_shape=pltpu.HBM((MH...  11.6 us
    pallas_call x1, Pallas kernels, first_conv(): pl.pallas_call(functools.partial(first_kernel, block), grid=(COLUMNS // b...  11.2 us
    pallas_call x1, Pallas kernels, second_conv(): pl.pallas_call(functools.partial(second_kernel, block), grid=(COLUMNS //...  10.1 us
    all_to_all x1, starting transfers between devices, per_device(): lax.all_to_all(tendency.reshape(N_LON, GROUP, TILES, 128), 'lon', 0, 0, t...  7.15 us
    all_to_all x1, starting transfers between devices, per_device(): coeffs = lax.all_to_all(coeffs, 'lat', 0, 0, tiled=True)  5.33 us
    all_to_all x1, starting transfers between devices, per_device(): returned = lax.all_to_all(returned, 'lat', 0, 0, tiled=True)  3.86 us
  transfers between devices with their start and end apart: 3, of which 3 were waited for; matrix products, arithmetic and copies ran while one was open for 4% of the time, Pallas kernels for 16%

profile of v3, /device:TPU:0, one launch (start us, length us, event | category | flops | bytes accessed | tf_op | source)
XLA Modules:
  0.0 93.5 jit_solution(12861677846945650741)
XLA Ops:
  0.7 11.2 %first_conv.1 = bf16[48,32,128]{2,1,0:T(8,128)(2,1)} custom-call(bf16[144,4096]{1,0:T(8,128)(2,1)} %bitcast.33, bf16[3,6,64]{2,1,0:T(8,128)(2,1)} %bitcast.35, f32[1,64]{1,0:T(1,128)} %bitcast.38, bf16[3,2,64]{2,1,0:T(2,128)(2,1)} %bitcast.37, s32[1,48]{1,0:T(1,128)} %bitcast.40, f32[1,2]{1,0:T(1,128)} %bitcast.39), custom_call_target="tpu_custom_call" | custom-call | flops 3000000000 | bytes 2000000 | tf_op jit(solution)/shard_map/first_conv/pallas_call | solution.py:205
  11.9 7.1 %all-to-all-start = ((bf16[16,3,32,128]{3,2,1,0:T(8,128)(2,1)}), bf16[16,3,32,128]{3,2,1,0:T(8,128)(2,1)S(1)}, u32[]{:S(2)}, u32[]{:S(2)}) async-start(bf16[16,3,32,128]{3,2,1,0:T(8,128)(2,1)} %bitcast.31), calls=%async_computation | async-start | bytes 786432 | tf_op jit(solution)/shard_map/all_to_all | solution.py:559
  19.0 0.1 reshape.49
  19.1 0.1 eq.15
  19.3 0.1 copy.19.wave_ref
  19.4 0.1 fusion
  19.6 5.8 %legendre_table.2.t0_ref = bf16[24,352,256]{2,1,0:T(8,128)(2,1)} custom-call(f32[24,1]{1,0:T(8,128)S(1)} %copy.19.wave_ref, f32[8,256]{1,0:T(8,128)S(1)} %copy-done, f32[1,384]{1,0:T(1,128)S(1)} %copy-done.1), custom_call_target="tpu_custom_call" | custom-call | flops 200000000 | bytes 9000000 | tf_op jit(solution)/shard_map/legendre_table/pallas_call | solution.py:336
  25.3 0.7 dynamic-slice_bitcast_fusion.q_ref
  26.0 1.0 %convolution_convert_fusion.f_ref.g_ref = bf16[384,2048]{1,0:T(8,128)(2,1)S(1)} fusion(bf16[344,2048]{1,0:T(8,128)(2,1)S(1)} %copy-done.6, s32[384]{0:T(512)S(1)} %eq.15), kind=kOutput, calls=%fused_computation | convolution fusion | flops 541983744 | bytes 2983424 | tf_op jit(solution)/shard_map/dot_general | solution.py:52
  27.0 1.8 %all-to-all-done.y_ref = bf16[16,3,32,128]{3,2,1,0:T(8,128)(2,1)S(1)} async-done(((bf16[16,3,32,128]{3,2,1,0:T(8,128)(2,1)}), bf16[16,3,32,128]{3,2,1,0:T(8,128)(2,1)S(1)}, u32[]{:S(2)}, u32[]{:S(2)}) %all-to-all-start) | async-done | bytes 393248 | tf_op jit(solution)/shard_map/all_to_all | solution.py:559
  28.8 1.4 %forward_fourier.1 = bf16[8,48,384]{2,1,0:T(8,128)(2,1)} custom-call(bf16[16,3,32,128]{3,2,1,0:T(8,128)(2,1)S(1)} %all-to-all-done.y_ref, bf16[384,2048]{1,0:T(8,128)(2,1)S(1)} %convolution_convert_fusion.f_ref.g_ref, bf16[384,2048]{1,0:T(8,128)(2,1)S(1)} %convolution_convert_fusion.f_ref.g_ref, f32[1,384]{1,0:T(1,128)S(1)} %dynamic-slice_bitcast_fusion.q_ref), custom_call_target="tpu_custom_call" | custom-call | flops 400000000 | bytes 3000000 | tf_op jit(solution)/shard_map/forward_fourier/pallas_call | solution.py:381
  30.2 5.3 %all-to-all-start.1 = ((bf16[8,48,384]{2,1,0:T(8,128)(2,1)}), bf16[8,48,384]{2,1,0:T(8,128)(2,1)S(1)}, u32[]{:S(2)}, u32[]{:S(2)}) async-start(bf16[8,48,384]{2,1,0:T(8,128)(2,1)} %forward_fourier.1), calls=%async_computation.1 | async-start | bytes 589824 | tf_op jit(solution)/shard_map/all_to_all | solution.py:575
  35.6 0.1 copy.20.wave_ref
  35.7 5.8 %legendre_table.3.t1_ref = bf16[24,352,256]{2,1,0:T(8,128)(2,1)} custom-call(f32[24,1]{1,0:T(8,128)S(1)} %copy.20.wave_ref, f32[8,256]{1,0:T(8,128)S(1)} %copy-done, f32[1,384]{1,0:T(1,128)S(1)} %copy-done.1), custom_call_target="tpu_custom_call" | custom-call | flops 200000000 | bytes 9000000 | tf_op jit(solution)/shard_map/legendre_table/pallas_call | solution.py:336
  41.5 1.0 %convolution_convert_fusion.1.f_ref.g_ref = bf16[384,2048]{1,0:T(8,128)(2,1)S(1)} fusion(bf16[384,344]{1,0:T(8,128)(2,1)S(1)} %fusion, bf16[344,2048]{1,0:T(8,128)(2,1)S(1)} %copy-done.5), kind=kOutput, calls=%fused_computation.1 | convolution fusion | flops 541851648 | bytes 3246080 | tf_op jit(solution)/shard_map/dot_general | solution.py:52
  42.5 1.0 %all-to-all-done.1.x_ref = bf16[8,48,384]{2,1,0:T(8,128)(2,1)S(1)} async-done(((bf16[8,48,384]{2,1,0:T(8,128)(2,1)}), bf16[8,48,384]{2,1,0:T(8,128)(2,1)S(1)}, u32[]{:S(2)}, u32[]{:S(2)}) %all-to-all-start.1) | async-done | bytes 294944 | tf_op jit(solution)/shard_map/all_to_all | solution.py:575
  43.5 11.9 %spectral_step.1 = (f32[3,43,688]{2,1,0:T(8,128)}, bf16[8,48,384]{2,1,0:T(8,128)(2,1)}) custom-call(s32[48]{0:T(128)S(1)} %get-tuple-element.34.wave_ref, bf16[8,48,384]{2,1,0:T(8,128)(2,1)S(1)} %all-to-all-done.1.x_ref, bf16[24,352,256]{2,1,0:T(8,128)(2,1)} %legendre_table.2.t0_ref, bf16[24,352,256]{2,1,0:T(8,128)(2,1)} %legendre_table.3.t1_ref, ...), custom_call_target="tpu_custom_call" | custom-call | flops 4000000000 | bytes 10000000 | tf_op jit(solution)/shard_map/spectral_step/pallas_call | solution.py:521
  55.3 3.9 %all-to-all-start.2 = ((bf16[8,48,384]{2,1,0:T(8,128)(2,1)}), bf16[8,48,384]{2,1,0:T(8,128)(2,1)S(1)}, u32[]{:S(2)}, u32[]{:S(2)}) async-start(bf16[8,48,384]{2,1,0:T(8,128)(2,1)} %get-tuple-element.46), calls=%async_computation.2 | async-start | bytes 589824 | tf_op jit(solution)/shard_map/all_to_all | solution.py:584
  59.2 0.6 copy.23
  59.8 3.5 %second_weights.1 = (bf16[1536,208]{1,0:T(8,128)(2,1)}, bf16[144,1536]{1,0:T(8,128)(2,1)}, f32[144,128]{1,0:T(8,128)}) custom-call(bf16[3,8,64]{2,1,0:T(8,128)(2,1)} %bitcast.36, f32[1,64]{1,0:T(1,128)} %bitcast.42, bf16[3,6,64]{2,1,0:T(8,128)(2,1)} %bitcast.32, s32[1,48]{1,0:T(1,128)} %bitcast.41, f32[1,6]{1,0:T(1,128)} %bitcast.43), custom_call_target="tpu_custom_call" | custom-call | flops 200000000 | bytes 2000000 | tf_op jit(solution)/shard_map/second_weights/pallas_call | solution.py:150
  63.3 3.8 %all-to-all-done.2 = bf16[8,48,384]{2,1,0:T(8,128)(2,1)S(1)} async-done(((bf16[8,48,384]{2,1,0:T(8,128)(2,1)}), bf16[8,48,384]{2,1,0:T(8,128)(2,1)S(1)}, u32[]{:S(2)}, u32[]{:S(2)}) %all-to-all-start.2) | async-done | bytes 294944 | tf_op jit(solution)/shard_map/all_to_all | solution.py:584
  67.1 1.4 %inverse_fourier.1 = bf16[16,3,32,128]{3,2,1,0:T(8,128)(2,1)} custom-call(bf16[384,384]{1,0:T(8,128)(2,1)S(1)} %bitcast.29, bf16[384,2048]{1,0:T(8,128)(2,1)S(1)} %convolution_convert_fusion.1.f_ref.g_ref, bf16[384,2048]{1,0:T(8,128)(2,1)S(1)} %convolution_convert_fusion.1.f_ref.g_ref), custom_call_target="tpu_custom_call" | custom-call | flops 400000000 | bytes 3000000 | tf_op jit(solution)/shard_map/inverse_fourier/pallas_call | solution.py:416
  68.5 14.9 %all_to_all.20 = bf16[16,3,32,128]{3,2,1,0:T(8,128)(2,1)S(1)} all-to-all(bf16[16,3,32,128]{3,2,1,0:T(8,128)(2,1)} %inverse_fourier.1), channel_id=1, replica_groups=mesh['lat'=8,'lon'=16] {'lon'}, dimensions={0} | all-to-all | bytes 786432 | tf_op jit(solution)/shard_map/all_to_all | solution.py:588
  83.4 10.1 %second_conv.1 = f32[144,4096]{1,0:T(8,128)} custom-call(bf16[144,4096]{1,0:T(8,128)(2,1)} %bitcast.34, bf16[48,32,128]{2,1,0:T(8,128)(2,1)S(1)} %bitcast.30, bf16[1536,208]{1,0:T(8,128)(2,1)S(1)} %copy-done.2, bf16[144,1536]{1,0:T(8,128)(2,1)S(1)} %copy-done.3, f32[144,128]{1,0:T(8,128)S(1)} %copy-done.4), custom_call_target="tpu_custom_call" | custom-call | flops 4000000000 | bytes 4000000 | tf_op jit(solution)/shard_map/second_conv/pallas_call | solution.py:255
  (25 shorter events, 0.1 us)
Async XLA Ops:
  0.6 18.4 %copy-start.8 = (s32[344]{0:T(512)S(1)}, s32[344]{0:T(512)}, u32[]{:S(2)}) copy-start(s32[344]{0:T(512)} %param.28) | copy-start | bytes 4132
  0.6 18.9 %copy-start.9 = (f32[344]{0:T(512)S(1)}, f32[344]{0:T(512)}, u32[]{:S(2)}) copy-start(f32[344]{0:T(512)} %param.22) | copy-start | bytes 4132
  0.7 18.9 %copy-start = (f32[8,256]{1,0:T(8,128)S(1)}, f32[8,256]{1,0:T(8,128)}, u32[]{:S(2)}) copy-start(f32[8,256]{1,0:T(8,128)} %constant.28.clone.lat_ref) | copy-start | bytes 24580
  0.7 18.9 %copy-start.1 = (f32[1,384]{1,0:T(1,128)S(1)}, f32[1,384]{1,0:T(1,128)}, u32[]{:S(2)}) copy-start(f32[1,384]{1,0:T(1,128)} %constant.29.clone.start_ref) | copy-start | bytes 4612
  11.9 16.9 %all-to-all-start = ((bf16[16,3,32,128]{3,2,1,0:T(8,128)(2,1)}), bf16[16,3,32,128]{3,2,1,0:T(8,128)(2,1)S(1)}, u32[]{:S(2)}, u32[]{:S(2)}) async-start(bf16[16,3,32,128]{3,2,1,0:T(8,128)(2,1)} %bitcast.31), calls=%async_computation | async-start | bytes 786432 | tf_op jit(solution)/shard_map/all_to_all | solution.py:559
  19.5 6.5 %copy-start.6 = (bf16[344,2048]{1,0:T(8,128)(2,1)S(1)}, bf16[344,2048]{1,0:T(8,128)(2,1)}, u32[]{:S(2)}) copy-start(bf16[344,2048]{1,0:T(8,128)(2,1)} %constant.27.clone) | copy-start | bytes 4227076
  30.2 13.2 %all-to-all-start.1 = ((bf16[8,48,384]{2,1,0:T(8,128)(2,1)}), bf16[8,48,384]{2,1,0:T(8,128)(2,1)S(1)}, u32[]{:S(2)}, u32[]{:S(2)}) async-start(bf16[8,48,384]{2,1,0:T(8,128)(2,1)} %forward_fourier.1), calls=%async_computation.1 | async-start | bytes 589824 | tf_op jit(solution)/shard_map/all_to_all | solution.py:575
  35.7 5.8 %copy-start.5 = (bf16[344,2048]{1,0:T(8,128)(2,1)S(1)}, bf16[344,2048]{1,0:T(8,128)(2,1)}, u32[]{:S(2)}) copy-start(bf16[344,2048]{1,0:T(8,128)(2,1)} %constant.31.clone) | copy-start | bytes 4227076
  42.5 16.7 %copy-start.7 = (bf16[6,3,64]{2,1,0:T(4,128)(2,1)S(1)}, bf16[6,3,64]{2,1,0:T(4,128)(2,1)}, u32[]{:S(2)}) copy-start(bf16[6,3,64]{2,1,0:T(4,128)(2,1)} %param.25) | copy-start | bytes 6916
  55.3 11.7 %all-to-all-start.2 = ((bf16[8,48,384]{2,1,0:T(8,128)(2,1)}), bf16[8,48,384]{2,1,0:T(8,128)(2,1)S(1)}, u32[]{:S(2)}, u32[]{:S(2)}) async-start(bf16[8,48,384]{2,1,0:T(8,128)(2,1)} %get-tuple-element.46), calls=%async_computation.2 | async-start | bytes 589824 | tf_op jit(solution)/shard_map/all_to_all | solution.py:584
  67.1 16.3 %copy-start.2 = (bf16[1536,208]{1,0:T(8,128)(2,1)S(1)}, bf16[1536,208]{1,0:T(8,128)(2,1)}, u32[]{:S(2)}) copy-start(bf16[1536,208]{1,0:T(8,128)(2,1)} %get-tuple-element.57.w1_ref) | copy-start | bytes 1916932
  67.1 16.3 %copy-start.3 = (bf16[144,1536]{1,0:T(8,128)(2,1)S(1)}, bf16[144,1536]{1,0:T(8,128)(2,1)}, u32[]{:S(2)}) copy-start(bf16[144,1536]{1,0:T(8,128)(2,1)} %get-tuple-element.58.w2_ref) | copy-start | bytes 1327108
  67.1 16.3 %copy-start.4 = (f32[144,128]{1,0:T(8,128)S(1)}, f32[144,128]{1,0:T(8,128)}, u32[]{:S(2)}) copy-start(f32[144,128]{1,0:T(8,128)} %get-tuple-element.59.b2_ref) | copy-start | bytes 221188

commit v4 on v3

--- a/solution.py
+++ b/solution.py
@@ -430,11 +430,24 @@
 
 
 WAVES = 8
-
-
-def spectral_kernel(wave_ref, x_ref, t0_ref, t1_ref, gain_ref, spec_ref, out_ref, c_ref, n_ref, r_ref, m_ref):
+GROUPS = -(-OWNED // WAVES)
+LAST = OWNED - (GROUPS - 1) * WAVES
+
+
+def spectral_kernel(wave_ref, x_ref, t0_ref, t1_ref, gain_ref, spec_ref, out_ref, c_ref, n_ref, r_ref, m_ref, t_ref, sems):
     step = pl.program_id(0)
     low = iota((MP, 128), 1) < 64
+
+    def table_copy(group):
+        first, count = group * WAVES, LAST if group == GROUPS - 1 else WAVES
+        source, at = (t0_ref, first) if first < MH else (t1_ref, first - MH)
+        return pltpu.make_async_copy(source.at[pl.ds(at, count)], t_ref.at[pl.ds(first, count)], sems.at[group])
+
+    @pl.when(step == 0)
+    def _():
+        for group in range(GROUPS):
+            table_copy(group).start()
+
     mirror = (iota((HALF, HALF), 0) + iota((HALF, HALF), 1) == HALF - 1).astype(F32).astype(BF)
 
     @pl.when(step == 0)
@@ -442,7 +455,9 @@
         for slab in (6, 7, 14, 15):
             for h in range(2):
                 c_ref[h, slab * SLAB : slab * SLAB + MP, :] = jnp.zeros((MP, 128), F32)
-        north = {}
+        for slab in range(6):
+            for h in range(4):
+                r_ref[h, slab * SLAB + OWNED : slab * SLAB + MP, :] = jnp.zeros((MP - OWNED, 128), F32)
         for pair in range(N_LAT // 2):
             for tile in range(3):
                 a = x_ref[2 * pair, :, 128 * tile : 128 * tile + 128].astype(F32)
@@ -465,26 +480,37 @@
     even = iota((8, KP), 1) % 2 == 0
     gain = gain_ref[...]
 
-    def waves(t_ref):
-        for mm in range(WAVES):
+    def waves(count):
+        boths = []
+        for mm in range(count):
             m = step * WAVES + mm
             left = jnp.concatenate([c_ref[h, pl.ds(m, 16, stride=SLAB), :] for h in range(2)], axis=1).astype(BF)
-            table = t_ref[mm]
-            both = lax.dot_general(left, table, NT, preferred_element_type=F32)
-            natural = jnp.where(even, both[:8], both[8:])
+            boths.append(lax.dot_general(left, t_ref[m], NT, preferred_element_type=F32))
+        rights = []
+        for mm in range(count):
+            m = step * WAVES + mm
+            natural = jnp.where(even, boths[mm][:8], boths[mm][8:])
             n_ref[0, pl.ds(m, 8, stride=SLAB), :] = natural[:, :128]
             n_ref[1, pl.ds(m, 8, stride=SLAB), :] = natural[:, 128:256]
             n_ref[2, pl.ds(m, 8, stride=SLAB), :] = jnp.concatenate([natural[:, 256:], jnp.zeros((8, 384 - KP), F32)], axis=1)
             scaled = natural * pltpu.roll(gain, 768 - wave_ref[m], 1)[:, :KP]
-            right = jnp.concatenate([jnp.where(even, scaled, 0.0), jnp.where(even, 0.0, scaled)], axis=0).astype(BF)
-            back = dot(right, table)
+            rights.append(jnp.concatenate([jnp.where(even, scaled, 0.0), jnp.where(even, 0.0, scaled)], axis=0).astype(BF))
+        for mm in range(count):
+            m = step * WAVES + mm
+            back = dot(rights[mm], t_ref[m])
             north, south = back[:8] + back[8:], back[:8] - back[8:]
             for h in range(2):
                 r_ref[h, pl.ds(m, 8, stride=SLAB), :] = north[:, 128 * h : 128 * h + 128]
                 r_ref[2 + h, pl.ds(m, 8, stride=SLAB), :] = south[:, 128 * h : 128 * h + 128]
 
-    pl.when(step < MH // WAVES)(lambda: waves(t0_ref))
-    pl.when(step >= MH // WAVES)(lambda: waves(t1_ref))
+    for group in range(GROUPS):
+
+        @pl.when(step == group)
+        def _():
+            table_copy(group).wait()
+
+    pl.when(step < GROUPS - 1)(lambda: waves(WAVES))
+    pl.when(step == GROUPS - 1)(lambda: waves(LAST))
 
     @pl.when(step == pl.num_programs(0) - 1)
     def _():
@@ -522,11 +548,11 @@
         spectral_kernel,
         grid_spec=pltpu.PrefetchScalarGridSpec(
             num_scalar_prefetch=1,
-            grid=(MP // WAVES,),
+            grid=(GROUPS,),
             in_specs=[
                 full(N_LAT, MP, 384),
-                pl.BlockSpec((WAVES, KP, HALF), lambda i, w: (jnp.minimum(i, MH // WAVES - 1), 0, 0)),
-                pl.BlockSpec((WAVES, KP, HALF), lambda i, w: (jnp.maximum(i - MH // WAVES, 0), 0, 0)),
+                pl.BlockSpec(memory_space=pltpu.HBM),
+                pl.BlockSpec(memory_space=pltpu.HBM),
                 full(8, 768),
             ],
             out_specs=(full(GROUP, OWNED, 2 * M), full(N_LAT, MP, 384)),
@@ -535,6 +561,8 @@
                 pltpu.VMEM((3, 8 * SLAB, 128), F32),
                 pltpu.VMEM((4, 8 * SLAB, 128), F32),
                 pltpu.VMEM((6 * MP, HALF), BF),
+                pltpu.VMEM((OWNED, KP, HALF), BF),
+                pltpu.SemaphoreType.DMA((GROUPS,)),
             ],
         ),
         out_shape=(

time: 94.2 us -> 89.5 us (0.950)
  Pallas kernels: 51.2 us -> 46.4 us
    pallas_call x1, Pallas kernels: 11.9 us -> 7.13 us  [spectral_step(): pl.pallas_call(spectral_kernel, grid_spec=pltpu.PrefetchScalarGridSpec(nu...]
  transfers between devices with their start and end apart: 3 -> 3, of which waited for: 3 -> 3; matrix products, arithmetic and copies ran while one was open for 4% -> 4% of each run, Pallas kernels for 16% -> 17%
where the time goes in v4:
time: 89.5 us; the launch traced here: 88.8 us
  Pallas kernels  46.4 us (52%)
  starting transfers between devices  16.3 us (18%)
  blocking collectives  14.9 us (17%)
  waiting for transfers between devices  6.5 us (7%)
  matrix products  2.03 us (2%)
  local copies, waits for them, and re-layouts  1.74 us (2%)
    all_to_all x1, blocking collectives, per_device(): filtered = lax.all_to_all(grid_values, 'lon', 0, 0, tiled=True)  14.9 us
    pallas_call x2, Pallas kernels, legendre_table(): pl.pallas_call(table_kernel, grid=(KP // CHUNK,), out_shape=pltpu.HBM((MH...  11.6 us
    pallas_call x1, Pallas kernels, first_conv(): pl.pallas_call(functools.partial(first_kernel, block), grid=(COLUMNS // b...  11.2 us
    pallas_call x1, Pallas kernels, second_conv(): pl.pallas_call(functools.partial(second_kernel, block), grid=(COLUMNS //...  10.2 us
    all_to_all x1, starting transfers between devices, per_device(): lax.all_to_all(tendency.reshape(N_LON, GROUP, TILES, 128), 'lon', 0, 0, t...  7.15 us
    pallas_call x1, Pallas kernels, spectral_step(): pl.pallas_call(spectral_kernel, grid_spec=pltpu.PrefetchScalarGridSpec(nu...  7.13 us
    all_to_all x1, starting transfers between devices, per_device(): coeffs = lax.all_to_all(coeffs, 'lat', 0, 0, tiled=True)  5.33 us
    all_to_all x1, starting transfers between devices, per_device(): returned = lax.all_to_all(returned, 'lat', 0, 0, tiled=True)  3.87 us
  transfers between devices with their start and end apart: 3, of which 3 were waited for; matrix products, arithmetic and copies ran while one was open for 4% of the time, Pallas kernels for 17%

profile of v4, /device:TPU:0, one launch (start us, length us, event | category | flops | bytes accessed | tf_op | source)
XLA Modules:
  0.0 88.8 jit_solution(15064767489012177875)
XLA Ops:
  0.7 11.2 %first_conv.1 = bf16[48,32,128]{2,1,0:T(8,128)(2,1)} custom-call(bf16[144,4096]{1,0:T(8,128)(2,1)} %bitcast.33, bf16[3,6,64]{2,1,0:T(8,128)(2,1)} %bitcast.35, f32[1,64]{1,0:T(1,128)} %bitcast.38, bf16[3,2,64]{2,1,0:T(2,128)(2,1)} %bitcast.37, s32[1,48]{1,0:T(1,128)} %bitcast.40, f32[1,2]{1,0:T(1,128)} %bitcast.39), custom_call_target="tpu_custom_call" | custom-call | flops 3000000000 | bytes 2000000 | tf_op jit(solution)/shard_map/first_conv/pallas_call | solution.py:205
  11.9 7.1 %all-to-all-start = ((bf16[16,3,32,128]{3,2,1,0:T(8,128)(2,1)}), bf16[16,3,32,128]{3,2,1,0:T(8,128)(2,1)S(1)}, u32[]{:S(2)}, u32[]{:S(2)}) async-start(bf16[16,3,32,128]{3,2,1,0:T(8,128)(2,1)} %bitcast.31), calls=%async_computation | async-start | bytes 786432 | tf_op jit(solution)/shard_map/all_to_all | solution.py:587
  19.0 0.1 reshape.49
  19.1 0.1 eq.15
  19.3 0.1 copy.19.wave_ref
  19.4 0.1 fusion
  19.6 5.8 %legendre_table.2.t0_ref = bf16[24,352,256]{2,1,0:T(8,128)(2,1)} custom-call(f32[24,1]{1,0:T(8,128)S(1)} %copy.19.wave_ref, f32[8,256]{1,0:T(8,128)S(1)} %copy-done, f32[1,384]{1,0:T(1,128)S(1)} %copy-done.1), custom_call_target="tpu_custom_call" | custom-call | flops 200000000 | bytes 9000000 | tf_op jit(solution)/shard_map/legendre_table/pallas_call | solution.py:336
  25.3 0.7 dynamic-slice_bitcast_fusion.q_ref
  26.0 1.0 %convolution_convert_fusion.f_ref.g_ref = bf16[384,2048]{1,0:T(8,128)(2,1)S(1)} fusion(bf16[344,2048]{1,0:T(8,128)(2,1)S(1)} %copy-done.6, s32[384]{0:T(512)S(1)} %eq.15), kind=kOutput, calls=%fused_computation | convolution fusion | flops 541983744 | bytes 2983424 | tf_op jit(solution)/shard_map/dot_general | solution.py:52
  27.0 1.8 %all-to-all-done.y_ref = bf16[16,3,32,128]{3,2,1,0:T(8,128)(2,1)S(1)} async-done(((bf16[16,3,32,128]{3,2,1,0:T(8,128)(2,1)}), bf16[16,3,32,128]{3,2,1,0:T(8,128)(2,1)S(1)}, u32[]{:S(2)}, u32[]{:S(2)}) %all-to-all-start) | async-done | bytes 393248 | tf_op jit(solution)/shard_map/all_to_all | solution.py:587
  28.8 1.4 %forward_fourier.1 = bf16[8,48,384]{2,1,0:T(8,128)(2,1)} custom-call(bf16[16,3,32,128]{3,2,1,0:T(8,128)(2,1)S(1)} %all-to-all-done.y_ref, bf16[384,2048]{1,0:T(8,128)(2,1)S(1)} %convolution_convert_fusion.f_ref.g_ref, bf16[384,2048]{1,0:T(8,128)(2,1)S(1)} %convolution_convert_fusion.f_ref.g_ref, f32[1,384]{1,0:T(1,128)S(1)} %dynamic-slice_bitcast_fusion.q_ref), custom_call_target="tpu_custom_call" | custom-call | flops 400000000 | bytes 3000000 | tf_op jit(solution)/shard_map/forward_fourier/pallas_call | solution.py:381
  30.2 5.3 %all-to-all-start.1 = ((bf16[8,48,384]{2,1,0:T(8,128)(2,1)}), bf16[8,48,384]{2,1,0:T(8,128)(2,1)S(1)}, u32[]{:S(2)}, u32[]{:S(2)}) async-start(bf16[8,48,384]{2,1,0:T(8,128)(2,1)} %forward_fourier.1), calls=%async_computation.1 | async-start | bytes 589824 | tf_op jit(solution)/shard_map/all_to_all | solution.py:603
  35.6 0.1 copy.20.wave_ref
  35.7 5.8 %legendre_table.3.t1_ref = bf16[24,352,256]{2,1,0:T(8,128)(2,1)} custom-call(f32[24,1]{1,0:T(8,128)S(1)} %copy.20.wave_ref, f32[8,256]{1,0:T(8,128)S(1)} %copy-done, f32[1,384]{1,0:T(1,128)S(1)} %copy-done.1), custom_call_target="tpu_custom_call" | custom-call | flops 200000000 | bytes 9000000 | tf_op jit(solution)/shard_map/legendre_table/pallas_call | solution.py:336
  41.5 1.0 %convolution_convert_fusion.1.f_ref.g_ref = bf16[384,2048]{1,0:T(8,128)(2,1)S(1)} fusion(bf16[384,344]{1,0:T(8,128)(2,1)S(1)} %fusion, bf16[344,2048]{1,0:T(8,128)(2,1)S(1)} %copy-done.5), kind=kOutput, calls=%fused_computation.1 | convolution fusion | flops 541851648 | bytes 3246080 | tf_op jit(solution)/shard_map/dot_general | solution.py:52
  42.5 1.0 %all-to-all-done.1.x_ref = bf16[8,48,384]{2,1,0:T(8,128)(2,1)S(1)} async-done(((bf16[8,48,384]{2,1,0:T(8,128)(2,1)}), bf16[8,48,384]{2,1,0:T(8,128)(2,1)S(1)}, u32[]{:S(2)}, u32[]{:S(2)}) %all-to-all-start.1) | async-done | bytes 294944 | tf_op jit(solution)/shard_map/all_to_all | solution.py:603
  43.5 7.1 %spectral_step.1 = (f32[3,43,688]{2,1,0:T(8,128)}, bf16[8,48,384]{2,1,0:T(8,128)(2,1)}) custom-call(s32[48]{0:T(128)S(1)} %get-tuple-element.34.wave_ref, bf16[8,48,384]{2,1,0:T(8,128)(2,1)S(1)} %all-to-all-done.1.x_ref, bf16[24,352,256]{2,1,0:T(8,128)(2,1)} %legendre_table.2.t0_ref, bf16[24,352,256]{2,1,0:T(8,128)(2,1)} %legendre_table.3.t1_ref, ...), custom_call_target="tpu_custom_call" | custom-call | flops 4000000000 | bytes 10000000 | tf_op jit(solution)/shard_map/spectral_step/pallas_call | solution.py:547
  50.6 3.9 %all-to-all-start.2 = ((bf16[8,48,384]{2,1,0:T(8,128)(2,1)}), bf16[8,48,384]{2,1,0:T(8,128)(2,1)S(1)}, u32[]{:S(2)}, u32[]{:S(2)}) async-start(bf16[8,48,384]{2,1,0:T(8,128)(2,1)} %get-tuple-element.46), calls=%async_computation.2 | async-start | bytes 589824 | tf_op jit(solution)/shard_map/all_to_all | solution.py:612
  54.5 0.6 copy.23
  55.1 3.5 %second_weights.1 = (bf16[1536,208]{1,0:T(8,128)(2,1)}, bf16[144,1536]{1,0:T(8,128)(2,1)}, f32[144,128]{1,0:T(8,128)}) custom-call(bf16[3,8,64]{2,1,0:T(8,128)(2,1)} %bitcast.36, f32[1,64]{1,0:T(1,128)} %bitcast.42, bf16[3,6,64]{2,1,0:T(8,128)(2,1)} %bitcast.32, s32[1,48]{1,0:T(1,128)} %bitcast.41, f32[1,6]{1,0:T(1,128)} %bitcast.43), custom_call_target="tpu_custom_call" | custom-call | flops 200000000 | bytes 2000000 | tf_op jit(solution)/shard_map/second_weights/pallas_call | solution.py:150
  58.6 3.8 %all-to-all-done.2 = bf16[8,48,384]{2,1,0:T(8,128)(2,1)S(1)} async-done(((bf16[8,48,384]{2,1,0:T(8,128)(2,1)}), bf16[8,48,384]{2,1,0:T(8,128)(2,1)S(1)}, u32[]{:S(2)}, u32[]{:S(2)}) %all-to-all-start.2) | async-done | bytes 294944 | tf_op jit(solution)/shard_map/all_to_all | solution.py:612
  62.4 1.5 %inverse_fourier.1 = bf16[16,3,32,128]{3,2,1,0:T(8,128)(2,1)} custom-call(bf16[384,384]{1,0:T(8,128)(2,1)S(1)} %bitcast.29, bf16[384,2048]{1,0:T(8,128)(2,1)S(1)} %convolution_convert_fusion.1.f_ref.g_ref, bf16[384,2048]{1,0:T(8,128)(2,1)S(1)} %convolution_convert_fusion.1.f_ref.g_ref), custom_call_target="tpu_custom_call" | custom-call | flops 400000000 | bytes 3000000 | tf_op jit(solution)/shard_map/inverse_fourier/pallas_call | solution.py:416
  63.8 14.9 %all_to_all.20 = bf16[16,3,32,128]{3,2,1,0:T(8,128)(2,1)S(1)} all-to-all(bf16[16,3,32,128]{3,2,1,0:T(8,128)(2,1)} %inverse_fourier.1), channel_id=1, replica_groups=mesh['lat'=8,'lon'=16] {'lon'}, dimensions={0} | all-to-all | bytes 786432 | tf_op jit(solution)/shard_map/all_to_all | solution.py:616
  78.7 10.2 %second_conv.1 = f32[144,4096]{1,0:T(8,128)} custom-call(bf16[144,4096]{1,0:T(8,128)(2,1)} %bitcast.34, bf16[48,32,128]{2,1,0:T(8,128)(2,1)S(1)} %bitcast.30, bf16[1536,208]{1,0:T(8,128)(2,1)S(1)} %copy-done.2, bf16[144,1536]{1,0:T(8,128)(2,1)S(1)} %copy-done.3, f32[144,128]{1,0:T(8,128)S(1)} %copy-done.4), custom_call_target="tpu_custom_call" | custom-call | flops 4000000000 | bytes 4000000 | tf_op jit(solution)/shard_map/second_conv/pallas_call | solution.py:255
  (25 shorter events, 0.1 us)
Async XLA Ops:
  0.6 18.4 %copy-start.8 = (s32[344]{0:T(512)S(1)}, s32[344]{0:T(512)}, u32[]{:S(2)}) copy-start(s32[344]{0:T(512)} %param.28) | copy-start | bytes 4132
  0.6 18.9 %copy-start.9 = (f32[344]{0:T(512)S(1)}, f32[344]{0:T(512)}, u32[]{:S(2)}) copy-start(f32[344]{0:T(512)} %param.22) | copy-start | bytes 4132
  0.7 18.9 %copy-start = (f32[8,256]{1,0:T(8,128)S(1)}, f32[8,256]{1,0:T(8,128)}, u32[]{:S(2)}) copy-start(f32[8,256]{1,0:T(8,128)} %constant.28.clone.lat_ref) | copy-start | bytes 24580
  0.7 18.9 %copy-start.1 = (f32[1,384]{1,0:T(1,128)S(1)}, f32[1,384]{1,0:T(1,128)}, u32[]{:S(2)}) copy-start(f32[1,384]{1,0:T(1,128)} %constant.29.clone.start_ref) | copy-start | bytes 4612
  11.9 16.9 %all-to-all-start = ((bf16[16,3,32,128]{3,2,1,0:T(8,128)(2,1)}), bf16[16,3,32,128]{3,2,1,0:T(8,128)(2,1)S(1)}, u32[]{:S(2)}, u32[]{:S(2)}) async-start(bf16[16,3,32,128]{3,2,1,0:T(8,128)(2,1)} %bitcast.31), calls=%async_computation | async-start | bytes 786432 | tf_op jit(solution)/shard_map/all_to_all | solution.py:587
  19.5 6.5 %copy-start.6 = (bf16[344,2048]{1,0:T(8,128)(2,1)S(1)}, bf16[344,2048]{1,0:T(8,128)(2,1)}, u32[]{:S(2)}) copy-start(bf16[344,2048]{1,0:T(8,128)(2,1)} %constant.27.clone) | copy-start | bytes 4227076
  30.2 13.2 %all-to-all-start.1 = ((bf16[8,48,384]{2,1,0:T(8,128)(2,1)}), bf16[8,48,384]{2,1,0:T(8,128)(2,1)S(1)}, u32[]{:S(2)}, u32[]{:S(2)}) async-start(bf16[8,48,384]{2,1,0:T(8,128)(2,1)} %forward_fourier.1), calls=%async_computation.1 | async-start | bytes 589824 | tf_op jit(solution)/shard_map/all_to_all | solution.py:603
  35.7 5.8 %copy-start.5 = (bf16[344,2048]{1,0:T(8,128)(2,1)S(1)}, bf16[344,2048]{1,0:T(8,128)(2,1)}, u32[]{:S(2)}) copy-start(bf16[344,2048]{1,0:T(8,128)(2,1)} %constant.31.clone) | copy-start | bytes 4227076
  42.5 12.0 %copy-start.7 = (bf16[6,3,64]{2,1,0:T(4,128)(2,1)S(1)}, bf16[6,3,64]{2,1,0:T(4,128)(2,1)}, u32[]{:S(2)}) copy-start(bf16[6,3,64]{2,1,0:T(4,128)(2,1)} %param.25) | copy-start | bytes 6916
  50.6 11.8 %all-to-all-start.2 = ((bf16[8,48,384]{2,1,0:T(8,128)(2,1)}), bf16[8,48,384]{2,1,0:T(8,128)(2,1)S(1)}, u32[]{:S(2)}, u32[]{:S(2)}) async-start(bf16[8,48,384]{2,1,0:T(8,128)(2,1)} %get-tuple-element.46), calls=%async_computation.2 | async-start | bytes 589824 | tf_op jit(solution)/shard_map/all_to_all | solution.py:612
  62.4 16.3 %copy-start.2 = (bf16[1536,208]{1,0:T(8,128)(2,1)S(1)}, bf16[1536,208]{1,0:T(8,128)(2,1)}, u32[]{:S(2)}) copy-start(bf16[1536,208]{1,0:T(8,128)(2,1)} %get-tuple-element.57.w1_ref) | copy-start | bytes 1916932
  62.4 16.3 %copy-start.3 = (bf16[144,1536]{1,0:T(8,128)(2,1)S(1)}, bf16[144,1536]{1,0:T(8,128)(2,1)}, u32[]{:S(2)}) copy-start(bf16[144,1536]{1,0:T(8,128)(2,1)} %get-tuple-element.58.w2_ref) | copy-start | bytes 1327108
  62.4 16.3 %copy-start.4 = (f32[144,128]{1,0:T(8,128)S(1)}, f32[144,128]{1,0:T(8,128)}, u32[]{:S(2)}) copy-start(f32[144,128]{1,0:T(8,128)} %get-tuple-element.59.b2_ref) | copy-start | bytes 221188

commit v5 on v4

--- a/solution.py
+++ b/solution.py
@@ -100,21 +100,26 @@
         var_col = jnp.where(column < base, var_col + FIELDS, slot_field)
         level_col = jnp.where(column < base, level_col, wide_order - LV * slot_field)
     level_col = jnp.where(column < width - 16, level_col, -100)
-    r = iota((HID, CH), 0)
-    spread = (over_levels(r) == iota((HID, CH), 1)).astype(F32).astype(BF)
-    level_row = iota((HID, width), 0)
-    level_row = level_row - LV * over_levels(level_row)
-    total = jnp.zeros((HID, width), F32)
     pick = (iota((variables, width), 0) == var_col).astype(F32).astype(BF)
+    same = (iota((CH, CH), 0) == iota((CH, CH), 1)).astype(F32).astype(BF)
+    blocks = []
     for tap in range(3):
-        tall = lax.dot_general(spread, w1_ref[tap], NT, preferred_element_type=F32)
-        wide = dot((0.5 * tall).astype(BF), pick)
-        total = jnp.where(level_col == level_row + 2 * (tap - 1), wide, total)
+        turned = lax.dot_general(same, w1_ref[tap], NT, preferred_element_type=F32)
+        blocks.append(dot((0.5 * turned).astype(BF), pick))
     bias = 0.5 * to_column(bias1_ref[...])
     high = bias.astype(BF).astype(F32)
     low = bias - high
-    block = jnp.where(column == width - 16, high, jnp.where(column == width - 15, low, 0.0)).astype(BF)
-    o1_ref[...] = (total + dot(spread, block)).astype(BF)
+    bias_block = jnp.where(column == width - 16, high, jnp.where(column == width - 15, low, 0.0))
+    level_row = iota((LV, width), 0)
+    hits = [level_col == level_row + 2 * (tap - 1) for tap in range(3)]
+    for channel in range(0, CH, 2):
+        pair = []
+        for o in (channel, channel + 1):
+            rows_o = jnp.broadcast_to(bias_block[o : o + 1], (LV, width))
+            for tap in range(3):
+                rows_o = jnp.where(hits[tap], blocks[tap][o : o + 1], rows_o)
+            pair.append(rows_o)
+        o1_ref[channel * LV : (channel + 2) * LV, :] = jnp.concatenate(pair, axis=0).astype(BF)
     if slots_in:
         row = iota((rows, 1), 0)
         field_row = over_levels(row)
@@ -122,9 +127,8 @@
         row = to_column(order.astype(F32)).astype(jnp.int32)
         field_row = (row >= LV).astype(jnp.int32)
     level_out = row - LV * field_row
-    c = iota((CH, HID), 1)
-    spread2 = (over_levels(c) == iota((CH, HID), 0)).astype(F32).astype(BF)
-    level_hid = iota((rows, HID), 1)
+    spread2 = (over_levels(iota((1, HID), 1)) == iota((CH, HID), 0)).astype(F32).astype(BF)
+    level_hid = iota((1, HID), 1)
     level_hid = level_hid - LV * over_levels(level_hid)
     total2 = jnp.zeros((rows, HID), F32)
     bias2 = jnp.zeros((rows, 128), F32)
@@ -277,6 +281,7 @@
 
 CHUNK = 176
 STRIDE = CHUNK + 1
+LANES = -(-CHUNK // 128) * 128
 
 
 def table_kernel(wave_ref, lat_ref, start_ref, out_ref, now_ref, old_ref, log_ref, ratio_ref, s_ref):
@@ -300,7 +305,14 @@
     log_scale = [log_ref[h] for h in range(2)]
     ratio = ratio_ref[...]
     scale = [None, None]
-    first = (step * CHUNK).astype(F32)
+    k = (step * CHUNK).astype(F32) + iota((MH, LANES), 1).astype(F32)
+    m = jnp.broadcast_to(wave_ref[...], (MH, LANES))
+    n = m + k
+    top = 4.0 * (n * n) - 1.0
+    bottom = k * (m + n)
+    root = lax.rsqrt(jnp.maximum(top * bottom, 1e-30))
+    ups = jnp.where(n <= M - 1.0, top * root, 0.0)
+    ratios = bottom * root
     for kk in range(CHUNK):
         if kk % 8 == 0:
             for h in range(2):
@@ -310,19 +322,14 @@
                 old[h] = old[h] * shrink
                 log_scale[h] = log_scale[h] + jnp.where(big, math.log(1e12), 0.0)
                 scale[h] = jnp.exp(log_scale[h])
-        k = first + kk
-        n = wave + k
-        top = 4.0 * (n * n) - 1.0
-        bottom = k * (wave + n)
-        root = lax.rsqrt(jnp.maximum(top * bottom, 1e-30))
-        up = jnp.where(n <= M - 1.0, top * root, 0.0)
+        up = jnp.broadcast_to(ups[:, kk : kk + 1], (MH, 128))
         for h in range(2):
             stepped = up * (sine[h] * now[h] - ratio * old[h])
             if kk == 0:
                 stepped = jnp.where(step == 0, 1.0, stepped)
             old[h], now[h] = now[h], stepped
             s_ref[h, pl.ds(kk, MH, stride=STRIDE), :] = stepped * scale[h]
-        ratio = bottom * root
+        ratio = jnp.broadcast_to(ratios[:, kk : kk + 1], (MH, 128))
     for h in range(2):
         now_ref[h], old_ref[h], log_ref[h] = now[h], old[h], log_scale[h]
     ratio_ref[...] = ratio
@@ -599,19 +606,19 @@
     pieces, table0, tables, gain, owned = lax.optimization_barrier((pieces, table0, tables, gain, owned))
 
     coeffs = forward_fourier(pieces, tables, band_quad)
-    coeffs, waves_late, chosen = lax.optimization_barrier((coeffs, waves_f[MH:], chosen))
+    coeffs, waves_late = lax.optimization_barrier((coeffs, waves_f[MH:]))
     coeffs = lax.all_to_all(coeffs, "lat", 0, 0, tiled=True)
     table1 = legendre_table(waves_late, lat_rows, start)
-    inverse_tables = dot(chosen, jnp.asarray(trig[:, 2 * NLON :])).astype(BF)
-    coeffs, table1, inverse_tables = lax.optimization_barrier((coeffs, table1, inverse_tables))
+    coeffs, table1 = lax.optimization_barrier((coeffs, table1))
 
     spectrum, returned = spectral_step(owned, coeffs, table0, table1, gain)
-    returned, mix_in, blend_bias, mix_out, mix_out_bias, level_order = lax.optimization_barrier(
-        (returned, mix_in, blend_bias, mix_out, mix_out_bias, level_order)
+    returned, mix_in, blend_bias, mix_out, mix_out_bias, level_order, chosen = lax.optimization_barrier(
+        (returned, mix_in, blend_bias, mix_out, mix_out_bias, level_order, chosen)
     )
     returned = lax.all_to_all(returned, "lat", 0, 0, tiled=True)
     m1, m2, mb = second_weights(mix_in.transpose(1, 2, 0), blend_bias, mix_out.transpose(1, 0, 2), mix_out_bias, level_order)
-    returned, m1, m2, mb = lax.optimization_barrier((returned, m1, m2, mb))
+    inverse_tables = dot(chosen, jnp.asarray(trig[:, 2 * NLON :])).astype(BF)
+    returned, m1, m2, mb, inverse_tables = lax.optimization_barrier((returned, m1, m2, mb, inverse_tables))
     grid_values = inverse_fourier(returned.reshape(N_LAT * MP, 384), inverse_tables)
     filtered = lax.all_to_all(grid_values, "lon", 0, 0, tiled=True)
     increment = second_conv(columns, filtered.reshape(ITEMS, TILES, 128), m1, m2, mb)

time: 89.5 us -> 87.5 us (0.978)
  Pallas kernels: 46.4 us -> 42.7 us
  waiting for transfers between devices: 6.5 us -> 8.12 us
  blocking collectives: 14.9 us -> 13.8 us
  matrix products: 2.03 us -> 2.99 us
    pallas_call x2, Pallas kernels: 11.6 us -> 9.84 us  [legendre_table(): pl.pallas_call(table_kernel, grid=(KP // CHUNK,), out_shape=pltpu.HBM((MH...]
    pallas_call x1, Pallas kernels: 11.2 us -> 10.1 us  [first_conv(): pl.pallas_call(functools.partial(first_kernel, block), grid=(COLUMNS // b...]
    all_to_all x1, blocking collectives: 14.9 us -> 13.8 us  [per_device(): filtered = lax.all_to_all(grid_values, 'lon', 0, 0, tiled=True)]
    all_to_all x1, waiting for transfers between devices: 0.96 us -> 2.01 us  [per_device(): coeffs = lax.all_to_all(coeffs, 'lat', 0, 0, tiled=True)]
    all_to_all x1, waiting for transfers between devices: 1.75 us -> 2.77 us  [per_device(): lax.all_to_all(tendency.reshape(N_LON, GROUP, TILES, 128), 'lon', 0, 0, t...]
    pallas_call x1, Pallas kernels: 3.5 us -> 2.51 us  [second_weights(): pl.pallas_call(weights_kernel, out_shape=(pltpu.HBM((HID, width), BF), pl...]
    dot_general x2, matrix products: 2.03 us -> 2.99 us  [dot(): return jnp.dot(a, b, preferred_element_type=F32)]
  transfers between devices with their start and end apart: 3 -> 3, of which waited for: 3 -> 3; matrix products, arithmetic and copies ran while one was open for 4% -> 6% of each run, Pallas kernels for 17% -> 14%
where the time goes in v5:
time: 87.5 us; the launch traced here: 86.9 us
  Pallas kernels  42.7 us (49%)
  starting transfers between devices  15.9 us (18%)
  blocking collectives  13.8 us (16%)
  waiting for transfers between devices  8.12 us (9%)
  matrix products  2.99 us (3%)
  local copies, waits for them, and re-layouts  1.74 us (2%)
    all_to_all x1, blocking collectives, per_device(): filtered = lax.all_to_all(grid_values, 'lon', 0, 0, tiled=True)  13.8 us
    pallas_call x1, Pallas kernels, second_conv(): pl.pallas_call(functools.partial(second_kernel, block), grid=(COLUMNS //...  10.1 us
    pallas_call x1, Pallas kernels, first_conv(): pl.pallas_call(functools.partial(first_kernel, block), grid=(COLUMNS // b...  10.1 us
    pallas_call x2, Pallas kernels, legendre_table(): pl.pallas_call(table_kernel, grid=(KP // CHUNK,), out_shape=pltpu.HBM((MH...  9.84 us
    pallas_call x1, Pallas kernels, spectral_step(): pl.pallas_call(spectral_kernel, grid_spec=pltpu.PrefetchScalarGridSpec(nu...  7.14 us
    all_to_all x1, starting transfers between devices, per_device(): lax.all_to_all(tendency.reshape(N_LON, GROUP, TILES, 128), 'lon', 0, 0, t...  7.12 us
    all_to_all x1, starting transfers between devices, per_device(): coeffs = lax.all_to_all(coeffs, 'lat', 0, 0, tiled=True)  5.35 us
    all_to_all x1, starting transfers between devices, per_device(): returned = lax.all_to_all(returned, 'lat', 0, 0, tiled=True)  3.42 us
  transfers between devices with their start and end apart: 3, of which 3 were waited for; matrix products, arithmetic and copies ran while one was open for 6% of the time, Pallas kernels for 14%

profile of v5, /device:TPU:0, one launch (start us, length us, event | category | flops | bytes accessed | tf_op | source)
XLA Modules:
  0.0 86.9 jit_solution(9258261705049872471)
XLA Ops:
  0.7 10.1 %first_conv.1 = bf16[48,32,128]{2,1,0:T(8,128)(2,1)} custom-call(bf16[144,4096]{1,0:T(8,128)(2,1)} %bitcast.33, bf16[3,6,64]{2,1,0:T(8,128)(2,1)} %bitcast.35, f32[1,64]{1,0:T(1,128)} %bitcast.38, bf16[3,2,64]{2,1,0:T(2,128)(2,1)} %bitcast.37, s32[1,48]{1,0:T(1,128)} %bitcast.40, f32[1,2]{1,0:T(1,128)} %bitcast.39), custom_call_target="tpu_custom_call" | custom-call | flops 3000000000 | bytes 2000000 | tf_op jit(solution)/shard_map/first_conv/pallas_call | solution.py:209
  10.8 7.1 %all-to-all-start = ((bf16[16,3,32,128]{3,2,1,0:T(8,128)(2,1)}), bf16[16,3,32,128]{3,2,1,0:T(8,128)(2,1)S(1)}, u32[]{:S(2)}, u32[]{:S(2)}) async-start(bf16[16,3,32,128]{3,2,1,0:T(8,128)(2,1)} %bitcast.31), calls=%async_computation | async-start | bytes 786432 | tf_op jit(solution)/shard_map/all_to_all | solution.py:594
  17.9 0.1 reshape.49
  18.1 0.1 copy.19.wave_ref
  18.2 0.1 eq.15
  18.3 4.9 %legendre_table.2.t0_ref = bf16[24,352,256]{2,1,0:T(8,128)(2,1)} custom-call(f32[24,1]{1,0:T(8,128)S(1)} %copy.19.wave_ref, f32[8,256]{1,0:T(8,128)S(1)} %copy-done, f32[1,384]{1,0:T(1,128)S(1)} %copy-done.1), custom_call_target="tpu_custom_call" | custom-call | flops 200000000 | bytes 9000000 | tf_op jit(solution)/shard_map/legendre_table/pallas_call | solution.py:343
  23.2 0.7 dynamic-slice_bitcast_fusion.q_ref
  23.9 1.1 %convolution_convert_fusion.f_ref.g_ref = bf16[384,2048]{1,0:T(8,128)(2,1)S(1)} fusion(bf16[344,2048]{1,0:T(8,128)(2,1)S(1)} %copy-done.6, s32[384]{0:T(512)S(1)} %eq.15), kind=kOutput, calls=%fused_computation | convolution fusion | flops 541983744 | bytes 2983424 | tf_op jit(solution)/shard_map/dot_general | solution.py:52
  25.0 2.8 %all-to-all-done.y_ref = bf16[16,3,32,128]{3,2,1,0:T(8,128)(2,1)S(1)} async-done(((bf16[16,3,32,128]{3,2,1,0:T(8,128)(2,1)}), bf16[16,3,32,128]{3,2,1,0:T(8,128)(2,1)S(1)}, u32[]{:S(2)}, u32[]{:S(2)}) %all-to-all-start) | async-done | bytes 393248 | tf_op jit(solution)/shard_map/all_to_all | solution.py:594
  27.8 1.5 %forward_fourier.1 = bf16[8,48,384]{2,1,0:T(8,128)(2,1)} custom-call(bf16[16,3,32,128]{3,2,1,0:T(8,128)(2,1)S(1)} %all-to-all-done.y_ref, bf16[384,2048]{1,0:T(8,128)(2,1)S(1)} %convolution_convert_fusion.f_ref.g_ref, bf16[384,2048]{1,0:T(8,128)(2,1)S(1)} %convolution_convert_fusion.f_ref.g_ref, f32[1,384]{1,0:T(1,128)S(1)} %dynamic-slice_bitcast_fusion.q_ref), custom_call_target="tpu_custom_call" | custom-call | flops 400000000 | bytes 3000000 | tf_op jit(solution)/shard_map/forward_fourier/pallas_call | solution.py:388
  29.2 5.4 %all-to-all-start.1 = ((bf16[8,48,384]{2,1,0:T(8,128)(2,1)}), bf16[8,48,384]{2,1,0:T(8,128)(2,1)S(1)}, u32[]{:S(2)}, u32[]{:S(2)}) async-start(bf16[8,48,384]{2,1,0:T(8,128)(2,1)} %forward_fourier.1), calls=%async_computation.1 | async-start | bytes 589824 | tf_op jit(solution)/shard_map/all_to_all | solution.py:610
  34.6 0.9 fusion
  35.4 0.1 copy.20.wave_ref
  35.5 4.9 %legendre_table.3.t1_ref = bf16[24,352,256]{2,1,0:T(8,128)(2,1)} custom-call(f32[24,1]{1,0:T(8,128)S(1)} %copy.20.wave_ref, f32[8,256]{1,0:T(8,128)S(1)} %copy-done, f32[1,384]{1,0:T(1,128)S(1)} %copy-done.1), custom_call_target="tpu_custom_call" | custom-call | flops 200000000 | bytes 9000000 | tf_op jit(solution)/shard_map/legendre_table/pallas_call | solution.py:343
  40.4 2.0 %all-to-all-done.1.x_ref = bf16[8,48,384]{2,1,0:T(8,128)(2,1)S(1)} async-done(((bf16[8,48,384]{2,1,0:T(8,128)(2,1)}), bf16[8,48,384]{2,1,0:T(8,128)(2,1)S(1)}, u32[]{:S(2)}, u32[]{:S(2)}) %all-to-all-start.1) | async-done | bytes 294944 | tf_op jit(solution)/shard_map/all_to_all | solution.py:610
  42.5 7.1 %spectral_step.1 = (f32[3,43,688]{2,1,0:T(8,128)}, bf16[8,48,384]{2,1,0:T(8,128)(2,1)}) custom-call(s32[48]{0:T(128)S(1)} %get-tuple-element.34.wave_ref, bf16[8,48,384]{2,1,0:T(8,128)(2,1)S(1)} %all-to-all-done.1.x_ref, bf16[24,352,256]{2,1,0:T(8,128)(2,1)} %legendre_table.2.t0_ref, bf16[24,352,256]{2,1,0:T(8,128)(2,1)} %legendre_table.3.t1_ref, ...), custom_call_target="tpu_custom_call" | custom-call | flops 4000000000 | bytes 10000000 | tf_op jit(solution)/shard_map/spectral_step/pallas_call | solution.py:554
  49.6 0.6 copy.23
  50.2 3.4 %all-to-all-start.2 = ((bf16[8,48,384]{2,1,0:T(8,128)(2,1)}), bf16[8,48,384]{2,1,0:T(8,128)(2,1)S(1)}, u32[]{:S(2)}, u32[]{:S(2)}) async-start(bf16[8,48,384]{2,1,0:T(8,128)(2,1)} %get-tuple-element.45), calls=%async_computation.2 | async-start | bytes 589824 | tf_op jit(solution)/shard_map/all_to_all | solution.py:618
  53.6 2.5 %second_weights.1 = (bf16[1536,208]{1,0:T(8,128)(2,1)}, bf16[144,1536]{1,0:T(8,128)(2,1)}, f32[144,128]{1,0:T(8,128)}) custom-call(bf16[3,8,64]{2,1,0:T(8,128)(2,1)} %bitcast.36, f32[1,64]{1,0:T(1,128)} %bitcast.42, bf16[3,6,64]{2,1,0:T(8,128)(2,1)} %bitcast.32, s32[1,48]{1,0:T(1,128)} %bitcast.41, f32[1,6]{1,0:T(1,128)} %bitcast.43), custom_call_target="tpu_custom_call" | custom-call | flops 200000000 | bytes 2000000 | tf_op jit(solution)/shard_map/second_weights/pallas_call | solution.py:154
  56.2 1.9 %convolution_convert_fusion.1.f_ref.g_ref = bf16[384,2048]{1,0:T(8,128)(2,1)S(1)} fusion(bf16[384,344]{1,0:T(8,128)(2,1)} %fusion, bf16[344,2048]{1,0:T(8,128)(2,1)S(1)} %copy-done.5), kind=kOutput, calls=%fused_computation.1 | convolution fusion | flops 541851648 | bytes 3246080 | tf_op jit(solution)/shard_map/dot_general | solution.py:52
  58.1 3.3 %all-to-all-done.2 = bf16[8,48,384]{2,1,0:T(8,128)(2,1)S(1)} async-done(((bf16[8,48,384]{2,1,0:T(8,128)(2,1)}), bf16[8,48,384]{2,1,0:T(8,128)(2,1)S(1)}, u32[]{:S(2)}, u32[]{:S(2)}) %all-to-all-start.2) | async-done | bytes 294944 | tf_op jit(solution)/shard_map/all_to_all | solution.py:618
  61.5 1.4 %inverse_fourier.1 = bf16[16,3,32,128]{3,2,1,0:T(8,128)(2,1)} custom-call(bf16[384,384]{1,0:T(8,128)(2,1)S(1)} %bitcast.29, bf16[384,2048]{1,0:T(8,128)(2,1)S(1)} %convolution_convert_fusion.1.f_ref.g_ref, bf16[384,2048]{1,0:T(8,128)(2,1)S(1)} %convolution_convert_fusion.1.f_ref.g_ref), custom_call_target="tpu_custom_call" | custom-call | flops 400000000 | bytes 3000000 | tf_op jit(solution)/shard_map/inverse_fourier/pallas_call | solution.py:423
  62.9 13.8 %all_to_all.20 = bf16[16,3,32,128]{3,2,1,0:T(8,128)(2,1)S(1)} all-to-all(bf16[16,3,32,128]{3,2,1,0:T(8,128)(2,1)} %inverse_fourier.1), channel_id=1, replica_groups=mesh['lat'=8,'lon'=16] {'lon'}, dimensions={0} | all-to-all | bytes 786432 | tf_op jit(solution)/shard_map/all_to_all | solution.py:623
  76.7 10.1 %second_conv.1 = f32[144,4096]{1,0:T(8,128)} custom-call(bf16[144,4096]{1,0:T(8,128)(2,1)} %bitcast.34, bf16[48,32,128]{2,1,0:T(8,128)(2,1)S(1)} %bitcast.30, bf16[1536,208]{1,0:T(8,128)(2,1)S(1)} %copy-done.2, bf16[144,1536]{1,0:T(8,128)(2,1)S(1)} %copy-done.3, f32[144,128]{1,0:T(8,128)S(1)} %copy-done.4), custom_call_target="tpu_custom_call" | custom-call | flops 4000000000 | bytes 4000000 | tf_op jit(solution)/shard_map/second_conv/pallas_call | solution.py:259
  (25 shorter events, 0.1 us)
Async XLA Ops:
  0.6 17.3 %copy-start.8 = (s32[344]{0:T(512)S(1)}, s32[344]{0:T(512)}, u32[]{:S(2)}) copy-start(s32[344]{0:T(512)} %param.28) | copy-start | bytes 4132
  0.6 17.6 %copy-start.9 = (f32[344]{0:T(512)S(1)}, f32[344]{0:T(512)}, u32[]{:S(2)}) copy-start(f32[344]{0:T(512)} %param.22) | copy-start | bytes 4132
  0.7 17.7 %copy-start = (f32[8,256]{1,0:T(8,128)S(1)}, f32[8,256]{1,0:T(8,128)}, u32[]{:S(2)}) copy-start(f32[8,256]{1,0:T(8,128)} %constant.28.clone.lat_ref) | copy-start | bytes 24580
  0.7 17.7 %copy-start.1 = (f32[1,384]{1,0:T(1,128)S(1)}, f32[1,384]{1,0:T(1,128)}, u32[]{:S(2)}) copy-start(f32[1,384]{1,0:T(1,128)} %constant.29.clone.start_ref) | copy-start | bytes 4612
  10.8 16.9 %all-to-all-start = ((bf16[16,3,32,128]{3,2,1,0:T(8,128)(2,1)}), bf16[16,3,32,128]{3,2,1,0:T(8,128)(2,1)S(1)}, u32[]{:S(2)}, u32[]{:S(2)}) async-start(bf16[16,3,32,128]{3,2,1,0:T(8,128)(2,1)} %bitcast.31), calls=%async_computation | async-start | bytes 786432 | tf_op jit(solution)/shard_map/all_to_all | solution.py:594
  18.3 5.6 %copy-start.6 = (bf16[344,2048]{1,0:T(8,128)(2,1)S(1)}, bf16[344,2048]{1,0:T(8,128)(2,1)}, u32[]{:S(2)}) copy-start(bf16[344,2048]{1,0:T(8,128)(2,1)} %constant.27.clone) | copy-start | bytes 4227076
  29.2 13.2 %all-to-all-start.1 = ((bf16[8,48,384]{2,1,0:T(8,128)(2,1)}), bf16[8,48,384]{2,1,0:T(8,128)(2,1)S(1)}, u32[]{:S(2)}, u32[]{:S(2)}) async-start(bf16[8,48,384]{2,1,0:T(8,128)(2,1)} %forward_fourier.1), calls=%async_computation.1 | async-start | bytes 589824 | tf_op jit(solution)/shard_map/all_to_all | solution.py:610
  40.4 9.2 %copy-start.7 = (bf16[6,3,64]{2,1,0:T(4,128)(2,1)S(1)}, bf16[6,3,64]{2,1,0:T(4,128)(2,1)}, u32[]{:S(2)}) copy-start(bf16[6,3,64]{2,1,0:T(4,128)(2,1)} %param.25) | copy-start | bytes 6916
  42.5 13.7 %copy-start.5 = (bf16[344,2048]{1,0:T(8,128)(2,1)S(1)}, bf16[344,2048]{1,0:T(8,128)(2,1)}, u32[]{:S(2)}) copy-start(bf16[344,2048]{1,0:T(8,128)(2,1)} %constant.31.clone) | copy-start | bytes 4227076
  50.2 11.2 %all-to-all-start.2 = ((bf16[8,48,384]{2,1,0:T(8,128)(2,1)}), bf16[8,48,384]{2,1,0:T(8,128)(2,1)S(1)}, u32[]{:S(2)}, u32[]{:S(2)}) async-start(bf16[8,48,384]{2,1,0:T(8,128)(2,1)} %get-tuple-element.45), calls=%async_computation.2 | async-start | bytes 589824 | tf_op jit(solution)/shard_map/all_to_all | solution.py:618
  61.4 15.3 %copy-start.2 = (bf16[1536,208]{1,0:T(8,128)(2,1)S(1)}, bf16[1536,208]{1,0:T(8,128)(2,1)}, u32[]{:S(2)}) copy-start(bf16[1536,208]{1,0:T(8,128)(2,1)} %get-tuple-element.57.w1_ref) | copy-start | bytes 1916932
  61.5 15.3 %copy-start.3 = (bf16[144,1536]{1,0:T(8,128)(2,1)S(1)}, bf16[144,1536]{1,0:T(8,128)(2,1)}, u32[]{:S(2)}) copy-start(bf16[144,1536]{1,0:T(8,128)(2,1)} %get-tuple-element.58.w2_ref) | copy-start | bytes 1327108
  61.5 15.3 %copy-start.4 = (f32[144,128]{1,0:T(8,128)S(1)}, f32[144,128]{1,0:T(8,128)}, u32[]{:S(2)}) copy-start(f32[144,128]{1,0:T(8,128)} %get-tuple-element.59.b2_ref) | copy-start | bytes 221188

commit v6 on v5

--- a/solution.py
+++ b/solution.py
@@ -24,6 +24,7 @@
 KP = 352
 HALF = NLAT // 2
 HID = CH * LV
+BAND = 8
 SLAB = 49
 BF, F32 = jnp.bfloat16, jnp.float32
 NT = (((1,), (1,)), ((), ()))
@@ -88,7 +89,7 @@
 
 def make_weights(w1_ref, bias1_ref, w2_ref, order_ref, bias2_ref, slots_in, o1_ref, o2_ref, ob_ref):
     width, rows = o1_ref.shape[1], o2_ref.shape[0]
-    variables, fields = w1_ref.shape[1], w2_ref.shape[1]
+    variables, fields = w1_ref.shape[1], bias2_ref.shape[1]
     order = order_ref[...]
     base = VARS * LV
     column = iota((1, width), 1)
@@ -110,32 +111,29 @@
     high = bias.astype(BF).astype(F32)
     low = bias - high
     bias_block = jnp.where(column == width - 16, high, jnp.where(column == width - 15, low, 0.0))
-    level_row = iota((LV, width), 0)
-    hits = [level_col == level_row + 2 * (tap - 1) for tap in range(3)]
-    for channel in range(0, CH, 2):
-        pair = []
-        for o in (channel, channel + 1):
-            rows_o = jnp.broadcast_to(bias_block[o : o + 1], (LV, width))
-            for tap in range(3):
-                rows_o = jnp.where(hits[tap], blocks[tap][o : o + 1], rows_o)
-            pair.append(rows_o)
-        o1_ref[channel * LV : (channel + 2) * LV, :] = jnp.concatenate(pair, axis=0).astype(BF)
+    for level in range(LV):
+        block = bias_block
+        for tap in range(3):
+            block = jnp.where(level_col == level + 2 * (tap - 1), blocks[tap], block)
+        o1_ref[level * CH : (level + 1) * CH, :] = block.astype(BF)
+    hidden = o2_ref.shape[1]
     if slots_in:
         row = iota((rows, 1), 0)
-        field_row = over_levels(row)
+        level_out = (row >> 3) - 2
+        field_row = row & 7
     else:
         row = to_column(order.astype(F32)).astype(jnp.int32)
         field_row = (row >= LV).astype(jnp.int32)
-    level_out = row - LV * field_row
-    spread2 = (over_levels(iota((1, HID), 1)) == iota((CH, HID), 0)).astype(F32).astype(BF)
-    level_hid = iota((1, HID), 1)
-    level_hid = level_hid - LV * over_levels(level_hid)
-    total2 = jnp.zeros((rows, HID), F32)
+        level_out = row - LV * field_row
+    spread2 = ((iota((CH, hidden), 1) & (CH - 1)) == iota((CH, hidden), 0)).astype(F32).astype(BF)
+    level_hid = iota((1, hidden), 1) >> 6
+    total2 = jnp.zeros((rows, hidden), F32)
     bias2 = jnp.zeros((rows, 128), F32)
     for tap in range(3):
         block = jnp.zeros((rows, CH), F32)
         for field in range(fields):
-            block = jnp.where(field_row == field, w2_ref[tap].astype(F32)[field : field + 1, :], block)
+            taps = w2_ref[field].astype(F32)[tap : tap + 1] if slots_in else w2_ref[tap].astype(F32)[field : field + 1]
+            block = jnp.where(field_row == field, taps, block)
         wide = dot(block.astype(BF), spread2)
         total2 = jnp.where(level_hid == level_out + 2 * (tap - 1), wide, total2)
     o2_ref[...] = total2.astype(BF)
@@ -150,36 +148,30 @@
 
 def second_weights(w1, bias1, w2, bias2, order):
     full = lambda *shape: pl.BlockSpec(shape, lambda i: (0,) * len(shape))
-    width, rows = VARS * LV + ITEMS + 16, VARS * LV
+    width, rows = VARS * LV + ITEMS + 16, 8 * BAND
     return pl.pallas_call(
         weights_kernel,
         out_shape=(
             pltpu.HBM((HID, width), BF),
-            pltpu.HBM((rows, HID), BF),
+            pltpu.HBM((rows, 4 * CH), BF),
             pltpu.HBM((rows, 128), F32),
         ),
         grid=(1,),
         in_specs=[full(*w1.shape), full(1, CH), full(*w2.shape), full(1, ITEMS), full(1, bias2.shape[0])],
-        out_specs=(full(HID, width), full(rows, HID), full(rows, 128)),
+        out_specs=(full(HID, width), full(rows, 4 * CH), full(rows, 128)),
         compiler_params=pltpu.CompilerParams(vmem_limit_bytes=20 * 2**20),
         cost_estimate=pl.CostEstimate(flops=2 * 10**8, bytes_accessed=2 * 10**6, transcendentals=0),
         name="second_weights",
     )(hbm(w1), hbm(bias1.reshape(1, CH)), hbm(w2), hbm(order.reshape(1, ITEMS)), hbm(bias2.reshape(1, -1)))
 
 
-def hidden_layer(w1_ref, w2_ref, v_ref, h_ref):
-    block = v_ref.shape[1]
-    step, tall = 256, HID // 2
+def hidden_layer(w1_ref, v_ref, h_ref, cols):
+    tall = HID // 2
     c1, c2 = 2 * math.sqrt(2 / math.pi), 8 * 0.044715 * math.sqrt(2 / math.pi)
-    results = []
-    for col in range(0, block, step):
-        cols = slice(col, col + step)
-        for row in range(0, HID, tall):
-            y = dot(w1_ref[row : row + tall, :], v_ref[:, cols])
-            u = y * (c1 + c2 * (y * y))
-            h_ref[row : row + tall, cols] = (y + y * jnp.tanh(u)).astype(BF)
-        results.append(dot(w2_ref[...], h_ref[:, cols]))
-    return jnp.concatenate(results, axis=1)
+    for row in range(0, HID, tall):
+        y = dot(w1_ref[row : row + tall, :], v_ref[:, cols])
+        u = y * (c1 + c2 * (y * y))
+        h_ref[row : row + tall, cols] = (y + y * jnp.tanh(u)).astype(BF)
 
 
 def first_kernel(
@@ -193,10 +185,13 @@
         v_ref[VARS * LV :, :] = jnp.ones((16, block), BF)
 
     v_ref[: VARS * LV, :] = state_ref[...]
-    result = hidden_layer(w1_ref, w2_ref, v_ref, h_ref)
     bias = b2_ref[...]
-    for tile in range(block // 128):
-        o_ref[pl.ds(step * (block // 128) + tile, ITEMS, stride=TILES + 1), :] = result[:, tile * 128 : (tile + 1) * 128] + bias
+    for col in range(0, block, 256):
+        hidden_layer(w1_ref, v_ref, h_ref, slice(col, col + 256))
+        result = dot(w2_ref[...], h_ref[:, col : col + 256])
+        for half in range(2):
+            tile = step * (block // 128) + col // 128 + half
+            o_ref[pl.ds(tile, ITEMS, stride=TILES + 1), :] = result[:, half * 128 : (half + 1) * 128] + bias
 
     @pl.when(step == pl.num_programs(0) - 1)
     def _():
@@ -233,7 +228,7 @@
     )(hbm(state), hbm(w1), hbm(bias1.reshape(1, CH)), hbm(w2), hbm(order.reshape(1, ITEMS)), hbm(bias2.reshape(1, -1)))
 
 
-def second_kernel(block, state_ref, filt_ref, w1_ref, w2_ref, b2_ref, out_ref, v_ref, h_ref, f_ref):
+def second_kernel(block, state_ref, filt_ref, w1_ref, w2_ref, b2_ref, out_ref, v_ref, h_ref, f_ref, e_ref):
     step = pl.program_id(0)
     base = VARS * LV
 
@@ -247,10 +242,23 @@
     for tile in range(block // 128):
         piece = f_ref[pl.ds(step * (block // 128) + tile, ITEMS, stride=TILES + 1), :]
         v_ref[base : base + ITEMS, tile * 128 : (tile + 1) * 128] = piece.astype(BF)
-    result = hidden_layer(w1_ref, w2_ref, v_ref, h_ref)
-    bias = b2_ref[...]
-    for tile in range(block // 128):
-        out_ref[:, tile * 128 : (tile + 1) * 128] = result[:, tile * 128 : (tile + 1) * 128] + bias
+    bias = b2_ref[0:8, :]
+    for col in range(0, block, 256):
+        hidden_layer(w1_ref, v_ref, h_ref, slice(col, col + 256))
+        levels = [None] * LV
+        for group in range(LV // 4):
+            part = dot(w2_ref[...], h_ref[group * 4 * CH : (group + 1) * 4 * CH, col : col + 256])
+            for at in range(BAND):
+                level = 4 * group - 2 + at
+                if 0 <= level < LV:
+                    piece = part[8 * at : 8 * at + 8]
+                    levels[level] = piece if levels[level] is None else levels[level] + piece
+        for half in range(2):
+            lanes = slice(col + half * 128, col + half * 128 + 128)
+            for level in range(LV):
+                e_ref[half, 9 * level : 9 * level + 8, :] = levels[level][:, half * 128 : (half + 1) * 128] + bias
+            for variable in range(VARS):
+                out_ref[variable * LV : (variable + 1) * LV, lanes] = e_ref[half, pl.ds(variable, LV, stride=9), :]
 
 
 def second_conv(state, filtered, w1, w2, b2, block=1024):
@@ -264,14 +272,15 @@
             pl.BlockSpec((VARS * LV, block), lambda i: (0, i)),
             full(ITEMS, TILES, 128),
             full(HID, width),
-            full(VARS * LV, HID),
-            full(VARS * LV, 128),
+            full(8 * BAND, 4 * CH),
+            full(8 * BAND, 128),
         ],
         out_specs=pl.BlockSpec((VARS * LV, block), lambda i: (0, i)),
         scratch_shapes=[
             pltpu.VMEM((width, block), BF),
             pltpu.VMEM((HID, block), BF),
             pltpu.VMEM((ITEMS * (TILES + 1), 128), F32),
+            pltpu.VMEM((2, 9 * LV, 128), F32),
         ],
         compiler_params=pltpu.CompilerParams(vmem_limit_bytes=24 * 2**20),
         cost_estimate=pl.CostEstimate(flops=4 * 10**9, bytes_accessed=4 * 10**6, transcendentals=HID * COLUMNS),
@@ -358,7 +367,7 @@
     return pltpu.roll(x, 64, 1)
 
 
-def forward_kernel(y_ref, f_ref, g_ref, q_ref, out_ref, x0_ref, x1_ref):
+def forward_kernel(band_ref, y_ref, f_ref, g_ref, q_ref, out_ref, x0_ref, x1_ref):
     low = iota((TILES, 128), 1) < 64
     x0_ref[192:256, :] = jnp.zeros((64, NLON), BF)
     x1_ref[0:64, :] = jnp.zeros((64, NLON), BF)
@@ -373,7 +382,7 @@
             for ref, place in ((x0_ref, place0), (x1_ref, place1)):
                 ref[place[item] : place[item] + 32, lanes] = even
                 ref[place[item] + 32 : place[item] + 64, lanes] = odd
-    quad = q_ref[...]
+    quad = q_ref[pl.ds(band_ref[0], 1), :]
     cosines = lax.dot_general(f_ref[...], x0_ref[...], NT, preferred_element_type=F32)
     sines = lax.dot_general(g_ref[...], x1_ref[...], NT, preferred_element_type=F32)
     tiles = (cosines[:, :128], cosines[:, 128:] + sines[:, :128], sines[:, 128:])
@@ -383,24 +392,25 @@
             out_ref[group, :, 128 * t : 128 * t + 128] = value[group * MP : (group + 1) * MP]
 
 
-def forward_fourier(pieces, tables, quad):
+def forward_fourier(band, pieces, tables, quad):
     full = lambda *shape: pl.BlockSpec(shape, lambda i: (0,) * len(shape))
     return pl.pallas_call(
         forward_kernel,
         grid=(1,),
         out_shape=pltpu.HBM((N_LAT, MP, 384), BF),
         in_specs=[
+            pl.BlockSpec(memory_space=pltpu.SMEM),
             full(N_LON, GROUP, TILES, 128),
             pl.BlockSpec((N_LAT * MP, NLON), lambda i: (0, 0)),
             pl.BlockSpec((N_LAT * MP, NLON), lambda i: (0, 1)),
-            full(1, 384),
+            full(N_LAT, 384),
         ],
         out_specs=full(N_LAT, MP, 384),
         scratch_shapes=[pltpu.VMEM((256, NLON), BF)] * 2,
         compiler_params=pltpu.CompilerParams(vmem_limit_bytes=20 * 2**20),
         cost_estimate=pl.CostEstimate(flops=4 * 10**8, bytes_accessed=3 * 10**6, transcendentals=0),
         name="forward_fourier",
-    )(pieces, tables, tables, quad)
+    )(band, pieces, tables, tables, hbm(quad))
 
 
 def inverse_kernel(r_ref, f_ref, g_ref, out_ref):
@@ -582,6 +592,10 @@
     )(waves, coeffs, hbm(table0), hbm(table1), gain)
 
 
+def one_hot(grouped):
+    return (grouped.reshape(N_LAT * MP)[:, None] == jnp.arange(M, dtype=jnp.int32)[None, :]).astype(BF)
+
+
 def per_device(
     state, conv_in, bias_in, conv_out, bias_out, spectral_gain, mix_in, blend_bias, mix_out, mix_out_bias, level_order, wave_order
 ):
@@ -594,30 +608,28 @@
     pieces = lax.all_to_all(tendency.reshape(N_LON, GROUP, TILES, 128), "lon", 0, 0, tiled=True)
 
     grouped = jnp.pad(wave_order.reshape(N_LAT, OWNED), ((0, 0), (0, MP - OWNED)), constant_values=-1)
-    chosen = (grouped.reshape(N_LAT * MP)[:, None] == jnp.arange(M, dtype=jnp.int32)[None, :]).astype(BF)
-    tables = dot(chosen, jnp.asarray(trig[:, : 2 * NLON])).astype(BF)
+    tables = dot(one_hot(grouped), jnp.asarray(trig[:, : 2 * NLON])).astype(BF)
     owned = lax.dynamic_slice_in_dim(grouped, band, 1, 0)[0]
     waves_f = jnp.where(owned < 0, 1000, owned).astype(F32)[:, None]
     lat_rows, start = jnp.asarray(lat_rows), jnp.asarray(start)
-    band_quad = lax.dynamic_slice_in_dim(jnp.asarray(quad), band, 1, 0)[0]
     gain = jnp.broadcast_to(jnp.pad(spectral_gain, (0, 768 - M))[None], (8, 768))
     owned = jnp.maximum(owned, 0)
     table0 = legendre_table(waves_f[:MH], lat_rows, start)
     pieces, table0, tables, gain, owned = lax.optimization_barrier((pieces, table0, tables, gain, owned))
 
-    coeffs = forward_fourier(pieces, tables, band_quad)
+    coeffs = forward_fourier(band.reshape(1), pieces, tables, jnp.asarray(quad[:, 0]))
     coeffs, waves_late = lax.optimization_barrier((coeffs, waves_f[MH:]))
     coeffs = lax.all_to_all(coeffs, "lat", 0, 0, tiled=True)
     table1 = legendre_table(waves_late, lat_rows, start)
     coeffs, table1 = lax.optimization_barrier((coeffs, table1))
 
     spectrum, returned = spectral_step(owned, coeffs, table0, table1, gain)
-    returned, mix_in, blend_bias, mix_out, mix_out_bias, level_order, chosen = lax.optimization_barrier(
-        (returned, mix_in, blend_bias, mix_out, mix_out_bias, level_order, chosen)
+    returned, mix_in, blend_bias, mix_out, mix_out_bias, level_order, grouped = lax.optimization_barrier(
+        (returned, mix_in, blend_bias, mix_out, mix_out_bias, level_order, grouped)
     )
     returned = lax.all_to_all(returned, "lat", 0, 0, tiled=True)
-    m1, m2, mb = second_weights(mix_in.transpose(1, 2, 0), blend_bias, mix_out.transpose(1, 0, 2), mix_out_bias, level_order)
-    inverse_tables = dot(chosen, jnp.asarray(trig[:, 2 * NLON :])).astype(BF)
+    m1, m2, mb = second_weights(mix_in.transpose(1, 2, 0), blend_bias, mix_out, mix_out_bias, level_order)
+    inverse_tables = dot(one_hot(grouped), jnp.asarray(trig[:, 2 * NLON :])).astype(BF)
     returned, m1, m2, mb, inverse_tables = lax.optimization_barrier((returned, m1, m2, mb, inverse_tables))
     grid_values = inverse_fourier(returned.reshape(N_LAT * MP, 384), inverse_tables)
     filtered = lax.all_to_all(grid_values, "lon", 0, 0, tiled=True)

time: 87.5 us -> 86.9 us (level)
  waiting for transfers between devices: 8.12 us -> 10.9 us
  local copies, waits for them, and re-layouts: 1.74 us -> 0.54 us
  matrix products: 2.99 us -> 2.08 us
    all_to_all x1, waiting for transfers between devices: 3.34 us -> 4.57 us  [per_device(): returned = lax.all_to_all(returned, 'lat', 0, 0, tiled=True)]
    all_to_all x1, waiting for transfers between devices: 2.01 us -> 2.92 us  [per_device(): coeffs = lax.all_to_all(coeffs, 'lat', 0, 0, tiled=True)]
    dot_general x2, matrix products: 2.99 us -> 2.08 us  [dot(): return jnp.dot(a, b, preferred_element_type=F32)]
  transfers between devices with their start and end apart: 3 -> 3, of which waited for: 3 -> 3; matrix products, arithmetic and copies ran while one was open for 6% -> 3% of each run, Pallas kernels for 14% -> 14%
where the time goes in v6:
time: 86.9 us; the launch traced here: 86.3 us
  Pallas kernels  42.9 us (49%)
  starting transfers between devices  15.9 us (18%)
  blocking collectives  13.2 us (15%)
  waiting for transfers between devices  10.9 us (13%)
  matrix products  2.08 us (2%)
    all_to_all x1, blocking collectives, per_device(): filtered = lax.all_to_all(grid_values, 'lon', 0, 0, tiled=True)  13.2 us
    pallas_call x1, Pallas kernels, first_conv(): pl.pallas_call(functools.partial(first_kernel, block), grid=(COLUMNS // b...  10.2 us
    pallas_call x1, Pallas kernels, second_conv(): pl.pallas_call(functools.partial(second_kernel, block), grid=(COLUMNS //...  10 us
    pallas_call x2, Pallas kernels, legendre_table(): pl.pallas_call(table_kernel, grid=(KP // CHUNK,), out_shape=pltpu.HBM((MH...  9.79 us
    pallas_call x1, Pallas kernels, spectral_step(): pl.pallas_call(spectral_kernel, grid_spec=pltpu.PrefetchScalarGridSpec(nu...  7.13 us
    all_to_all x1, starting transfers between devices, per_device(): lax.all_to_all(tendency.reshape(N_LON, GROUP, TILES, 128), 'lon', 0, 0, t...  7.13 us
    all_to_all x1, starting transfers between devices, per_device(): coeffs = lax.all_to_all(coeffs, 'lat', 0, 0, tiled=True)  5.32 us
    all_to_all x1, waiting for transfers between devices, per_device(): returned = lax.all_to_all(returned, 'lat', 0, 0, tiled=True)  4.57 us
  transfers between devices with their start and end apart: 3, of which 3 were waited for; matrix products, arithmetic and copies ran while one was open for 3% of the time, Pallas kernels for 14%

profile of v6, /device:TPU:0, one launch (start us, length us, event | category | flops | bytes accessed | tf_op | source)
XLA Modules:
  0.0 86.3 jit_solution(8383472961408572900)
XLA Ops:
  0.7 0.0 copy-start
  0.7 10.2 %first_conv.1 = bf16[48,32,128]{2,1,0:T(8,128)(2,1)} custom-call(bf16[144,4096]{1,0:T(8,128)(2,1)} %bitcast.27, bf16[3,6,64]{2,1,0:T(8,128)(2,1)} %bitcast.29, f32[1,64]{1,0:T(1,128)} %bitcast.32, bf16[3,2,64]{2,1,0:T(2,128)(2,1)} %bitcast.31, s32[1,48]{1,0:T(1,128)} %bitcast.34, f32[1,2]{1,0:T(1,128)} %bitcast.33), custom_call_target="tpu_custom_call" | custom-call | flops 3000000000 | bytes 2000000 | tf_op jit(solution)/shard_map/first_conv/pallas_call | solution.py:204
  10.8 7.1 %all-to-all-start = ((bf16[16,3,32,128]{3,2,1,0:T(8,128)(2,1)}), bf16[16,3,32,128]{3,2,1,0:T(8,128)(2,1)S(1)}, u32[]{:S(2)}, u32[]{:S(2)}) async-start(bf16[16,3,32,128]{3,2,1,0:T(8,128)(2,1)} %bitcast.26), calls=%async_computation | async-start | bytes 786432 | tf_op jit(solution)/shard_map/all_to_all | solution.py:608
  18.0 0.1 reshape.53
  18.1 0.1 slice_bitcast_fusion
  18.2 0.1 eq.30
  18.2 0.1 copy.19.wave_ref
  18.4 4.9 %legendre_table.2.t0_ref = bf16[24,352,256]{2,1,0:T(8,128)(2,1)} custom-call(f32[24,1]{1,0:T(8,128)S(1)} %copy.19.wave_ref, f32[8,256]{1,0:T(8,128)S(1)} %copy-done, f32[1,384]{1,0:T(1,128)S(1)} %copy-done.1), custom_call_target="tpu_custom_call" | custom-call | flops 200000000 | bytes 9000000 | tf_op jit(solution)/shard_map/legendre_table/pallas_call | solution.py:352
  23.3 1.1 %convolution_convert_fusion.1.f_ref.g_ref = bf16[384,2048]{1,0:T(8,128)(2,1)S(1)} fusion(bf16[344,2048]{1,0:T(8,128)(2,1)S(1)} %copy-done.6, s32[384]{0:T(512)S(1)} %eq.30), kind=kOutput, calls=%fused_computation.1 | convolution fusion | flops 541983744 | bytes 2983424 | tf_op jit(solution)/shard_map/dot_general | solution.py:53
  24.3 3.4 %all-to-all-done.y_ref = bf16[16,3,32,128]{3,2,1,0:T(8,128)(2,1)S(1)} async-done(((bf16[16,3,32,128]{3,2,1,0:T(8,128)(2,1)}), bf16[16,3,32,128]{3,2,1,0:T(8,128)(2,1)S(1)}, u32[]{:S(2)}, u32[]{:S(2)}) %all-to-all-start) | async-done | bytes 393248 | tf_op jit(solution)/shard_map/all_to_all | solution.py:608
  27.8 2.1 %forward_fourier.1 = bf16[8,48,384]{2,1,0:T(8,128)(2,1)} custom-call(s32[1]{0:T(128)} %bitcast.9.band_ref, bf16[16,3,32,128]{3,2,1,0:T(8,128)(2,1)S(1)} %all-to-all-done.y_ref, bf16[384,2048]{1,0:T(8,128)(2,1)S(1)} %convolution_convert_fusion.1.f_ref.g_ref, bf16[384,2048]{1,0:T(8,128)(2,1)S(1)} %convolution_convert_fusion.1.f_ref.g_ref, ...), custom_call_target="tpu_custom_call" | custom-call | flops 400000000 | bytes 3000000 | tf_op jit(solution)/shard_map/forward_fourier/pallas_call | solution.py:397
  29.9 5.3 %all-to-all-start.1 = ((bf16[8,48,384]{2,1,0:T(8,128)(2,1)}), bf16[8,48,384]{2,1,0:T(8,128)(2,1)S(1)}, u32[]{:S(2)}, u32[]{:S(2)}) async-start(bf16[8,48,384]{2,1,0:T(8,128)(2,1)} %forward_fourier.1), calls=%async_computation.1 | async-start | bytes 589824 | tf_op jit(solution)/shard_map/all_to_all | solution.py:622
  35.3 0.1 copy.20.wave_ref
  35.3 4.9 %legendre_table.3.t1_ref = bf16[24,352,256]{2,1,0:T(8,128)(2,1)} custom-call(f32[24,1]{1,0:T(8,128)S(1)} %copy.20.wave_ref, f32[8,256]{1,0:T(8,128)S(1)} %copy-done, f32[1,384]{1,0:T(1,128)S(1)} %copy-done.1), custom_call_target="tpu_custom_call" | custom-call | flops 200000000 | bytes 9000000 | tf_op jit(solution)/shard_map/legendre_table/pallas_call | solution.py:352
  40.2 2.9 %all-to-all-done.1.x_ref = bf16[8,48,384]{2,1,0:T(8,128)(2,1)S(1)} async-done(((bf16[8,48,384]{2,1,0:T(8,128)(2,1)}), bf16[8,48,384]{2,1,0:T(8,128)(2,1)S(1)}, u32[]{:S(2)}, u32[]{:S(2)}) %all-to-all-start.1) | async-done | bytes 294944 | tf_op jit(solution)/shard_map/all_to_all | solution.py:622
  43.2 7.1 %spectral_step.1 = (f32[3,43,688]{2,1,0:T(8,128)}, bf16[8,48,384]{2,1,0:T(8,128)(2,1)}) custom-call(s32[48]{0:T(128)S(1)} %get-tuple-element.34.wave_ref, bf16[8,48,384]{2,1,0:T(8,128)(2,1)S(1)} %all-to-all-done.1.x_ref, bf16[24,352,256]{2,1,0:T(8,128)(2,1)} %legendre_table.2.t0_ref, bf16[24,352,256]{2,1,0:T(8,128)(2,1)} %legendre_table.3.t1_ref, ...), custom_call_target="tpu_custom_call" | custom-call | flops 4000000000 | bytes 10000000 | tf_op jit(solution)/shard_map/spectral_step/pallas_call | solution.py:564
  50.3 0.1 eq.34
  50.4 3.4 %all-to-all-start.2 = ((bf16[8,48,384]{2,1,0:T(8,128)(2,1)}), bf16[8,48,384]{2,1,0:T(8,128)(2,1)S(1)}, u32[]{:S(2)}, u32[]{:S(2)}) async-start(bf16[8,48,384]{2,1,0:T(8,128)(2,1)} %get-tuple-element.45), calls=%async_computation.2 | async-start | bytes 589824 | tf_op jit(solution)/shard_map/all_to_all | solution.py:630
  53.8 2.2 %second_weights.1 = (bf16[1536,208]{1,0:T(8,128)(2,1)}, bf16[64,256]{1,0:T(8,128)(2,1)}, f32[64,128]{1,0:T(8,128)}) custom-call(bf16[3,8,64]{2,1,0:T(8,128)(2,1)} %bitcast.30, f32[1,64]{1,0:T(1,128)} %bitcast.36, bf16[6,3,64]{2,1,0:T(4,128)(2,1)} %w2_ref, s32[1,48]{1,0:T(1,128)} %bitcast.35, f32[1,6]{1,0:T(1,128)} %bitcast.37), custom_call_target="tpu_custom_call" | custom-call | flops 200000000 | bytes 2000000 | tf_op jit(solution)/shard_map/second_weights/pallas_call | solution.py:152
  56.0 1.0 %convolution_convert_fusion.f_ref.g_ref = bf16[384,2048]{1,0:T(8,128)(2,1)S(1)} fusion(bf16[344,2048]{1,0:T(8,128)(2,1)S(1)} %copy-done.5, s32[384]{0:T(512)S(1)} %eq.34), kind=kOutput, calls=%fused_computation | convolution fusion | flops 541983744 | bytes 2983424 | tf_op jit(solution)/shard_map/dot_general | solution.py:53
  57.0 4.6 %all-to-all-done.2 = bf16[8,48,384]{2,1,0:T(8,128)(2,1)S(1)} async-done(((bf16[8,48,384]{2,1,0:T(8,128)(2,1)}), bf16[8,48,384]{2,1,0:T(8,128)(2,1)S(1)}, u32[]{:S(2)}, u32[]{:S(2)}) %all-to-all-start.2) | async-done | bytes 294944 | tf_op jit(solution)/shard_map/all_to_all | solution.py:630
  61.6 1.5 %inverse_fourier.1 = bf16[16,3,32,128]{3,2,1,0:T(8,128)(2,1)} custom-call(bf16[384,384]{1,0:T(8,128)(2,1)S(1)} %bitcast.24, bf16[384,2048]{1,0:T(8,128)(2,1)S(1)} %convolution_convert_fusion.f_ref.g_ref, bf16[384,2048]{1,0:T(8,128)(2,1)S(1)} %convolution_convert_fusion.f_ref.g_ref), custom_call_target="tpu_custom_call" | custom-call | flops 400000000 | bytes 3000000 | tf_op jit(solution)/shard_map/inverse_fourier/pallas_call | solution.py:433
  63.1 13.2 %all_to_all.20 = bf16[16,3,32,128]{3,2,1,0:T(8,128)(2,1)S(1)} all-to-all(bf16[16,3,32,128]{3,2,1,0:T(8,128)(2,1)} %inverse_fourier.1), channel_id=1, replica_groups=mesh['lat'=8,'lon'=16] {'lon'}, dimensions={0} | all-to-all | bytes 786432 | tf_op jit(solution)/shard_map/all_to_all | solution.py:635
  76.3 10.0 %second_conv.1 = f32[144,4096]{1,0:T(8,128)} custom-call(bf16[144,4096]{1,0:T(8,128)(2,1)} %bitcast.28, bf16[48,32,128]{2,1,0:T(8,128)(2,1)S(1)} %bitcast.25, bf16[1536,208]{1,0:T(8,128)(2,1)S(1)} %copy-done.2, bf16[64,256]{1,0:T(8,128)(2,1)S(1)} %copy-done.3, f32[64,128]{1,0:T(8,128)S(1)} %copy-done.4), custom_call_target="tpu_custom_call" | custom-call | flops 4000000000 | bytes 4000000 | tf_op jit(solution)/shard_map/second_conv/pallas_call | solution.py:267
  (21 shorter events, 0.1 us)
Async XLA Ops:
  0.6 17.3 %copy-start.7 = (s32[344]{0:T(512)S(1)}, s32[344]{0:T(512)}, u32[]{:S(2)}) copy-start(s32[344]{0:T(512)} %param.28) | copy-start | bytes 4132
  0.6 17.7 %copy-start.8 = (f32[344]{0:T(512)S(1)}, f32[344]{0:T(512)}, u32[]{:S(2)}) copy-start(f32[344]{0:T(512)} %param.22) | copy-start | bytes 4132
  0.7 17.7 %copy-start = (f32[8,256]{1,0:T(8,128)S(1)}, f32[8,256]{1,0:T(8,128)}, u32[]{:S(2)}) copy-start(f32[8,256]{1,0:T(8,128)} %constant.28.clone.lat_ref) | copy-start | bytes 24580
  0.7 17.7 %copy-start.1 = (f32[1,384]{1,0:T(1,128)S(1)}, f32[1,384]{1,0:T(1,128)}, u32[]{:S(2)}) copy-start(f32[1,384]{1,0:T(1,128)} %constant.29.clone.start_ref) | copy-start | bytes 4612
  10.8 16.9 %all-to-all-start = ((bf16[16,3,32,128]{3,2,1,0:T(8,128)(2,1)}), bf16[16,3,32,128]{3,2,1,0:T(8,128)(2,1)S(1)}, u32[]{:S(2)}, u32[]{:S(2)}) async-start(bf16[16,3,32,128]{3,2,1,0:T(8,128)(2,1)} %bitcast.26), calls=%async_computation | async-start | bytes 786432 | tf_op jit(solution)/shard_map/all_to_all | solution.py:608
  18.4 4.9 %copy-start.6 = (bf16[344,2048]{1,0:T(8,128)(2,1)S(1)}, bf16[344,2048]{1,0:T(8,128)(2,1)}, u32[]{:S(2)}) copy-start(bf16[344,2048]{1,0:T(8,128)(2,1)} %constant.27.clone) | copy-start | bytes 4227076
  29.9 13.2 %all-to-all-start.1 = ((bf16[8,48,384]{2,1,0:T(8,128)(2,1)}), bf16[8,48,384]{2,1,0:T(8,128)(2,1)S(1)}, u32[]{:S(2)}, u32[]{:S(2)}) async-start(bf16[8,48,384]{2,1,0:T(8,128)(2,1)} %forward_fourier.1), calls=%async_computation.1 | async-start | bytes 589824 | tf_op jit(solution)/shard_map/all_to_all | solution.py:622
  40.2 15.8 %copy-start.5 = (bf16[344,2048]{1,0:T(8,128)(2,1)S(1)}, bf16[344,2048]{1,0:T(8,128)(2,1)}, u32[]{:S(2)}) copy-start(bf16[344,2048]{1,0:T(8,128)(2,1)} %constant.31.clone) | copy-start | bytes 4227076
  50.4 11.2 %all-to-all-start.2 = ((bf16[8,48,384]{2,1,0:T(8,128)(2,1)}), bf16[8,48,384]{2,1,0:T(8,128)(2,1)S(1)}, u32[]{:S(2)}, u32[]{:S(2)}) async-start(bf16[8,48,384]{2,1,0:T(8,128)(2,1)} %get-tuple-element.45), calls=%async_computation.2 | async-start | bytes 589824 | tf_op jit(solution)/shard_map/all_to_all | solution.py:630
  61.6 14.7 %copy-start.2 = (bf16[1536,208]{1,0:T(8,128)(2,1)S(1)}, bf16[1536,208]{1,0:T(8,128)(2,1)}, u32[]{:S(2)}) copy-start(bf16[1536,208]{1,0:T(8,128)(2,1)} %get-tuple-element.57.w1_ref) | copy-start | bytes 1916932
  61.6 14.7 %copy-start.3 = (bf16[64,256]{1,0:T(8,128)(2,1)S(1)}, bf16[64,256]{1,0:T(8,128)(2,1)}, u32[]{:S(2)}) copy-start(bf16[64,256]{1,0:T(8,128)(2,1)} %get-tuple-element.58.w2_ref) | copy-start | bytes 98308
  61.6 14.7 %copy-start.4 = (f32[64,128]{1,0:T(8,128)S(1)}, f32[64,128]{1,0:T(8,128)}, u32[]{:S(2)}) copy-start(f32[64,128]{1,0:T(8,128)} %get-tuple-element.59.b2_ref) | copy-start | bytes 98308

commit v7 on v6

--- a/solution.py
+++ b/solution.py
@@ -270,10 +270,10 @@
         out_shape=pltpu.HBM((VARS * LV, COLUMNS), F32),
         in_specs=[
             pl.BlockSpec((VARS * LV, block), lambda i: (0, i)),
-            full(ITEMS, TILES, 128),
-            full(HID, width),
-            full(8 * BAND, 4 * CH),
-            full(8 * BAND, 128),
+            pl.BlockSpec(memory_space=pltpu.VMEM),
+            pl.BlockSpec(memory_space=pltpu.VMEM),
+            pl.BlockSpec(memory_space=pltpu.VMEM),
+            pl.BlockSpec(memory_space=pltpu.VMEM),
         ],
         out_specs=pl.BlockSpec((VARS * LV, block), lambda i: (0, i)),
         scratch_shapes=[
@@ -367,7 +367,7 @@
     return pltpu.roll(x, 64, 1)
 
 
-def forward_kernel(band_ref, y_ref, f_ref, g_ref, q_ref, out_ref, x0_ref, x1_ref):
+def forward_kernel(y_ref, f_ref, q_ref, out_ref, x0_ref, x1_ref):
     low = iota((TILES, 128), 1) < 64
     x0_ref[192:256, :] = jnp.zeros((64, NLON), BF)
     x1_ref[0:64, :] = jnp.zeros((64, NLON), BF)
@@ -382,9 +382,9 @@
             for ref, place in ((x0_ref, place0), (x1_ref, place1)):
                 ref[place[item] : place[item] + 32, lanes] = even
                 ref[place[item] + 32 : place[item] + 64, lanes] = odd
-    quad = q_ref[pl.ds(band_ref[0], 1), :]
-    cosines = lax.dot_general(f_ref[...], x0_ref[...], NT, preferred_element_type=F32)
-    sines = lax.dot_general(g_ref[...], x1_ref[...], NT, preferred_element_type=F32)
+    quad = q_ref[...]
+    cosines = lax.dot_general(f_ref[:, :NLON], x0_ref[...], NT, preferred_element_type=F32)
+    sines = lax.dot_general(f_ref[:, NLON:], x1_ref[...], NT, preferred_element_type=F32)
     tiles = (cosines[:, :128], cosines[:, 128:] + sines[:, :128], sines[:, 128:])
     for t, value in enumerate(tiles):
         value = (value * quad[:, 128 * t : 128 * t + 128]).astype(BF)
@@ -392,32 +392,26 @@
             out_ref[group, :, 128 * t : 128 * t + 128] = value[group * MP : (group + 1) * MP]
 
 
-def forward_fourier(band, pieces, tables, quad):
+def forward_fourier(pieces, tables, quad):
     full = lambda *shape: pl.BlockSpec(shape, lambda i: (0,) * len(shape))
     return pl.pallas_call(
         forward_kernel,
         grid=(1,),
         out_shape=pltpu.HBM((N_LAT, MP, 384), BF),
-        in_specs=[
-            pl.BlockSpec(memory_space=pltpu.SMEM),
-            full(N_LON, GROUP, TILES, 128),
-            pl.BlockSpec((N_LAT * MP, NLON), lambda i: (0, 0)),
-            pl.BlockSpec((N_LAT * MP, NLON), lambda i: (0, 1)),
-            full(N_LAT, 384),
-        ],
+        in_specs=[pl.BlockSpec(memory_space=pltpu.VMEM)] * 3,
         out_specs=full(N_LAT, MP, 384),
         scratch_shapes=[pltpu.VMEM((256, NLON), BF)] * 2,
         compiler_params=pltpu.CompilerParams(vmem_limit_bytes=20 * 2**20),
         cost_estimate=pl.CostEstimate(flops=4 * 10**8, bytes_accessed=3 * 10**6, transcendentals=0),
         name="forward_fourier",
-    )(band, pieces, tables, tables, hbm(quad))
-
-
-def inverse_kernel(r_ref, f_ref, g_ref, out_ref):
+    )(pieces, tables, quad)
+
+
+def inverse_kernel(r_ref, f_ref, out_ref):
     turned = [r_ref[:, 128 * t : 128 * t + 128].astype(F32).T.astype(BF) for t in range(3)]
     cosines = jnp.concatenate([turned[0], turned[1][:64]], axis=0)
     sines = jnp.concatenate([turned[2], turned[1][64:]], axis=0)
-    grid = dot(cosines, f_ref[...]) + dot(sines, g_ref[...])
+    grid = dot(cosines, f_ref[:, :NLON]) + dot(sines, f_ref[:, NLON:])
     low = iota((TILES, 128), 1) < 64
     for pair in range(N_LON // 2):
         for item in range(GROUP):
@@ -434,16 +428,12 @@
         inverse_kernel,
         grid=(1,),
         out_shape=pltpu.HBM((N_LON, GROUP, TILES, 128), BF),
-        in_specs=[
-            full(N_LAT * MP, 384),
-            pl.BlockSpec((N_LAT * MP, NLON), lambda i: (0, 0)),
-            pl.BlockSpec((N_LAT * MP, NLON), lambda i: (0, 1)),
-        ],
+        in_specs=[pl.BlockSpec(memory_space=pltpu.VMEM)] * 2,
         out_specs=full(N_LON, GROUP, TILES, 128),
         compiler_params=pltpu.CompilerParams(vmem_limit_bytes=20 * 2**20),
         cost_estimate=pl.CostEstimate(flops=4 * 10**8, bytes_accessed=3 * 10**6, transcendentals=0),
         name="inverse_fourier",
-    )(returned, tables, tables)
+    )(returned, tables)
 
 
 WAVES = 8
@@ -567,10 +557,10 @@
             num_scalar_prefetch=1,
             grid=(GROUPS,),
             in_specs=[
-                full(N_LAT, MP, 384),
+                pl.BlockSpec(memory_space=pltpu.VMEM),
                 pl.BlockSpec(memory_space=pltpu.HBM),
                 pl.BlockSpec(memory_space=pltpu.HBM),
-                full(8, 768),
+                pl.BlockSpec(memory_space=pltpu.VMEM),
             ],
             out_specs=(full(GROUP, OWNED, 2 * M), full(N_LAT, MP, 384)),
             scratch_shapes=[
@@ -612,12 +602,15 @@
     owned = lax.dynamic_slice_in_dim(grouped, band, 1, 0)[0]
     waves_f = jnp.where(owned < 0, 1000, owned).astype(F32)[:, None]
     lat_rows, start = jnp.asarray(lat_rows), jnp.asarray(start)
+    band_quad = lax.dynamic_slice_in_dim(jnp.asarray(quad), band, 1, 0)[0]
     gain = jnp.broadcast_to(jnp.pad(spectral_gain, (0, 768 - M))[None], (8, 768))
     owned = jnp.maximum(owned, 0)
     table0 = legendre_table(waves_f[:MH], lat_rows, start)
-    pieces, table0, tables, gain, owned = lax.optimization_barrier((pieces, table0, tables, gain, owned))
-
-    coeffs = forward_fourier(band.reshape(1), pieces, tables, jnp.asarray(quad[:, 0]))
+    pieces, table0, tables, gain, owned, band_quad = lax.optimization_barrier(
+        (pieces, table0, tables, gain, owned, band_quad)
+    )
+
+    coeffs = forward_fourier(pieces, tables, band_quad)
     coeffs, waves_late = lax.optimization_barrier((coeffs, waves_f[MH:]))
     coeffs = lax.all_to_all(coeffs, "lat", 0, 0, tiled=True)
     table1 = legendre_table(waves_late, lat_rows, start)

time: 86.9 us -> 86.9 us (level)
  waiting for transfers between devices: 10.9 us -> 8.89 us
  matrix products: 2.08 us -> 3.4 us
    all_to_all x1, waiting for transfers between devices: 4.57 us -> 3.2 us  [per_device(): returned = lax.all_to_all(returned, 'lat', 0, 0, tiled=True)]
    dot_general x2, matrix products: 2.08 us -> 3.4 us  [dot(): return jnp.dot(a, b, preferred_element_type=F32)]
  transfers between devices with their start and end apart: 3 -> 3, of which waited for: 3 -> 3; matrix products, arithmetic and copies ran while one was open for 3% -> 5% of each run, Pallas kernels for 14% -> 14%
where the time goes in v7:
time: 86.9 us; the launch traced here: 86.2 us
  Pallas kernels  42.2 us (49%)
  starting transfers between devices  15.9 us (18%)
  blocking collectives  13.8 us (16%)
  waiting for transfers between devices  8.89 us (10%)
  matrix products  3.4 us (4%)
  local copies, waits for them, and re-layouts  1.21 us (1%)
    all_to_all x1, blocking collectives, per_device(): filtered = lax.all_to_all(grid_values, 'lon', 0, 0, tiled=True)  13.8 us
    pallas_call x1, Pallas kernels, first_conv(): pl.pallas_call(functools.partial(first_kernel, block), grid=(COLUMNS // b...  10.2 us
    pallas_call x1, Pallas kernels, second_conv(): pl.pallas_call(functools.partial(second_kernel, block), grid=(COLUMNS //...  10 us
    pallas_call x2, Pallas kernels, legendre_table(): pl.pallas_call(table_kernel, grid=(KP // CHUNK,), out_shape=pltpu.HBM((MH...  9.81 us
    pallas_call x1, Pallas kernels, spectral_step(): pl.pallas_call(spectral_kernel, grid_spec=pltpu.PrefetchScalarGridSpec(nu...  7.13 us
    all_to_all x1, starting transfers between devices, per_device(): lax.all_to_all(tendency.reshape(N_LON, GROUP, TILES, 128), 'lon', 0, 0, t...  7.13 us
    all_to_all x1, starting transfers between devices, per_device(): coeffs = lax.all_to_all(coeffs, 'lat', 0, 0, tiled=True)  5.32 us
    all_to_all x1, starting transfers between devices, per_device(): returned = lax.all_to_all(returned, 'lat', 0, 0, tiled=True)  3.42 us
  transfers between devices with their start and end apart: 3, of which 3 were waited for; matrix products, arithmetic and copies ran while one was open for 5% of the time, Pallas kernels for 14%

profile of v7, /device:TPU:0, one launch (start us, length us, event | category | flops | bytes accessed | tf_op | source)
XLA Modules:
  0.0 86.2 jit_solution(16366553686636135236)
XLA Ops:
  0.7 10.2 %first_conv.1 = bf16[48,32,128]{2,1,0:T(8,128)(2,1)} custom-call(bf16[144,4096]{1,0:T(8,128)(2,1)} %bitcast.28, bf16[3,6,64]{2,1,0:T(8,128)(2,1)} %bitcast.30, f32[1,64]{1,0:T(1,128)} %bitcast.33, bf16[3,2,64]{2,1,0:T(2,128)(2,1)} %bitcast.32, s32[1,48]{1,0:T(1,128)} %bitcast.35, f32[1,2]{1,0:T(1,128)} %bitcast.34), custom_call_target="tpu_custom_call" | custom-call | flops 3000000000 | bytes 2000000 | tf_op jit(solution)/shard_map/first_conv/pallas_call | solution.py:204
  10.8 7.1 %all-to-all-start = ((bf16[16,3,32,128]{3,2,1,0:T(8,128)(2,1)}), bf16[16,3,32,128]{3,2,1,0:T(8,128)(2,1)S(1)}, u32[]{:S(2)}, u32[]{:S(2)}) async-start(bf16[16,3,32,128]{3,2,1,0:T(8,128)(2,1)} %bitcast.27), calls=%async_computation | async-start | bytes 786432 | tf_op jit(solution)/shard_map/all_to_all | solution.py:598
  18.0 0.1 reshape.50
  18.1 0.1 slice_bitcast_fusion
  18.2 0.1 eq.30
  18.2 0.1 copy.19.wave_ref
  18.4 4.9 %legendre_table.2.t0_ref = bf16[24,352,256]{2,1,0:T(8,128)(2,1)} custom-call(f32[24,1]{1,0:T(8,128)S(1)} %copy.19.wave_ref, f32[8,256]{1,0:T(8,128)S(1)} %copy-done, f32[1,384]{1,0:T(1,128)S(1)} %copy-done.1), custom_call_target="tpu_custom_call" | custom-call | flops 200000000 | bytes 9000000 | tf_op jit(solution)/shard_map/legendre_table/pallas_call | solution.py:352
  23.3 0.7 dynamic-slice_bitcast_fusion.q_ref
  23.9 1.0 %convolution_convert_fusion.1.f_ref = bf16[384,2048]{1,0:T(8,128)(2,1)S(1)} fusion(bf16[344,2048]{1,0:T(8,128)(2,1)S(1)} %copy-done.5, s32[384]{0:T(512)S(1)} %eq.30), kind=kOutput, calls=%fused_computation.1 | convolution fusion | flops 541983744 | bytes 2983424 | tf_op jit(solution)/shard_map/dot_general | solution.py:53
  25.0 2.8 %all-to-all-done.y_ref = bf16[16,3,32,128]{3,2,1,0:T(8,128)(2,1)S(1)} async-done(((bf16[16,3,32,128]{3,2,1,0:T(8,128)(2,1)}), bf16[16,3,32,128]{3,2,1,0:T(8,128)(2,1)S(1)}, u32[]{:S(2)}, u32[]{:S(2)}) %all-to-all-start) | async-done | bytes 393248 | tf_op jit(solution)/shard_map/all_to_all | solution.py:598
  27.8 1.4 %forward_fourier.1 = bf16[8,48,384]{2,1,0:T(8,128)(2,1)} custom-call(bf16[16,3,32,128]{3,2,1,0:T(8,128)(2,1)S(1)} %all-to-all-done.y_ref, bf16[384,2048]{1,0:T(8,128)(2,1)S(1)} %convolution_convert_fusion.1.f_ref, f32[1,384]{1,0:T(1,128)S(1)} %dynamic-slice_bitcast_fusion.q_ref), custom_call_target="tpu_custom_call" | custom-call | flops 400000000 | bytes 3000000 | tf_op jit(solution)/shard_map/forward_fourier/pallas_call | solution.py:397
  29.2 5.3 %all-to-all-start.1 = ((bf16[8,48,384]{2,1,0:T(8,128)(2,1)}), bf16[8,48,384]{2,1,0:T(8,128)(2,1)S(1)}, u32[]{:S(2)}, u32[]{:S(2)}) async-start(bf16[8,48,384]{2,1,0:T(8,128)(2,1)} %forward_fourier.1), calls=%async_computation.1 | async-start | bytes 589824 | tf_op jit(solution)/shard_map/all_to_all | solution.py:615
  34.5 0.1 copy.20.wave_ref
  34.6 4.9 %legendre_table.3.t1_ref = bf16[24,352,256]{2,1,0:T(8,128)(2,1)} custom-call(f32[24,1]{1,0:T(8,128)S(1)} %copy.20.wave_ref, f32[8,256]{1,0:T(8,128)S(1)} %copy-done, f32[1,384]{1,0:T(1,128)S(1)} %copy-done.1), custom_call_target="tpu_custom_call" | custom-call | flops 200000000 | bytes 9000000 | tf_op jit(solution)/shard_map/legendre_table/pallas_call | solution.py:352
  39.6 2.9 %all-to-all-done.1.x_ref = bf16[8,48,384]{2,1,0:T(8,128)(2,1)S(1)} async-done(((bf16[8,48,384]{2,1,0:T(8,128)(2,1)}), bf16[8,48,384]{2,1,0:T(8,128)(2,1)S(1)}, u32[]{:S(2)}, u32[]{:S(2)}) %all-to-all-start.1) | async-done | bytes 294944 | tf_op jit(solution)/shard_map/all_to_all | solution.py:615
  42.4 7.1 %spectral_step.1 = (f32[3,43,688]{2,1,0:T(8,128)}, bf16[8,48,384]{2,1,0:T(8,128)(2,1)}) custom-call(s32[48]{0:T(128)S(1)} %get-tuple-element.35.wave_ref, bf16[8,48,384]{2,1,0:T(8,128)(2,1)S(1)} %all-to-all-done.1.x_ref, bf16[24,352,256]{2,1,0:T(8,128)(2,1)} %legendre_table.2.t0_ref, bf16[24,352,256]{2,1,0:T(8,128)(2,1)} %legendre_table.3.t1_ref, ...), custom_call_target="tpu_custom_call" | custom-call | flops 4000000000 | bytes 10000000 | tf_op jit(solution)/shard_map/spectral_step/pallas_call | solution.py:554
  49.6 0.1 eq.34
  49.7 3.4 %all-to-all-start.2 = ((bf16[8,48,384]{2,1,0:T(8,128)(2,1)}), bf16[8,48,384]{2,1,0:T(8,128)(2,1)S(1)}, u32[]{:S(2)}, u32[]{:S(2)}) async-start(bf16[8,48,384]{2,1,0:T(8,128)(2,1)} %get-tuple-element.47), calls=%async_computation.2 | async-start | bytes 589824 | tf_op jit(solution)/shard_map/all_to_all | solution.py:623
  53.1 2.2 %second_weights.1 = (bf16[1536,208]{1,0:T(8,128)(2,1)}, bf16[64,256]{1,0:T(8,128)(2,1)}, f32[64,128]{1,0:T(8,128)}) custom-call(bf16[3,8,64]{2,1,0:T(8,128)(2,1)} %bitcast.31, f32[1,64]{1,0:T(1,128)} %bitcast.37, bf16[6,3,64]{2,1,0:T(4,128)(2,1)} %w2_ref, s32[1,48]{1,0:T(1,128)} %bitcast.36, f32[1,6]{1,0:T(1,128)} %bitcast.38), custom_call_target="tpu_custom_call" | custom-call | flops 200000000 | bytes 2000000 | tf_op jit(solution)/shard_map/second_weights/pallas_call | solution.py:152
  55.3 2.4 %convolution_convert_fusion.f_ref = bf16[384,2048]{1,0:T(8,128)(2,1)S(1)} fusion(bf16[344,2048]{1,0:T(8,128)(2,1)} %constant.31.clone, s32[384]{0:T(512)S(1)} %eq.34), kind=kOutput, calls=%fused_computation | convolution fusion | flops 541983744 | bytes 2983424 | tf_op jit(solution)/shard_map/dot_general | solution.py:53
  57.7 3.2 %all-to-all-done.2 = bf16[8,48,384]{2,1,0:T(8,128)(2,1)S(1)} async-done(((bf16[8,48,384]{2,1,0:T(8,128)(2,1)}), bf16[8,48,384]{2,1,0:T(8,128)(2,1)S(1)}, u32[]{:S(2)}, u32[]{:S(2)}) %all-to-all-start.2) | async-done | bytes 294944 | tf_op jit(solution)/shard_map/all_to_all | solution.py:623
  60.9 1.5 %inverse_fourier.1 = bf16[16,3,32,128]{3,2,1,0:T(8,128)(2,1)} custom-call(bf16[384,384]{1,0:T(8,128)(2,1)S(1)} %bitcast.25, bf16[384,2048]{1,0:T(8,128)(2,1)S(1)} %convolution_convert_fusion.f_ref), custom_call_target="tpu_custom_call" | custom-call | flops 400000000 | bytes 3000000 | tf_op jit(solution)/shard_map/inverse_fourier/pallas_call | solution.py:427
  62.4 13.8 %all_to_all.20 = bf16[16,3,32,128]{3,2,1,0:T(8,128)(2,1)S(1)} all-to-all(bf16[16,3,32,128]{3,2,1,0:T(8,128)(2,1)} %inverse_fourier.1), channel_id=1, replica_groups=mesh['lat'=8,'lon'=16] {'lon'}, dimensions={0} | all-to-all | bytes 786432 | tf_op jit(solution)/shard_map/all_to_all | solution.py:628
  76.2 10.0 %second_conv.1 = f32[144,4096]{1,0:T(8,128)} custom-call(bf16[144,4096]{1,0:T(8,128)(2,1)} %bitcast.29, bf16[48,32,128]{2,1,0:T(8,128)(2,1)S(1)} %bitcast.26, bf16[1536,208]{1,0:T(8,128)(2,1)S(1)} %copy-done.2, bf16[64,256]{1,0:T(8,128)(2,1)S(1)} %copy-done.3, f32[64,128]{1,0:T(8,128)S(1)} %copy-done.4), custom_call_target="tpu_custom_call" | custom-call | flops 4000000000 | bytes 4000000 | tf_op jit(solution)/shard_map/second_conv/pallas_call | solution.py:267
  (20 shorter events, 0.1 us)
Async XLA Ops:
  0.6 17.3 %copy-start.6 = (s32[344]{0:T(512)S(1)}, s32[344]{0:T(512)}, u32[]{:S(2)}) copy-start(s32[344]{0:T(512)} %param.28) | copy-start | bytes 4132
  0.6 17.7 %copy-start.7 = (f32[344]{0:T(512)S(1)}, f32[344]{0:T(512)}, u32[]{:S(2)}) copy-start(f32[344]{0:T(512)} %param.22) | copy-start | bytes 4132
  0.7 17.7 %copy-start = (f32[8,256]{1,0:T(8,128)S(1)}, f32[8,256]{1,0:T(8,128)}, u32[]{:S(2)}) copy-start(f32[8,256]{1,0:T(8,128)} %constant.28.clone.lat_ref) | copy-start | bytes 24580
  0.7 17.7 %copy-start.1 = (f32[1,384]{1,0:T(1,128)S(1)}, f32[1,384]{1,0:T(1,128)}, u32[]{:S(2)}) copy-start(f32[1,384]{1,0:T(1,128)} %constant.29.clone.start_ref) | copy-start | bytes 4612
  10.8 16.9 %all-to-all-start = ((bf16[16,3,32,128]{3,2,1,0:T(8,128)(2,1)}), bf16[16,3,32,128]{3,2,1,0:T(8,128)(2,1)S(1)}, u32[]{:S(2)}, u32[]{:S(2)}) async-start(bf16[16,3,32,128]{3,2,1,0:T(8,128)(2,1)} %bitcast.27), calls=%async_computation | async-start | bytes 786432 | tf_op jit(solution)/shard_map/all_to_all | solution.py:598
  18.4 5.6 %copy-start.5 = (bf16[344,2048]{1,0:T(8,128)(2,1)S(1)}, bf16[344,2048]{1,0:T(8,128)(2,1)}, u32[]{:S(2)}) copy-start(bf16[344,2048]{1,0:T(8,128)(2,1)} %constant.27.clone) | copy-start | bytes 4227076
  29.2 13.2 %all-to-all-start.1 = ((bf16[8,48,384]{2,1,0:T(8,128)(2,1)}), bf16[8,48,384]{2,1,0:T(8,128)(2,1)S(1)}, u32[]{:S(2)}, u32[]{:S(2)}) async-start(bf16[8,48,384]{2,1,0:T(8,128)(2,1)} %forward_fourier.1), calls=%async_computation.1 | async-start | bytes 589824 | tf_op jit(solution)/shard_map/all_to_all | solution.py:615
  49.7 11.2 %all-to-all-start.2 = ((bf16[8,48,384]{2,1,0:T(8,128)(2,1)}), bf16[8,48,384]{2,1,0:T(8,128)(2,1)S(1)}, u32[]{:S(2)}, u32[]{:S(2)}) async-start(bf16[8,48,384]{2,1,0:T(8,128)(2,1)} %get-tuple-element.47), calls=%async_computation.2 | async-start | bytes 589824 | tf_op jit(solution)/shard_map/all_to_all | solution.py:623
  57.7 18.5 %copy-start.2 = (bf16[1536,208]{1,0:T(8,128)(2,1)S(1)}, bf16[1536,208]{1,0:T(8,128)(2,1)}, u32[]{:S(2)}) copy-start(bf16[1536,208]{1,0:T(8,128)(2,1)} %get-tuple-element.59.w1_ref) | copy-start | bytes 1916932
  57.7 18.5 %copy-start.3 = (bf16[64,256]{1,0:T(8,128)(2,1)S(1)}, bf16[64,256]{1,0:T(8,128)(2,1)}, u32[]{:S(2)}) copy-start(bf16[64,256]{1,0:T(8,128)(2,1)} %get-tuple-element.60.w2_ref) | copy-start | bytes 98308
  57.7 18.5 %copy-start.4 = (f32[64,128]{1,0:T(8,128)S(1)}, f32[64,128]{1,0:T(8,128)}, u32[]{:S(2)}) copy-start(f32[64,128]{1,0:T(8,128)} %get-tuple-element.61.b2_ref) | copy-start | bytes 98308

commit v8 on v7

--- a/solution.py
+++ b/solution.py
@@ -199,7 +199,7 @@
             out_ref[item] = o_ref[item * (TILES + 1) : item * (TILES + 1) + TILES, :].astype(BF)
 
 
-def first_conv(state, w1, bias1, w2, bias2, order, block=1024):
+def first_conv(state, w1, bias1, w2, bias2, order, block=COLUMNS):
     full = lambda *shape: pl.BlockSpec(shape, lambda i: (0,) * len(shape))
     return pl.pallas_call(
         functools.partial(first_kernel, block),
@@ -222,7 +222,7 @@
             pltpu.VMEM((HID, block), BF),
             pltpu.VMEM((ITEMS * (TILES + 1), 128), F32),
         ],
-        compiler_params=pltpu.CompilerParams(vmem_limit_bytes=24 * 2**20),
+        compiler_params=pltpu.CompilerParams(vmem_limit_bytes=40 * 2**20),
         cost_estimate=pl.CostEstimate(flops=3 * 10**9, bytes_accessed=2 * 10**6, transcendentals=HID * COLUMNS),
         name="first_conv",
     )(hbm(state), hbm(w1), hbm(bias1.reshape(1, CH)), hbm(w2), hbm(order.reshape(1, ITEMS)), hbm(bias2.reshape(1, -1)))
@@ -261,7 +261,7 @@
                 out_ref[variable * LV : (variable + 1) * LV, lanes] = e_ref[half, pl.ds(variable, LV, stride=9), :]
 
 
-def second_conv(state, filtered, w1, w2, b2, block=1024):
+def second_conv(state, filtered, w1, w2, b2, block=2048):
     full = lambda *shape: pl.BlockSpec(shape, lambda i: (0,) * len(shape))
     width = VARS * LV + ITEMS + 16
     return pl.pallas_call(
@@ -282,7 +282,7 @@
             pltpu.VMEM((ITEMS * (TILES + 1), 128), F32),
             pltpu.VMEM((2, 9 * LV, 128), F32),
         ],
-        compiler_params=pltpu.CompilerParams(vmem_limit_bytes=24 * 2**20),
+        compiler_params=pltpu.CompilerParams(vmem_limit_bytes=40 * 2**20),
         cost_estimate=pl.CostEstimate(flops=4 * 10**9, bytes_accessed=4 * 10**6, transcendentals=HID * COLUMNS),
         name="second_conv",
     )(hbm(state), filtered, w1, w2, b2)
@@ -382,7 +382,7 @@
             for ref, place in ((x0_ref, place0), (x1_ref, place1)):
                 ref[place[item] : place[item] + 32, lanes] = even
                 ref[place[item] + 32 : place[item] + 64, lanes] = odd
-    quad = q_ref[...]
+    quad = q_ref[pl.ds(lax.axis_index("lat"), 1), :]
     cosines = lax.dot_general(f_ref[:, :NLON], x0_ref[...], NT, preferred_element_type=F32)
     sines = lax.dot_general(f_ref[:, NLON:], x1_ref[...], NT, preferred_element_type=F32)
     tiles = (cosines[:, :128], cosines[:, 128:] + sines[:, :128], sines[:, 128:])
@@ -602,7 +602,7 @@
     owned = lax.dynamic_slice_in_dim(grouped, band, 1, 0)[0]
     waves_f = jnp.where(owned < 0, 1000, owned).astype(F32)[:, None]
     lat_rows, start = jnp.asarray(lat_rows), jnp.asarray(start)
-    band_quad = lax.dynamic_slice_in_dim(jnp.asarray(quad), band, 1, 0)[0]
+    band_quad = jnp.asarray(quad[:, 0])
     gain = jnp.broadcast_to(jnp.pad(spectral_gain, (0, 768 - M))[None], (8, 768))
     owned = jnp.maximum(owned, 0)
     table0 = legendre_table(waves_f[:MH], lat_rows, start)

time: 86.9 us -> 85.2 us (0.980)
  Pallas kernels: 42.2 us -> 41.2 us
where the time goes in v8:
time: 85.2 us; the launch traced here: 84.6 us
  Pallas kernels  41.2 us (48%)
  starting transfers between devices  15.8 us (19%)
  blocking collectives  13.2 us (15%)
  waiting for transfers between devices  9.59 us (11%)
  matrix products  3.4 us (4%)
    all_to_all x1, blocking collectives, per_device(): filtered = lax.all_to_all(grid_values, 'lon', 0, 0, tiled=True)  13.2 us
    pallas_call x2, Pallas kernels, legendre_table(): pl.pallas_call(table_kernel, grid=(KP // CHUNK,), out_shape=pltpu.HBM((MH...  9.79 us
    pallas_call x1, Pallas kernels, second_conv(): pl.pallas_call(functools.partial(second_kernel, block), grid=(COLUMNS //...  9.74 us
    pallas_call x1, Pallas kernels, first_conv(): pl.pallas_call(functools.partial(first_kernel, block), grid=(COLUMNS // b...  9.44 us
    pallas_call x1, Pallas kernels, spectral_step(): pl.pallas_call(spectral_kernel, grid_spec=pltpu.PrefetchScalarGridSpec(nu...  7.13 us
    all_to_all x1, starting transfers between devices, per_device(): lax.all_to_all(tendency.reshape(N_LON, GROUP, TILES, 128), 'lon', 0, 0, t...  7.11 us
    all_to_all x1, starting transfers between devices, per_device(): coeffs = lax.all_to_all(coeffs, 'lat', 0, 0, tiled=True)  5.31 us
    all_to_all x1, waiting for transfers between devices, per_device(): lax.all_to_all(tendency.reshape(N_LON, GROUP, TILES, 128), 'lon', 0, 0, t...  3.48 us
  transfers between devices with their start and end apart: 3, of which 3 were waited for; matrix products, arithmetic and copies ran while one was open for 5% of the time, Pallas kernels for 14%

profile of v8, /device:TPU:0, one launch (start us, length us, event | category | flops | bytes accessed | tf_op | source)
XLA Modules:
  0.0 84.6 jit_solution(16199215683622392342)
XLA Ops:
  0.7 0.0 copy-start
  0.7 9.4 %first_conv.1 = bf16[48,32,128]{2,1,0:T(8,128)(2,1)} custom-call(bf16[144,4096]{1,0:T(8,128)(2,1)} %bitcast.26, bf16[3,6,64]{2,1,0:T(8,128)(2,1)} %bitcast.28, f32[1,64]{1,0:T(1,128)} %bitcast.31, bf16[3,2,64]{2,1,0:T(2,128)(2,1)} %bitcast.30, s32[1,48]{1,0:T(1,128)} %bitcast.33, f32[1,2]{1,0:T(1,128)} %bitcast.32), custom_call_target="tpu_custom_call" | custom-call | flops 3000000000 | bytes 2000000 | tf_op jit(solution)/shard_map/first_conv/pallas_call | solution.py:204
  10.1 7.1 %all-to-all-start = ((bf16[16,3,32,128]{3,2,1,0:T(8,128)(2,1)}), bf16[16,3,32,128]{3,2,1,0:T(8,128)(2,1)S(1)}, u32[]{:S(2)}, u32[]{:S(2)}) async-start(bf16[16,3,32,128]{3,2,1,0:T(8,128)(2,1)} %bitcast.25), calls=%async_computation | async-start | bytes 786432 | tf_op jit(solution)/shard_map/all_to_all | solution.py:598
  17.3 0.1 reshape.50
  17.3 0.1 slice_bitcast_fusion
  17.4 0.1 eq.30
  17.5 0.1 copy.19.wave_ref
  17.6 4.9 %legendre_table.2.t0_ref = bf16[24,352,256]{2,1,0:T(8,128)(2,1)} custom-call(f32[24,1]{1,0:T(8,128)S(1)} %copy.19.wave_ref, f32[8,256]{1,0:T(8,128)S(1)} %copy-done, f32[1,384]{1,0:T(1,128)S(1)} %copy-done.2), custom_call_target="tpu_custom_call" | custom-call | flops 200000000 | bytes 9000000 | tf_op jit(solution)/shard_map/legendre_table/pallas_call | solution.py:352
  22.6 1.0 %convolution_convert_fusion.1.f_ref = bf16[384,2048]{1,0:T(8,128)(2,1)S(1)} fusion(bf16[344,2048]{1,0:T(8,128)(2,1)S(1)} %copy-done.6, s32[384]{0:T(512)S(1)} %eq.30), kind=kOutput, calls=%fused_computation.1 | convolution fusion | flops 541983744 | bytes 2983424 | tf_op jit(solution)/shard_map/dot_general | solution.py:53
  23.6 3.5 %all-to-all-done.y_ref = bf16[16,3,32,128]{3,2,1,0:T(8,128)(2,1)S(1)} async-done(((bf16[16,3,32,128]{3,2,1,0:T(8,128)(2,1)}), bf16[16,3,32,128]{3,2,1,0:T(8,128)(2,1)S(1)}, u32[]{:S(2)}, u32[]{:S(2)}) %all-to-all-start) | async-done | bytes 393248 | tf_op jit(solution)/shard_map/all_to_all | solution.py:598
  27.1 1.5 %forward_fourier.1 = bf16[8,48,384]{2,1,0:T(8,128)(2,1)} custom-call(bf16[16,3,32,128]{3,2,1,0:T(8,128)(2,1)S(1)} %all-to-all-done.y_ref, bf16[384,2048]{1,0:T(8,128)(2,1)S(1)} %convolution_convert_fusion.1.f_ref, f32[8,384]{1,0:T(8,128)S(1)} %copy-done.1), custom_call_target="tpu_custom_call" | custom-call | flops 400000000 | bytes 3000000 | tf_op jit(solution)/shard_map/forward_fourier/pallas_call | solution.py:397
  28.5 5.3 %all-to-all-start.1 = ((bf16[8,48,384]{2,1,0:T(8,128)(2,1)}), bf16[8,48,384]{2,1,0:T(8,128)(2,1)S(1)}, u32[]{:S(2)}, u32[]{:S(2)}) async-start(bf16[8,48,384]{2,1,0:T(8,128)(2,1)} %forward_fourier.1), calls=%async_computation.1 | async-start | bytes 589824 | tf_op jit(solution)/shard_map/all_to_all | solution.py:615
  33.8 0.1 copy.20.wave_ref
  33.9 4.9 %legendre_table.3.t1_ref = bf16[24,352,256]{2,1,0:T(8,128)(2,1)} custom-call(f32[24,1]{1,0:T(8,128)S(1)} %copy.20.wave_ref, f32[8,256]{1,0:T(8,128)S(1)} %copy-done, f32[1,384]{1,0:T(1,128)S(1)} %copy-done.2), custom_call_target="tpu_custom_call" | custom-call | flops 200000000 | bytes 9000000 | tf_op jit(solution)/shard_map/legendre_table/pallas_call | solution.py:352
  38.8 2.9 %all-to-all-done.1.x_ref = bf16[8,48,384]{2,1,0:T(8,128)(2,1)S(1)} async-done(((bf16[8,48,384]{2,1,0:T(8,128)(2,1)}), bf16[8,48,384]{2,1,0:T(8,128)(2,1)S(1)}, u32[]{:S(2)}, u32[]{:S(2)}) %all-to-all-start.1) | async-done | bytes 294944 | tf_op jit(solution)/shard_map/all_to_all | solution.py:615
  41.7 7.1 %spectral_step.1 = (f32[3,43,688]{2,1,0:T(8,128)}, bf16[8,48,384]{2,1,0:T(8,128)(2,1)}) custom-call(s32[48]{0:T(128)S(1)} %get-tuple-element.35.wave_ref, bf16[8,48,384]{2,1,0:T(8,128)(2,1)S(1)} %all-to-all-done.1.x_ref, bf16[24,352,256]{2,1,0:T(8,128)(2,1)} %legendre_table.2.t0_ref, bf16[24,352,256]{2,1,0:T(8,128)(2,1)} %legendre_table.3.t1_ref, ...), custom_call_target="tpu_custom_call" | custom-call | flops 4000000000 | bytes 10000000 | tf_op jit(solution)/shard_map/spectral_step/pallas_call | solution.py:554
  48.9 0.1 eq.34
  48.9 3.4 %all-to-all-start.2 = ((bf16[8,48,384]{2,1,0:T(8,128)(2,1)}), bf16[8,48,384]{2,1,0:T(8,128)(2,1)S(1)}, u32[]{:S(2)}, u32[]{:S(2)}) async-start(bf16[8,48,384]{2,1,0:T(8,128)(2,1)} %get-tuple-element.47), calls=%async_computation.2 | async-start | bytes 589824 | tf_op jit(solution)/shard_map/all_to_all | solution.py:623
  52.4 2.2 %second_weights.1 = (bf16[1536,208]{1,0:T(8,128)(2,1)}, bf16[64,256]{1,0:T(8,128)(2,1)}, f32[64,128]{1,0:T(8,128)}) custom-call(bf16[3,8,64]{2,1,0:T(8,128)(2,1)} %bitcast.29, f32[1,64]{1,0:T(1,128)} %bitcast.35, bf16[6,3,64]{2,1,0:T(4,128)(2,1)} %w2_ref, s32[1,48]{1,0:T(1,128)} %bitcast.34, f32[1,6]{1,0:T(1,128)} %bitcast.36), custom_call_target="tpu_custom_call" | custom-call | flops 200000000 | bytes 2000000 | tf_op jit(solution)/shard_map/second_weights/pallas_call | solution.py:152
  54.6 2.4 %convolution_convert_fusion.f_ref = bf16[384,2048]{1,0:T(8,128)(2,1)S(1)} fusion(bf16[344,2048]{1,0:T(8,128)(2,1)} %constant.31.clone, s32[384]{0:T(512)S(1)} %eq.34), kind=kOutput, calls=%fused_computation | convolution fusion | flops 541983744 | bytes 2983424 | tf_op jit(solution)/shard_map/dot_general | solution.py:53
  57.0 3.2 %all-to-all-done.2 = bf16[8,48,384]{2,1,0:T(8,128)(2,1)S(1)} async-done(((bf16[8,48,384]{2,1,0:T(8,128)(2,1)}), bf16[8,48,384]{2,1,0:T(8,128)(2,1)S(1)}, u32[]{:S(2)}, u32[]{:S(2)}) %all-to-all-start.2) | async-done | bytes 294944 | tf_op jit(solution)/shard_map/all_to_all | solution.py:623
  60.2 1.5 %inverse_fourier.1 = bf16[16,3,32,128]{3,2,1,0:T(8,128)(2,1)} custom-call(bf16[384,384]{1,0:T(8,128)(2,1)S(1)} %bitcast.23, bf16[384,2048]{1,0:T(8,128)(2,1)S(1)} %convolution_convert_fusion.f_ref), custom_call_target="tpu_custom_call" | custom-call | flops 400000000 | bytes 3000000 | tf_op jit(solution)/shard_map/inverse_fourier/pallas_call | solution.py:427
  61.6 13.2 %all_to_all.20 = bf16[16,3,32,128]{3,2,1,0:T(8,128)(2,1)S(1)} all-to-all(bf16[16,3,32,128]{3,2,1,0:T(8,128)(2,1)} %inverse_fourier.1), channel_id=1, replica_groups=mesh['lat'=8,'lon'=16] {'lon'}, dimensions={0} | all-to-all | bytes 786432 | tf_op jit(solution)/shard_map/all_to_all | solution.py:628
  74.8 9.7 %second_conv.1 = f32[144,4096]{1,0:T(8,128)} custom-call(bf16[144,4096]{1,0:T(8,128)(2,1)} %bitcast.27, bf16[48,32,128]{2,1,0:T(8,128)(2,1)S(1)} %bitcast.24, bf16[1536,208]{1,0:T(8,128)(2,1)S(1)} %copy-done.3, bf16[64,256]{1,0:T(8,128)(2,1)S(1)} %copy-done.4, f32[64,128]{1,0:T(8,128)S(1)} %copy-done.5), custom_call_target="tpu_custom_call" | custom-call | flops 4000000000 | bytes 4000000 | tf_op jit(solution)/shard_map/second_conv/pallas_call | solution.py:267
  (21 shorter events, 0.1 us)
Async XLA Ops:
  0.6 16.6 %copy-start.7 = (s32[344]{0:T(512)S(1)}, s32[344]{0:T(512)}, u32[]{:S(2)}) copy-start(s32[344]{0:T(512)} %param.28) | copy-start | bytes 4132
  0.6 17.0 %copy-start.8 = (f32[344]{0:T(512)S(1)}, f32[344]{0:T(512)}, u32[]{:S(2)}) copy-start(f32[344]{0:T(512)} %param.22) | copy-start | bytes 4132
  0.7 17.0 %copy-start = (f32[8,256]{1,0:T(8,128)S(1)}, f32[8,256]{1,0:T(8,128)}, u32[]{:S(2)}) copy-start(f32[8,256]{1,0:T(8,128)} %constant.28.clone.lat_ref) | copy-start | bytes 24580
  0.7 16.9 %copy-start.2 = (f32[1,384]{1,0:T(1,128)S(1)}, f32[1,384]{1,0:T(1,128)}, u32[]{:S(2)}) copy-start(f32[1,384]{1,0:T(1,128)} %constant.29.clone.start_ref) | copy-start | bytes 4612
  10.1 16.9 %all-to-all-start = ((bf16[16,3,32,128]{3,2,1,0:T(8,128)(2,1)}), bf16[16,3,32,128]{3,2,1,0:T(8,128)(2,1)S(1)}, u32[]{:S(2)}, u32[]{:S(2)}) async-start(bf16[16,3,32,128]{3,2,1,0:T(8,128)(2,1)} %bitcast.25), calls=%async_computation | async-start | bytes 786432 | tf_op jit(solution)/shard_map/all_to_all | solution.py:598
  17.6 4.9 %copy-start.6 = (bf16[344,2048]{1,0:T(8,128)(2,1)S(1)}, bf16[344,2048]{1,0:T(8,128)(2,1)}, u32[]{:S(2)}) copy-start(bf16[344,2048]{1,0:T(8,128)(2,1)} %constant.27.clone) | copy-start | bytes 4227076
  22.5 4.5 %copy-start.1 = (f32[8,384]{1,0:T(8,128)S(1)}, f32[8,384]{1,0:T(8,128)}, u32[]{:S(2)}) copy-start(f32[8,384]{1,0:T(8,128)} %constant.30.clone.q_ref) | copy-start | bytes 36868
  28.5 13.2 %all-to-all-start.1 = ((bf16[8,48,384]{2,1,0:T(8,128)(2,1)}), bf16[8,48,384]{2,1,0:T(8,128)(2,1)S(1)}, u32[]{:S(2)}, u32[]{:S(2)}) async-start(bf16[8,48,384]{2,1,0:T(8,128)(2,1)} %forward_fourier.1), calls=%async_computation.1 | async-start | bytes 589824 | tf_op jit(solution)/shard_map/all_to_all | solution.py:615
  48.9 11.2 %all-to-all-start.2 = ((bf16[8,48,384]{2,1,0:T(8,128)(2,1)}), bf16[8,48,384]{2,1,0:T(8,128)(2,1)S(1)}, u32[]{:S(2)}, u32[]{:S(2)}) async-start(bf16[8,48,384]{2,1,0:T(8,128)(2,1)} %get-tuple-element.47), calls=%async_computation.2 | async-start | bytes 589824 | tf_op jit(solution)/shard_map/all_to_all | solution.py:623
  57.0 17.9 %copy-start.3 = (bf16[1536,208]{1,0:T(8,128)(2,1)S(1)}, bf16[1536,208]{1,0:T(8,128)(2,1)}, u32[]{:S(2)}) copy-start(bf16[1536,208]{1,0:T(8,128)(2,1)} %get-tuple-element.59.w1_ref) | copy-start | bytes 1916932
  57.0 17.9 %copy-start.4 = (bf16[64,256]{1,0:T(8,128)(2,1)S(1)}, bf16[64,256]{1,0:T(8,128)(2,1)}, u32[]{:S(2)}) copy-start(bf16[64,256]{1,0:T(8,128)(2,1)} %get-tuple-element.60.w2_ref) | copy-start | bytes 98308
  57.0 17.8 %copy-start.5 = (f32[64,128]{1,0:T(8,128)S(1)}, f32[64,128]{1,0:T(8,128)}, u32[]{:S(2)}) copy-start(f32[64,128]{1,0:T(8,128)} %get-tuple-element.61.b2_ref) | copy-start | bytes 98308

commit v9 on v8

--- a/solution.py
+++ b/solution.py
@@ -436,7 +436,7 @@
     )(returned, tables)
 
 
-WAVES = 8
+WAVES = 12
 GROUPS = -(-OWNED // WAVES)
 LAST = OWNED - (GROUPS - 1) * WAVES
 

time: 85.2 us -> 85.1 us (level)
  no operation moved by 1% of the time
where the time goes in v9:
time: 85.1 us; the launch traced here: 84.5 us
  Pallas kernels  41.1 us (48%)
  starting transfers between devices  15.8 us (19%)
  blocking collectives  13.2 us (16%)
  waiting for transfers between devices  9.6 us (11%)
  matrix products  3.4 us (4%)
    all_to_all x1, blocking collectives, per_device(): filtered = lax.all_to_all(grid_values, 'lon', 0, 0, tiled=True)  13.2 us
    pallas_call x2, Pallas kernels, legendre_table(): pl.pallas_call(table_kernel, grid=(KP // CHUNK,), out_shape=pltpu.HBM((MH...  9.79 us
    pallas_call x1, Pallas kernels, second_conv(): pl.pallas_call(functools.partial(second_kernel, block), grid=(COLUMNS //...  9.73 us
    pallas_call x1, Pallas kernels, first_conv(): pl.pallas_call(functools.partial(first_kernel, block), grid=(COLUMNS // b...  9.44 us
    all_to_all x1, starting transfers between devices, per_device(): lax.all_to_all(tendency.reshape(N_LON, GROUP, TILES, 128), 'lon', 0, 0, t...  7.11 us
    pallas_call x1, Pallas kernels, spectral_step(): pl.pallas_call(spectral_kernel, grid_spec=pltpu.PrefetchScalarGridSpec(nu...  7.04 us
    all_to_all x1, starting transfers between devices, per_device(): coeffs = lax.all_to_all(coeffs, 'lat', 0, 0, tiled=True)  5.31 us
    all_to_all x1, waiting for transfers between devices, per_device(): lax.all_to_all(tendency.reshape(N_LON, GROUP, TILES, 128), 'lon', 0, 0, t...  3.48 us
  transfers between devices with their start and end apart: 3, of which 3 were waited for; matrix products, arithmetic and copies ran while one was open for 5% of the time, Pallas kernels for 14%

profile of v9, /device:TPU:0, one launch (start us, length us, event | category | flops | bytes accessed | tf_op | source)
XLA Modules:
  0.0 84.5 jit_solution(14236477122537068854)
XLA Ops:
  0.7 0.0 copy-start
  0.7 9.4 %first_conv.1 = bf16[48,32,128]{2,1,0:T(8,128)(2,1)} custom-call(bf16[144,4096]{1,0:T(8,128)(2,1)} %bitcast.26, bf16[3,6,64]{2,1,0:T(8,128)(2,1)} %bitcast.28, f32[1,64]{1,0:T(1,128)} %bitcast.31, bf16[3,2,64]{2,1,0:T(2,128)(2,1)} %bitcast.30, s32[1,48]{1,0:T(1,128)} %bitcast.33, f32[1,2]{1,0:T(1,128)} %bitcast.32), custom_call_target="tpu_custom_call" | custom-call | flops 3000000000 | bytes 2000000 | tf_op jit(solution)/shard_map/first_conv/pallas_call | solution.py:204
  10.1 7.1 %all-to-all-start = ((bf16[16,3,32,128]{3,2,1,0:T(8,128)(2,1)}), bf16[16,3,32,128]{3,2,1,0:T(8,128)(2,1)S(1)}, u32[]{:S(2)}, u32[]{:S(2)}) async-start(bf16[16,3,32,128]{3,2,1,0:T(8,128)(2,1)} %bitcast.25), calls=%async_computation | async-start | bytes 786432 | tf_op jit(solution)/shard_map/all_to_all | solution.py:598
  17.3 0.1 reshape.50
  17.3 0.1 slice_bitcast_fusion
  17.4 0.1 eq.30
  17.5 0.1 copy.19.wave_ref
  17.6 4.9 %legendre_table.2.t0_ref = bf16[24,352,256]{2,1,0:T(8,128)(2,1)} custom-call(f32[24,1]{1,0:T(8,128)S(1)} %copy.19.wave_ref, f32[8,256]{1,0:T(8,128)S(1)} %copy-done, f32[1,384]{1,0:T(1,128)S(1)} %copy-done.2), custom_call_target="tpu_custom_call" | custom-call | flops 200000000 | bytes 9000000 | tf_op jit(solution)/shard_map/legendre_table/pallas_call | solution.py:352
  22.6 1.0 %convolution_convert_fusion.1.f_ref = bf16[384,2048]{1,0:T(8,128)(2,1)S(1)} fusion(bf16[344,2048]{1,0:T(8,128)(2,1)S(1)} %copy-done.6, s32[384]{0:T(512)S(1)} %eq.30), kind=kOutput, calls=%fused_computation.1 | convolution fusion | flops 541983744 | bytes 2983424 | tf_op jit(solution)/shard_map/dot_general | solution.py:53
  23.6 3.5 %all-to-all-done.y_ref = bf16[16,3,32,128]{3,2,1,0:T(8,128)(2,1)S(1)} async-done(((bf16[16,3,32,128]{3,2,1,0:T(8,128)(2,1)}), bf16[16,3,32,128]{3,2,1,0:T(8,128)(2,1)S(1)}, u32[]{:S(2)}, u32[]{:S(2)}) %all-to-all-start) | async-done | bytes 393248 | tf_op jit(solution)/shard_map/all_to_all | solution.py:598
  27.1 1.5 %forward_fourier.1 = bf16[8,48,384]{2,1,0:T(8,128)(2,1)} custom-call(bf16[16,3,32,128]{3,2,1,0:T(8,128)(2,1)S(1)} %all-to-all-done.y_ref, bf16[384,2048]{1,0:T(8,128)(2,1)S(1)} %convolution_convert_fusion.1.f_ref, f32[8,384]{1,0:T(8,128)S(1)} %copy-done.1), custom_call_target="tpu_custom_call" | custom-call | flops 400000000 | bytes 3000000 | tf_op jit(solution)/shard_map/forward_fourier/pallas_call | solution.py:397
  28.5 5.3 %all-to-all-start.1 = ((bf16[8,48,384]{2,1,0:T(8,128)(2,1)}), bf16[8,48,384]{2,1,0:T(8,128)(2,1)S(1)}, u32[]{:S(2)}, u32[]{:S(2)}) async-start(bf16[8,48,384]{2,1,0:T(8,128)(2,1)} %forward_fourier.1), calls=%async_computation.1 | async-start | bytes 589824 | tf_op jit(solution)/shard_map/all_to_all | solution.py:615
  33.8 0.1 copy.20.wave_ref
  33.9 4.9 %legendre_table.3.t1_ref = bf16[24,352,256]{2,1,0:T(8,128)(2,1)} custom-call(f32[24,1]{1,0:T(8,128)S(1)} %copy.20.wave_ref, f32[8,256]{1,0:T(8,128)S(1)} %copy-done, f32[1,384]{1,0:T(1,128)S(1)} %copy-done.2), custom_call_target="tpu_custom_call" | custom-call | flops 200000000 | bytes 9000000 | tf_op jit(solution)/shard_map/legendre_table/pallas_call | solution.py:352
  38.8 2.9 %all-to-all-done.1.x_ref = bf16[8,48,384]{2,1,0:T(8,128)(2,1)S(1)} async-done(((bf16[8,48,384]{2,1,0:T(8,128)(2,1)}), bf16[8,48,384]{2,1,0:T(8,128)(2,1)S(1)}, u32[]{:S(2)}, u32[]{:S(2)}) %all-to-all-start.1) | async-done | bytes 294944 | tf_op jit(solution)/shard_map/all_to_all | solution.py:615
  41.7 7.0 %spectral_step.1 = (f32[3,43,688]{2,1,0:T(8,128)}, bf16[8,48,384]{2,1,0:T(8,128)(2,1)}) custom-call(s32[48]{0:T(128)S(1)} %get-tuple-element.35.wave_ref, bf16[8,48,384]{2,1,0:T(8,128)(2,1)S(1)} %all-to-all-done.1.x_ref, bf16[24,352,256]{2,1,0:T(8,128)(2,1)} %legendre_table.2.t0_ref, bf16[24,352,256]{2,1,0:T(8,128)(2,1)} %legendre_table.3.t1_ref, ...), custom_call_target="tpu_custom_call" | custom-call | flops 4000000000 | bytes 10000000 | tf_op jit(solution)/shard_map/spectral_step/pallas_call | solution.py:554
  48.8 0.1 eq.34
  48.9 3.4 %all-to-all-start.2 = ((bf16[8,48,384]{2,1,0:T(8,128)(2,1)}), bf16[8,48,384]{2,1,0:T(8,128)(2,1)S(1)}, u32[]{:S(2)}, u32[]{:S(2)}) async-start(bf16[8,48,384]{2,1,0:T(8,128)(2,1)} %get-tuple-element.47), calls=%async_computation.2 | async-start | bytes 589824 | tf_op jit(solution)/shard_map/all_to_all | solution.py:623
  52.3 2.2 %second_weights.1 = (bf16[1536,208]{1,0:T(8,128)(2,1)}, bf16[64,256]{1,0:T(8,128)(2,1)}, f32[64,128]{1,0:T(8,128)}) custom-call(bf16[3,8,64]{2,1,0:T(8,128)(2,1)} %bitcast.29, f32[1,64]{1,0:T(1,128)} %bitcast.35, bf16[6,3,64]{2,1,0:T(4,128)(2,1)} %w2_ref, s32[1,48]{1,0:T(1,128)} %bitcast.34, f32[1,6]{1,0:T(1,128)} %bitcast.36), custom_call_target="tpu_custom_call" | custom-call | flops 200000000 | bytes 2000000 | tf_op jit(solution)/shard_map/second_weights/pallas_call | solution.py:152
  54.5 2.4 %convolution_convert_fusion.f_ref = bf16[384,2048]{1,0:T(8,128)(2,1)S(1)} fusion(bf16[344,2048]{1,0:T(8,128)(2,1)} %constant.31.clone, s32[384]{0:T(512)S(1)} %eq.34), kind=kOutput, calls=%fused_computation | convolution fusion | flops 541983744 | bytes 2983424 | tf_op jit(solution)/shard_map/dot_general | solution.py:53
  56.9 3.2 %all-to-all-done.2 = bf16[8,48,384]{2,1,0:T(8,128)(2,1)S(1)} async-done(((bf16[8,48,384]{2,1,0:T(8,128)(2,1)}), bf16[8,48,384]{2,1,0:T(8,128)(2,1)S(1)}, u32[]{:S(2)}, u32[]{:S(2)}) %all-to-all-start.2) | async-done | bytes 294944 | tf_op jit(solution)/shard_map/all_to_all | solution.py:623
  60.1 1.5 %inverse_fourier.1 = bf16[16,3,32,128]{3,2,1,0:T(8,128)(2,1)} custom-call(bf16[384,384]{1,0:T(8,128)(2,1)S(1)} %bitcast.23, bf16[384,2048]{1,0:T(8,128)(2,1)S(1)} %convolution_convert_fusion.f_ref), custom_call_target="tpu_custom_call" | custom-call | flops 400000000 | bytes 3000000 | tf_op jit(solution)/shard_map/inverse_fourier/pallas_call | solution.py:427
  61.5 13.2 %all_to_all.20 = bf16[16,3,32,128]{3,2,1,0:T(8,128)(2,1)S(1)} all-to-all(bf16[16,3,32,128]{3,2,1,0:T(8,128)(2,1)} %inverse_fourier.1), channel_id=1, replica_groups=mesh['lat'=8,'lon'=16] {'lon'}, dimensions={0} | all-to-all | bytes 786432 | tf_op jit(solution)/shard_map/all_to_all | solution.py:628
  74.7 9.7 %second_conv.1 = f32[144,4096]{1,0:T(8,128)} custom-call(bf16[144,4096]{1,0:T(8,128)(2,1)} %bitcast.27, bf16[48,32,128]{2,1,0:T(8,128)(2,1)S(1)} %bitcast.24, bf16[1536,208]{1,0:T(8,128)(2,1)S(1)} %copy-done.3, bf16[64,256]{1,0:T(8,128)(2,1)S(1)} %copy-done.4, f32[64,128]{1,0:T(8,128)S(1)} %copy-done.5), custom_call_target="tpu_custom_call" | custom-call | flops 4000000000 | bytes 4000000 | tf_op jit(solution)/shard_map/second_conv/pallas_call | solution.py:267
  (21 shorter events, 0.1 us)
Async XLA Ops:
  0.6 16.6 %copy-start.7 = (s32[344]{0:T(512)S(1)}, s32[344]{0:T(512)}, u32[]{:S(2)}) copy-start(s32[344]{0:T(512)} %param.28) | copy-start | bytes 4132
  0.6 17.0 %copy-start.8 = (f32[344]{0:T(512)S(1)}, f32[344]{0:T(512)}, u32[]{:S(2)}) copy-start(f32[344]{0:T(512)} %param.22) | copy-start | bytes 4132
  0.7 17.0 %copy-start = (f32[8,256]{1,0:T(8,128)S(1)}, f32[8,256]{1,0:T(8,128)}, u32[]{:S(2)}) copy-start(f32[8,256]{1,0:T(8,128)} %constant.28.clone.lat_ref) | copy-start | bytes 24580
  0.7 16.9 %copy-start.2 = (f32[1,384]{1,0:T(1,128)S(1)}, f32[1,384]{1,0:T(1,128)}, u32[]{:S(2)}) copy-start(f32[1,384]{1,0:T(1,128)} %constant.29.clone.start_ref) | copy-start | bytes 4612
  10.1 16.9 %all-to-all-start = ((bf16[16,3,32,128]{3,2,1,0:T(8,128)(2,1)}), bf16[16,3,32,128]{3,2,1,0:T(8,128)(2,1)S(1)}, u32[]{:S(2)}, u32[]{:S(2)}) async-start(bf16[16,3,32,128]{3,2,1,0:T(8,128)(2,1)} %bitcast.25), calls=%async_computation | async-start | bytes 786432 | tf_op jit(solution)/shard_map/all_to_all | solution.py:598
  17.6 4.9 %copy-start.6 = (bf16[344,2048]{1,0:T(8,128)(2,1)S(1)}, bf16[344,2048]{1,0:T(8,128)(2,1)}, u32[]{:S(2)}) copy-start(bf16[344,2048]{1,0:T(8,128)(2,1)} %constant.27.clone) | copy-start | bytes 4227076
  22.5 4.5 %copy-start.1 = (f32[8,384]{1,0:T(8,128)S(1)}, f32[8,384]{1,0:T(8,128)}, u32[]{:S(2)}) copy-start(f32[8,384]{1,0:T(8,128)} %constant.30.clone.q_ref) | copy-start | bytes 36868
  28.5 13.2 %all-to-all-start.1 = ((bf16[8,48,384]{2,1,0:T(8,128)(2,1)}), bf16[8,48,384]{2,1,0:T(8,128)(2,1)S(1)}, u32[]{:S(2)}, u32[]{:S(2)}) async-start(bf16[8,48,384]{2,1,0:T(8,128)(2,1)} %forward_fourier.1), calls=%async_computation.1 | async-start | bytes 589824 | tf_op jit(solution)/shard_map/all_to_all | solution.py:615
  48.9 11.2 %all-to-all-start.2 = ((bf16[8,48,384]{2,1,0:T(8,128)(2,1)}), bf16[8,48,384]{2,1,0:T(8,128)(2,1)S(1)}, u32[]{:S(2)}, u32[]{:S(2)}) async-start(bf16[8,48,384]{2,1,0:T(8,128)(2,1)} %get-tuple-element.47), calls=%async_computation.2 | async-start | bytes 589824 | tf_op jit(solution)/shard_map/all_to_all | solution.py:623
  56.9 17.9 %copy-start.3 = (bf16[1536,208]{1,0:T(8,128)(2,1)S(1)}, bf16[1536,208]{1,0:T(8,128)(2,1)}, u32[]{:S(2)}) copy-start(bf16[1536,208]{1,0:T(8,128)(2,1)} %get-tuple-element.59.w1_ref) | copy-start | bytes 1916932
  56.9 17.9 %copy-start.4 = (bf16[64,256]{1,0:T(8,128)(2,1)S(1)}, bf16[64,256]{1,0:T(8,128)(2,1)}, u32[]{:S(2)}) copy-start(bf16[64,256]{1,0:T(8,128)(2,1)} %get-tuple-element.60.w2_ref) | copy-start | bytes 98308
  56.9 17.8 %copy-start.5 = (f32[64,128]{1,0:T(8,128)S(1)}, f32[64,128]{1,0:T(8,128)}, u32[]{:S(2)}) copy-start(f32[64,128]{1,0:T(8,128)} %get-tuple-element.61.b2_ref) | copy-start | bytes 98308
